TPU v7x, 32 devices: a whole 2x2x4 slice. The times are simulated.
32 devices in a mesh: group: 2 (over y), tx: 4 (over z), ty: 2 (over x), ch: 2 (over core).
Axes of the slice: x: 2, y: 2, z: 4, core: 2. Of those that a mesh axis runs over, the one named last changes fastest.
Arguments:
- fine_features: bfloat16 [32, 65536], P('ch', ('group', 'tx', 'ty')), parts along dimension 1, may hold values from -6 to 6
- neighbours: int32 [27, 65536], P(None, ('group', 'tx', 'ty')), parts along dimension 1, may hold values from 0 to 6656, as said below
- face_send: int32 [4, 8192], P(None, ('group', 'tx', 'ty')), parts along dimension 1, may hold values from 0 to 4095
- corner_send: int32 [4, 2048], P(None, ('group', 'tx', 'ty')), parts along dimension 1, may hold values from 0 to 4095
- owner_side: int32 [65536], P(('group', 'tx', 'ty')), parts along dimension 0, may hold values from 0 to 8, as said below
- owner_slot: int32 [65536], P(('group', 'tx', 'ty')), parts along dimension 0, may hold values from 0 to 255
- conv_weight: bfloat16 [27, 32, 32], replicated, may hold values from -0.21875 to 0.21875
- coarse_weight: bfloat16 [32, 128], replicated, may hold values from -0.25 to 0.25
- coarse_grad: bfloat16 [128, 4096], P(None, ('group', 'tx', 'ty')), parts along dimension 1, may hold values from -6 to 6
Outputs:
- coarse_out: bfloat16 [128, 4096], P('ch', ('group', 'tx', 'ty')), parts along dimension 1
- input_grad: bfloat16 [32, 65536], P('ch', ('group', 'tx', 'ty')), parts along dimension 1
- conv_weight_grad: float32 [54, 32, 32], P('group', None, 'ch'), parts along dimension 0
- coarse_weight_grad: float32 [64, 128], P('group', 'ch'), parts along dimension 0
There are 2 independent parts, one for each index of `group`. A program takes and returns all parts, laid end to end along the dimension named above; an argument that names none is the same for every part. Nothing has to cross between parts.
Inputs may be any that keep to these rules, and one draw needn't show every extreme that they name: `neighbours`: entries below 4096 are the tile's own rows, then come four blocks of 512 and four of 128 rows in the order of the steps; the largest value means no neighbour. Entry 13 of every voxel is its own row. `owner_side`: the named tile always exists. Among the rows of one tile every value other than 0 is named at most 256 times, and in every tile some value exactly 256 times.
All inputs are finite; a program needn't handle non-finite values.
Results may differ from a plain program's by a relative error of at most 0.0059.
Values may be sent and summed in bfloat16 or wider, within the bound.
No kernel may reach another device: no remote copies, remote signals or barrier semaphores. Data moves between devices by JAX's collectives and lax.ppermute only.
A program may use at most 64 MiB of HBM per device.

v0:
```python
import jax
import jax.numpy as jnp
from jax import lax
from jax.sharding import PartitionSpec as P

CORNER_STEPS = ((-1, -1), (-1, 1), (1, -1), (1, 1))
CORNER_OPPOSITE = (3, 2, 1, 0)


def from_behind(value, axis, by):
    count = lax.axis_size(axis)
    pairs = [(i, i + by) for i in range(count) if 0 <= i + by < count]
    return lax.ppermute(value, axis, pairs)


def shift_tx(packet, stride):
    return from_behind(packet, "tx", stride)


def shift_ty(packet, stride):
    return from_behind(packet, "ty", stride)


def shift_both(packet, stride):
    return from_behind(packet, ("tx", "ty"), stride)


def pool_tx(packet, stride):
    return from_behind(packet, "tx", stride)


def pool_ty(packet, stride):
    return from_behind(packet, "ty", stride)


def pool_both(packet, stride):
    return from_behind(packet, ("tx", "ty"), stride)


def gather_channels(values):
    return lax.all_gather(values, "ch", axis=0, tiled=True)


def silu_slope(values):
    sigma = jax.nn.sigmoid(values)
    return sigma * (1.0 + values * (1.0 - sigma))


def rim_forward(face_out, corner_out, y_count, y_index, shifters):
    along_x, along_y, along_both = shifters
    faces = [
        along_x(face_out[:, 1], 1),
        along_x(face_out[:, 0], -1),
        along_y(face_out[:, 3], 1),
        along_y(face_out[:, 2], -1),
    ]
    corners = []
    for direction in range(4):
        step_x, step_y = CORNER_STEPS[direction]
        moved = along_both(corner_out[:, CORNER_OPPOSITE[direction]], -(step_x * y_count + step_y))
        inside = (y_index + step_y >= 0) & (y_index + step_y < y_count)
        corners.append(jnp.where(inside, moved, jnp.zeros_like(moved)))
    return (jnp.concatenate(faces, axis=1), jnp.concatenate(corners, axis=1))


def rim_backward(face_grad, corner_grad, y_count, y_index):
    faces = [
        shift_tx(face_grad[:, 1], 1),
        shift_tx(face_grad[:, 0], -1),
        shift_ty(face_grad[:, 3], 1),
        shift_ty(face_grad[:, 2], -1),
    ]
    corners = []
    for target in range(4):
        direction = CORNER_OPPOSITE[target]
        step_x, step_y = CORNER_STEPS[direction]
        moved = shift_both(corner_grad[:, direction], step_x * y_count + step_y)
        inside = (y_index - step_y >= 0) & (y_index - step_y < y_count)
        corners.append(jnp.where(inside, moved, jnp.zeros_like(moved)))
    return (jnp.concatenate(faces, axis=1), jnp.concatenate(corners, axis=1))


def shards(
    fine_features,
    neighbours,
    face_send,
    corner_send,
    owner_side,
    owner_slot,
    conv_weight,
    coarse_weight,
    coarse_grad,
):
    chan_share = fine_features.shape[0]
    voxels = fine_features.shape[1]
    face_rows = face_send.shape[1]
    corner_rows = corner_send.shape[1]
    offset_count = neighbours.shape[0]
    coarse_rows = coarse_grad.shape[1]
    coarse_share = coarse_grad.shape[0] // lax.axis_size("ch")
    core_index = lax.axis_index("ch")
    y_count = lax.axis_size("ty")
    y_index = lax.axis_index("ty")
    halo_end = voxels + 4 * face_rows + 4 * corner_rows
    data_shifters = (shift_tx, shift_ty, shift_both)
    wc_rows = lax.dynamic_slice_in_dim(coarse_weight, core_index * chan_share, chan_share, 0)
    pooled_grad = jnp.dot(wc_rows, coarse_grad, preferred_element_type=jnp.float32).astype(
        jnp.bfloat16
    )
    spread = jnp.broadcast_to(pooled_grad[:, None, :], (chan_share, 4, coarse_rows))
    face_out = jnp.take(fine_features, face_send, axis=1)
    corner_out = jnp.take(fine_features, corner_send, axis=1)
    face_in, corner_in = rim_forward(face_out, corner_out, y_count, y_index, data_shifters)
    ext_own = jnp.concatenate(
        [fine_features, face_in, corner_in, jnp.zeros((chan_share, 128), jnp.bfloat16)], axis=1
    )
    ext_full = gather_channels(ext_own)
    extent = ext_full.shape[1]
    w_out = lax.dynamic_slice_in_dim(conv_weight, core_index * chan_share, chan_share, 2)
    w_in = lax.dynamic_slice_in_dim(conv_weight, core_index * chan_share, chan_share, 1)

    def forward_step(offset, running):
        picked = jnp.take(
            ext_full, lax.dynamic_index_in_dim(neighbours, offset, 0, keepdims=False), axis=1
        )
        weight = lax.dynamic_index_in_dim(w_out, offset, 0, keepdims=False)
        return running + lax.dot_general(
            weight, picked, (((0,), (0,)), ((), ())), preferred_element_type=jnp.float32
        )

    hidden = lax.fori_loop(
        0, offset_count, forward_step, jnp.zeros((chan_share, voxels), jnp.float32)
    )
    active = jax.nn.silu(hidden).astype(jnp.bfloat16)
    slot_cols = owner_side * coarse_rows + owner_slot
    span = 9 * coarse_rows
    block_rows = min(voxels, 512)

    def pool_step(number, running):
        columns = lax.dynamic_slice_in_dim(active, number * block_rows, block_rows, 1)
        slot_ids = lax.dynamic_slice_in_dim(slot_cols, number * block_rows, block_rows, 0)
        one_hot = (slot_ids[:, None] == jnp.arange(span, dtype=jnp.int32)[None, :]).astype(
            jnp.bfloat16
        )
        return running + jnp.dot(columns, one_hot, preferred_element_type=jnp.float32)

    partial_value = lax.fori_loop(
        0, voxels // block_rows, pool_step, jnp.zeros((chan_share, span), jnp.float32)
    )
    face_part = partial_value[:, coarse_rows : 5 * coarse_rows].reshape(chan_share, 4, coarse_rows)
    corner_part = partial_value[:, 5 * coarse_rows :].reshape(chan_share, 4, coarse_rows)
    face_sums, corner_sums = rim_forward(
        face_part, corner_part, y_count, y_index, (pool_tx, pool_ty, pool_both)
    )
    pooled = (
        partial_value[:, :coarse_rows]
        + jnp.sum(face_sums.reshape(chan_share, 4, coarse_rows), axis=1)
        + jnp.sum(corner_sums.reshape(chan_share, 4, coarse_rows), axis=1)
    )
    pooled_full = gather_channels(pooled.astype(jnp.bfloat16))
    wc_cols = lax.dynamic_slice_in_dim(coarse_weight, core_index * coarse_share, coarse_share, 1)
    coarse_out = lax.dot_general(
        wc_cols, pooled_full, (((0,), (0,)), ((), ())), preferred_element_type=jnp.float32
    ).astype(jnp.bfloat16)
    grad_rows = lax.dynamic_slice_in_dim(coarse_grad, core_index * coarse_share, coarse_share, 0)
    coarse_part = lax.dot_general(
        pooled_full, grad_rows, (((1,), (1,)), ((), ())), preferred_element_type=jnp.float32
    )
    face_parents, corner_parents = rim_forward(spread, spread, y_count, y_index, data_shifters)
    parent_grads = jnp.concatenate([pooled_grad, face_parents, corner_parents], axis=1)
    active_grad = jnp.take(parent_grads, slot_cols, axis=1)
    hidden_grad = (active_grad.astype(jnp.float32) * silu_slope(hidden)).astype(jnp.bfloat16)

    def weight_step(offset, grads):
        picked = jnp.take(
            ext_full, lax.dynamic_index_in_dim(neighbours, offset, 0, keepdims=False), axis=1
        )
        contrib = lax.dot_general(
            picked, hidden_grad, (((1,), (1,)), ((), ())), preferred_element_type=jnp.float32
        )
        return lax.dynamic_update_index_in_dim(grads, contrib, offset, 0)

    conv_part = lax.fori_loop(
        0,
        offset_count,
        weight_step,
        jnp.zeros((offset_count, ext_full.shape[0], chan_share), jnp.float32),
    )
    full_grad = gather_channels(hidden_grad)

    def input_step(offset, grads):
        weight = lax.dynamic_index_in_dim(w_in, offset, 0, keepdims=False)
        contrib = jnp.dot(weight, full_grad, preferred_element_type=jnp.float32)
        return grads.at[:, lax.dynamic_index_in_dim(neighbours, offset, 0, keepdims=False)].add(
            contrib
        )

    ext_grad = lax.fori_loop(
        0, offset_count, input_step, jnp.zeros((chan_share, extent), jnp.float32)
    )
    face_grad = (
        ext_grad[:, voxels : voxels + 4 * face_rows]
        .astype(jnp.bfloat16)
        .reshape(chan_share, 4, face_rows)
    )
    corner_grad = (
        ext_grad[:, voxels + 4 * face_rows : halo_end]
        .astype(jnp.bfloat16)
        .reshape(chan_share, 4, corner_rows)
    )
    face_back, corner_back = rim_backward(face_grad, corner_grad, y_count, y_index)
    own_part = ext_grad[:, :voxels]
    own_part = own_part.at[:, face_send.reshape(-1)].add(face_back.astype(jnp.float32))
    own_part = own_part.at[:, corner_send.reshape(-1)].add(corner_back.astype(jnp.float32))
    input_grad = own_part.astype(jnp.bfloat16)
    conv_weight_grad, coarse_weight_grad = lax.psum((conv_part, coarse_part), ("tx", "ty"))
    return (coarse_out, input_grad, conv_weight_grad, coarse_weight_grad)


def solution(mesh):
    in_specs = (
        P("ch", ("group", "tx", "ty")),
        P(None, ("group", "tx", "ty")),
        P(None, ("group", "tx", "ty")),
        P(None, ("group", "tx", "ty")),
        P(("group", "tx", "ty")),
        P(("group", "tx", "ty")),
        P(),
        P(),
        P(None, ("group", "tx", "ty")),
    )
    out_specs = (
        P("ch", ("group", "tx", "ty")),
        P("ch", ("group", "tx", "ty")),
        P("group", None, "ch"),
        P("group", "ch"),
    )
    return jax.shard_map(shards, mesh=mesh, in_specs=in_specs, out_specs=out_specs, check_vma=False)
```

profile of v0, /device:TPU:0, one launch (start us, length us, event | category | flops | bytes accessed | tf_op | source)
XLA Modules:
  0.0 1890.8 jit_solution(4601786155863525819)
XLA Ops:
  100.5 408.0 %while.56 = (s32[]{:T(128)}, f32[16,4096]{1,0:T(8,128)S(1)}, bf16[27,32,16]{1,2,0:T(8,128)(2,1)}, s32[27,4096]{1,0:T(8,128)}, bf16[32,6784]{0,1:T(8,128)(2,1)S(1)}, /*index=5*/s32[]{:T(128)}, s32[]{:T(128)}) while((s32[]{:T(128)}, f32[16,4096]{1,0:T(8,128)S(1)}, bf16[27,32,16]{1,2,0:T(8,128)(2,1)}, s32[27,4096]{1,0:T(8,128)}, ...), condition=%wide.region_1.3_spmd.clone, body=%wide.region_0.0_spmd.clone.sunk | while | flops 4497411 | bytes 1421415 | solution.py:131
  513.3 733.4 %while.54 = (s32[]{:T(128)}, f32[16,6784]{0,1:T(8,128)}, s32[27,4096]{1,0:T(8,128)}, bf16[27,16,32]{2,1,0:T(8,128)(2,1)S(1)}, bf16[32,4096]{1,0:T(8,128)(2,1)S(1)}, /*index=5*/s32[]{:T(128)}) while((s32[]{:T(128)}, f32[16,6784]{0,1:T(8,128)}, s32[27,4096]{1,0:T(8,128)}, bf16[27,16,32]{2,1,0:T(8,128)(2,1)S(1)}, ...), condition=%wide.region_8.10_spmd, body=%wide.region_6.9_spmd.sunk | while | flops 4272130 | bytes 1888341 | solution.py:198
  516.4 24.1 %scatter_fusion = f32[16,6784]{0,1:T(8,128)} fusion(f32[16,6784]{0,1:T(8,128)} %get-tuple-element.771, s32[4096]{0:T(1024)S(1)} %bitcast.142, f32[4096,16]{1,0:T(8,128)} %copy.299), kind=kCustom, calls=%fused_computation.5.clone.1 | custom fusion | flops 65536 | bytes 802816 | tf_op jit(solution)/shard_map/while/body/eval_jaxpr/scatter-add | solution.py:194
  543.6 24.1 %scatter_fusion = f32[16,6784]{0,1:T(8,128)} fusion(f32[16,6784]{0,1:T(8,128)} %get-tuple-element.771, s32[4096]{0:T(1024)S(1)} %bitcast.142, f32[4096,16]{1,0:T(8,128)} %copy.299), kind=kCustom, calls=%fused_computation.5.clone.1 | custom fusion | flops 65536 | bytes 802816 | tf_op jit(solution)/shard_map/while/body/eval_jaxpr/scatter-add | solution.py:194
  570.7 24.1 %scatter_fusion = f32[16,6784]{0,1:T(8,128)} fusion(f32[16,6784]{0,1:T(8,128)} %get-tuple-element.771, s32[4096]{0:T(1024)S(1)} %bitcast.142, f32[4096,16]{1,0:T(8,128)} %copy.299), kind=kCustom, calls=%fused_computation.5.clone.1 | custom fusion | flops 65536 | bytes 802816 | tf_op jit(solution)/shard_map/while/body/eval_jaxpr/scatter-add | solution.py:194
  597.9 24.1 %scatter_fusion = f32[16,6784]{0,1:T(8,128)} fusion(f32[16,6784]{0,1:T(8,128)} %get-tuple-element.771, s32[4096]{0:T(1024)S(1)} %bitcast.142, f32[4096,16]{1,0:T(8,128)} %copy.299), kind=kCustom, calls=%fused_computation.5.clone.1 | custom fusion | flops 65536 | bytes 802816 | tf_op jit(solution)/shard_map/while/body/eval_jaxpr/scatter-add | solution.py:194
  625.1 24.1 %scatter_fusion = f32[16,6784]{0,1:T(8,128)} fusion(f32[16,6784]{0,1:T(8,128)} %get-tuple-element.771, s32[4096]{0:T(1024)S(1)} %bitcast.142, f32[4096,16]{1,0:T(8,128)} %copy.299), kind=kCustom, calls=%fused_computation.5.clone.1 | custom fusion | flops 65536 | bytes 802816 | tf_op jit(solution)/shard_map/while/body/eval_jaxpr/scatter-add | solution.py:194
  652.2 24.1 %scatter_fusion = f32[16,6784]{0,1:T(8,128)} fusion(f32[16,6784]{0,1:T(8,128)} %get-tuple-element.771, s32[4096]{0:T(1024)S(1)} %bitcast.142, f32[4096,16]{1,0:T(8,128)} %copy.299), kind=kCustom, calls=%fused_computation.5.clone.1 | custom fusion | flops 65536 | bytes 802816 | tf_op jit(solution)/shard_map/while/body/eval_jaxpr/scatter-add | solution.py:194
  679.4 24.1 %scatter_fusion = f32[16,6784]{0,1:T(8,128)} fusion(f32[16,6784]{0,1:T(8,128)} %get-tuple-element.771, s32[4096]{0:T(1024)S(1)} %bitcast.142, f32[4096,16]{1,0:T(8,128)} %copy.299), kind=kCustom, calls=%fused_computation.5.clone.1 | custom fusion | flops 65536 | bytes 802816 | tf_op jit(solution)/shard_map/while/body/eval_jaxpr/scatter-add | solution.py:194
  706.5 24.1 %scatter_fusion = f32[16,6784]{0,1:T(8,128)} fusion(f32[16,6784]{0,1:T(8,128)} %get-tuple-element.771, s32[4096]{0:T(1024)S(1)} %bitcast.142, f32[4096,16]{1,0:T(8,128)} %copy.299), kind=kCustom, calls=%fused_computation.5.clone.1 | custom fusion | flops 65536 | bytes 802816 | tf_op jit(solution)/shard_map/while/body/eval_jaxpr/scatter-add | solution.py:194
  733.7 24.1 %scatter_fusion = f32[16,6784]{0,1:T(8,128)} fusion(f32[16,6784]{0,1:T(8,128)} %get-tuple-element.771, s32[4096]{0:T(1024)S(1)} %bitcast.142, f32[4096,16]{1,0:T(8,128)} %copy.299), kind=kCustom, calls=%fused_computation.5.clone.1 | custom fusion | flops 65536 | bytes 802816 | tf_op jit(solution)/shard_map/while/body/eval_jaxpr/scatter-add | solution.py:194
  760.9 24.1 %scatter_fusion = f32[16,6784]{0,1:T(8,128)} fusion(f32[16,6784]{0,1:T(8,128)} %get-tuple-element.771, s32[4096]{0:T(1024)S(1)} %bitcast.142, f32[4096,16]{1,0:T(8,128)} %copy.299), kind=kCustom, calls=%fused_computation.5.clone.1 | custom fusion | flops 65536 | bytes 802816 | tf_op jit(solution)/shard_map/while/body/eval_jaxpr/scatter-add | solution.py:194
  788.0 24.1 %scatter_fusion = f32[16,6784]{0,1:T(8,128)} fusion(f32[16,6784]{0,1:T(8,128)} %get-tuple-element.771, s32[4096]{0:T(1024)S(1)} %bitcast.142, f32[4096,16]{1,0:T(8,128)} %copy.299), kind=kCustom, calls=%fused_computation.5.clone.1 | custom fusion | flops 65536 | bytes 802816 | tf_op jit(solution)/shard_map/while/body/eval_jaxpr/scatter-add | solution.py:194
  815.2 24.1 %scatter_fusion = f32[16,6784]{0,1:T(8,128)} fusion(f32[16,6784]{0,1:T(8,128)} %get-tuple-element.771, s32[4096]{0:T(1024)S(1)} %bitcast.142, f32[4096,16]{1,0:T(8,128)} %copy.299), kind=kCustom, calls=%fused_computation.5.clone.1 | custom fusion | flops 65536 | bytes 802816 | tf_op jit(solution)/shard_map/while/body/eval_jaxpr/scatter-add | solution.py:194
  842.3 24.1 %scatter_fusion = f32[16,6784]{0,1:T(8,128)} fusion(f32[16,6784]{0,1:T(8,128)} %get-tuple-element.771, s32[4096]{0:T(1024)S(1)} %bitcast.142, f32[4096,16]{1,0:T(8,128)} %copy.299), kind=kCustom, calls=%fused_computation.5.clone.1 | custom fusion | flops 65536 | bytes 802816 | tf_op jit(solution)/shard_map/while/body/eval_jaxpr/scatter-add | solution.py:194
  923.8 24.1 %scatter_fusion = f32[16,6784]{0,1:T(8,128)} fusion(f32[16,6784]{0,1:T(8,128)} %get-tuple-element.771, s32[4096]{0:T(1024)S(1)} %bitcast.142, f32[4096,16]{1,0:T(8,128)} %copy.299), kind=kCustom, calls=%fused_computation.5.clone.1 | custom fusion | flops 65536 | bytes 802816 | tf_op jit(solution)/shard_map/while/body/eval_jaxpr/scatter-add | solution.py:194
  978.1 24.1 %scatter_fusion = f32[16,6784]{0,1:T(8,128)} fusion(f32[16,6784]{0,1:T(8,128)} %get-tuple-element.771, s32[4096]{0:T(1024)S(1)} %bitcast.142, f32[4096,16]{1,0:T(8,128)} %copy.299), kind=kCustom, calls=%fused_computation.5.clone.1 | custom fusion | flops 65536 | bytes 802816 | tf_op jit(solution)/shard_map/while/body/eval_jaxpr/scatter-add | solution.py:194
  1005.3 24.1 %scatter_fusion = f32[16,6784]{0,1:T(8,128)} fusion(f32[16,6784]{0,1:T(8,128)} %get-tuple-element.771, s32[4096]{0:T(1024)S(1)} %bitcast.142, f32[4096,16]{1,0:T(8,128)} %copy.299), kind=kCustom, calls=%fused_computation.5.clone.1 | custom fusion | flops 65536 | bytes 802816 | tf_op jit(solution)/shard_map/while/body/eval_jaxpr/scatter-add | solution.py:194
  1086.8 24.1 %scatter_fusion = f32[16,6784]{0,1:T(8,128)} fusion(f32[16,6784]{0,1:T(8,128)} %get-tuple-element.771, s32[4096]{0:T(1024)S(1)} %bitcast.142, f32[4096,16]{1,0:T(8,128)} %copy.299), kind=kCustom, calls=%fused_computation.5.clone.1 | custom fusion | flops 65536 | bytes 802816 | tf_op jit(solution)/shard_map/while/body/eval_jaxpr/scatter-add | solution.py:194
  1114.0 24.1 %scatter_fusion = f32[16,6784]{0,1:T(8,128)} fusion(f32[16,6784]{0,1:T(8,128)} %get-tuple-element.771, s32[4096]{0:T(1024)S(1)} %bitcast.142, f32[4096,16]{1,0:T(8,128)} %copy.299), kind=kCustom, calls=%fused_computation.5.clone.1 | custom fusion | flops 65536 | bytes 802816 | tf_op jit(solution)/shard_map/while/body/eval_jaxpr/scatter-add | solution.py:194
  1141.1 24.1 %scatter_fusion = f32[16,6784]{0,1:T(8,128)} fusion(f32[16,6784]{0,1:T(8,128)} %get-tuple-element.771, s32[4096]{0:T(1024)S(1)} %bitcast.142, f32[4096,16]{1,0:T(8,128)} %copy.299), kind=kCustom, calls=%fused_computation.5.clone.1 | custom fusion | flops 65536 | bytes 802816 | tf_op jit(solution)/shard_map/while/body/eval_jaxpr/scatter-add | solution.py:194
  1168.3 24.1 %scatter_fusion = f32[16,6784]{0,1:T(8,128)} fusion(f32[16,6784]{0,1:T(8,128)} %get-tuple-element.771, s32[4096]{0:T(1024)S(1)} %bitcast.142, f32[4096,16]{1,0:T(8,128)} %copy.299), kind=kCustom, calls=%fused_computation.5.clone.1 | custom fusion | flops 65536 | bytes 802816 | tf_op jit(solution)/shard_map/while/body/eval_jaxpr/scatter-add | solution.py:194
  1260.5 496.8 %while.55 = (s32[]{:T(128)}, f32[27,32,16]{1,2,0:T(8,128)}, s32[27,4096]{1,0:T(8,128)}, bf16[32,6784]{0,1:T(8,128)(2,1)S(1)}, bf16[16,4096]{1,0:T(8,128)(2,1)S(1)}, /*index=5*/s32[]{:T(128)}) while((s32[]{:T(128)}, f32[27,32,16]{1,2,0:T(8,128)}, s32[27,4096]{1,0:T(8,128)}, bf16[32,6784]{0,1:T(8,128)(2,1)S(1)}, ...), condition=%wide.region_12.14_spmd, body=%wide.region_11.13_spmd.sunk | while | flops 4366338 | bytes 1818709 | solution.py:183
  1853.9 36.9 %all-reduce = (f32[27,32,16]{1,2,0:T(8,128)}, f32[32,64]{1,0:T(8,128)}) all-reduce(f32[27,32,16]{1,2,0:T(8,128)} %get-tuple-element.369, f32[32,64]{1,0:T(8,128)S(1)} %fusion.25), channel_id=1, replica_groups=mesh['group'=2,'tx'=4,'ty'=2,'ch'=2] {'tx','ty'}, use_global_device_ids=true, to_apply=%region_13.15 | all-reduce | flops 15872 | bytes 126976 | tf_op jit(solution)/shard_map/psum | solution.py:216
  (560 shorter events, 1377.4 us)
Async XLA Ops:
  1.7 65.2 %collective-permute-start.23 = (bf16[16,256]{1,0:T(8,128)(2,1)S(1)}, bf16[16,256]{1,0:T(8,128)(2,1)S(1)}, u32[]{:S(2)}, u32[]{:S(2)}) collective-permute-start(bf16[16,256]{1,0:T(8,128)(2,1)S(1)} %get-tuple-element.600), channel_id=1, source_target_pairs={{6,0},{8,2},{10,4},{12,6},{14,8},{7,1},{9,3},{11,5},{13,7},{15,9},... | collective-permute-start | bytes 24584 | tf_op jit(solution)/shard_map/ppermute | solution.py:13
  3.0 57.5 %collective-permute-start.22 = (bf16[16,256]{1,0:T(8,128)(2,1)S(1)}, bf16[16,256]{1,0:T(8,128)(2,1)S(1)}, u32[]{:S(2)}, u32[]{:S(2)}) collective-permute-start(bf16[16,256]{1,0:T(8,128)(2,1)S(1)} %get-tuple-element.600), channel_id=1, source_target_pairs={{2,0},{4,2},{6,4},{8,6},{10,8},{12,10},{14,12},{3,1},{5,3},{7,5},{... | collective-permute-start | bytes 24584 | tf_op jit(solution)/shard_map/ppermute | solution.py:13
  4.3 51.6 %collective-permute-start.21 = (bf16[16,256]{1,0:T(8,128)(2,1)S(1)}, bf16[16,256]{1,0:T(8,128)(2,1)S(1)}, u32[]{:S(2)}, u32[]{:S(2)}) collective-permute-start(bf16[16,256]{1,0:T(8,128)(2,1)S(1)} %get-tuple-element.600), channel_id=1, source_target_pairs={{0,2},{2,4},{4,6},{6,8},{8,10},{10,12},{12,14},{1,3},{3,5},{5,7},{... | collective-permute-start | bytes 24584 | tf_op jit(solution)/shard_map/ppermute | solution.py:13
  9.8 44.8 %collective-permute-start.20 = (bf16[16,256]{1,0:T(8,128)(2,1)S(1)}, bf16[16,256]{1,0:T(8,128)(2,1)S(1)}, u32[]{:S(2)}, u32[]{:S(2)}) collective-permute-start(bf16[16,256]{1,0:T(8,128)(2,1)S(1)} %get-tuple-element.600), channel_id=1, source_target_pairs={{0,6},{2,8},{4,10},{6,12},{8,14},{1,7},{3,9},{5,11},{7,13},{9,15},... | collective-permute-start | bytes 24584 | tf_op jit(solution)/shard_map/ppermute | solution.py:13
  16.2 21.2 %collective-permute-start.16 = (bf16[16,256]{1,0:T(8,128)(2,1)S(1)}, bf16[16,256]{1,0:T(8,128)(2,1)S(1)}, u32[]{:S(2)}, u32[]{:S(2)}) collective-permute-start(bf16[16,256]{1,0:T(8,128)(2,1)S(1)} %get-tuple-element.600), channel_id=1, source_target_pairs={{0,4},{4,8},{8,12},{1,5},{5,9},{9,13},{2,6},{6,10},{10,14},{3,7},{... | collective-permute-start | bytes 24584 | tf_op jit(solution)/shard_map/ppermute | solution.py:13
  53.3 43.5 %collective-permute-start.7 = (bf16[16,128]{1,0:T(8,128)(2,1)S(1)}, bf16[16,128]{1,0:T(8,128)(2,1)S(1)}, u32[]{:S(2)}, u32[]{:S(2)}) collective-permute-start(bf16[16,128]{1,0:T(8,128)(2,1)S(1)} %get-tuple-element.595), channel_id=1, source_target_pairs={{6,0},{8,2},{10,4},{12,6},{14,8},{7,1},{9,3},{11,5},{13,7},{15,9},... | collective-permute-start | bytes 12296 | tf_op jit(solution)/shard_map/ppermute | solution.py:13
  54.6 42.2 %collective-permute-start.6 = (bf16[16,128]{1,0:T(8,128)(2,1)S(1)}, bf16[16,128]{1,0:T(8,128)(2,1)S(1)}, u32[]{:S(2)}, u32[]{:S(2)}) collective-permute-start(bf16[16,128]{1,0:T(8,128)(2,1)S(1)} %get-tuple-element.596), channel_id=1, source_target_pairs={{2,0},{4,2},{6,4},{8,6},{10,8},{12,10},{14,12},{3,1},{5,3},{7,5},{... | collective-permute-start | bytes 12296 | tf_op jit(solution)/shard_map/ppermute | solution.py:13
  55.9 40.9 %collective-permute-start.5 = (bf16[16,128]{1,0:T(8,128)(2,1)S(1)}, bf16[16,128]{1,0:T(8,128)(2,1)S(1)}, u32[]{:S(2)}, u32[]{:S(2)}) collective-permute-start(bf16[16,128]{1,0:T(8,128)(2,1)S(1)} %get-tuple-element.597), channel_id=1, source_target_pairs={{0,2},{2,4},{4,6},{6,8},{8,10},{10,12},{12,14},{1,3},{3,5},{5,7},{... | collective-permute-start | bytes 12296 | tf_op jit(solution)/shard_map/ppermute | solution.py:13
  60.5 36.3 %collective-permute-start.4 = (bf16[16,128]{1,0:T(8,128)(2,1)S(1)}, bf16[16,128]{1,0:T(8,128)(2,1)S(1)}, u32[]{:S(2)}, u32[]{:S(2)}) collective-permute-start(bf16[16,128]{1,0:T(8,128)(2,1)S(1)} %get-tuple-element.598), channel_id=1, source_target_pairs={{0,6},{2,8},{4,10},{6,12},{8,14},{1,7},{3,9},{5,11},{7,13},{9,15},... | collective-permute-start | bytes 12296 | tf_op jit(solution)/shard_map/ppermute | solution.py:13
  66.9 14.7 collective-permute-start
  1759.8 59.4 %collective-permute-start.10 = (f32[16,256]{1,0:T(8,128)}, f32[16,256]{1,0:T(8,128)}, u32[]{:S(2)}, u32[]{:S(2)}) collective-permute-start(f32[16,256]{1,0:T(8,128)} %bitcast.108), channel_id=1, source_target_pairs={{0,2},{1,3},{4,6},{5,7},{8,10},{9,11},{12,14},{13,15},{16,18},{17,... | collective-permute-start | bytes 49160 | tf_op jit(solution)/shard_map/ppermute | solution.py:13
  1762.0 58.5 %collective-permute-start.11 = (f32[16,256]{1,0:T(8,128)}, f32[16,256]{1,0:T(8,128)}, u32[]{:S(2)}, u32[]{:S(2)}) collective-permute-start(f32[16,256]{1,0:T(8,128)} %bitcast.111), channel_id=1, source_target_pairs={{2,0},{3,1},{6,4},{7,5},{10,8},{11,9},{14,12},{15,13},{18,16},{19,... | collective-permute-start | bytes 49160 | tf_op jit(solution)/shard_map/ppermute | solution.py:13
  1763.3 58.5 %collective-permute-start.9 = (f32[16,256]{1,0:T(8,128)}, f32[16,256]{1,0:T(8,128)}, u32[]{:S(2)}, u32[]{:S(2)}) collective-permute-start(f32[16,256]{1,0:T(8,128)} %bitcast.109), channel_id=1, source_target_pairs={{4,0},{8,4},{12,8},{5,1},{9,5},{13,9},{6,2},{10,6},{14,10},{7,3},{... | collective-permute-start | bytes 49160 | tf_op jit(solution)/shard_map/ppermute | solution.py:13
  1764.6 61.8 %collective-permute-start.8 = (f32[16,256]{1,0:T(8,128)}, f32[16,256]{1,0:T(8,128)}, u32[]{:S(2)}, u32[]{:S(2)}) collective-permute-start(f32[16,256]{1,0:T(8,128)} %bitcast.110), channel_id=1, source_target_pairs={{0,4},{4,8},{8,12},{1,5},{5,9},{9,13},{2,6},{6,10},{10,14},{3,7},{... | collective-permute-start | bytes 49160 | tf_op jit(solution)/shard_map/ppermute | solution.py:13
  1770.0 6.5 collective-permute-start.31
  1776.5 7.3 collective-permute-start.29
  1783.8 5.8 collective-permute-start.30
  1794.6 6.8 collective-permute-start.15
  1806.5 5.9 collective-permute-start.14
  1812.4 19.5 %collective-permute-start.12 = (f32[16,256]{1,0:T(8,128)S(1)}, f32[16,256]{1,0:T(8,128)S(1)}, u32[]{:S(2)}, u32[]{:S(2)}) collective-permute-start(f32[16,256]{1,0:T(8,128)S(1)} %bitcast.154), channel_id=1, source_target_pairs={{0,6},{2,8},{4,10},{6,12},{8,14},{1,7},{3,9},{5,11},{7,13},{9,15},... | collective-permute-start | bytes 49160 | tf_op jit(solution)/shard_map/ppermute | solution.py:13
  1819.3 16.2 collective-permute-start.27
  1820.6 14.9 collective-permute-start.25
  1821.9 13.6 collective-permute-start.26
  1826.4 9.1 collective-permute-start.24
  (16 other events, 1238.6 us)
where the time goes:
time: 1900 us; the launch traced here: 1890 us
  local copies, waits for them, and re-layouts  869 us (46%)
  other arithmetic  704 us (37%)
  matrix products  139 us (7%)
  starting transfers between devices  91.8 us (5%)
  blocking collectives  42.8 us (2%)
  waiting for transfers between devices  42 us (2%)
    scatter-add x27, other arithmetic, input_step(): grads.at[:, lax.dynamic_index_in_dim(neighbours, offset, 0, keepdims=False)]  651 us
    gather x27, local copies, waits for them, and re-layouts, weight_step(): jnp.take(ext_full, lax.dynamic_index_in_dim(neighbours, offset, 0, keepdi...  402 us
    gather x27, local copies, waits for them, and re-layouts, forward_step(): jnp.take(ext_full, lax.dynamic_index_in_dim(neighbours, offset, 0, keepdi...  328 us
    ppermute x32, starting transfers between devices, from_behind(): return lax.ppermute(value, axis, pairs)  91.8 us
    dot_general x27, matrix products, weight_step(): lax.dot_general(picked, hidden_grad, (((1,), (1,)), ((), ())), preferred_...  69.2 us
    dot_general x27, matrix products, forward_step(): lax.dot_general(weight, picked, (((0,), (0,)), ((), ())), preferred_eleme...  54.4 us
    dot_general x27, local copies, waits for them, and re-layouts, input_step(): contrib = jnp.dot(weight, full_grad, preferred_element_type=jnp.float32)  52.7 us
    ppermute x32, waiting for transfers between devices, from_behind(): return lax.ppermute(value, axis, pairs)  42 us
  transfers between devices with their start and end apart: 32, of which 13 were waited for; matrix products, arithmetic and copies ran while one was open for 2% of the time, Pallas kernels for 0%

commit v1 on v0

v1 whole, which is shorter than its diff:
```python
import functools

import jax
import jax.numpy as jnp
from jax import lax
from jax.experimental import pallas as pl
from jax.experimental.pallas import tpu as pltpu
from jax.sharding import PartitionSpec as P

BF = jnp.bfloat16
F32 = jnp.float32
FACE_STEPS = ((-1, 0), (1, 0), (0, -1), (0, 1))
CORNER_STEPS = ((-1, -1), (-1, 1), (1, -1), (1, 1))
LOW = 256
VMEM_LIMIT = 56 << 20


def call(kernel, name, outs, scratch, flops, *args, smem=1):
    specs = [pl.BlockSpec(memory_space=pltpu.SMEM)] * smem
    specs += [pl.BlockSpec(memory_space=pltpu.VMEM)] * (len(args) - smem)
    return pl.pallas_call(
        kernel,
        name=name,
        out_shape=[jax.ShapeDtypeStruct(s, d) for s, d in outs],
        in_specs=specs,
        out_specs=[pl.BlockSpec(memory_space=pltpu.VMEM)] * len(outs),
        scratch_shapes=[pltpu.VMEM(s, d) for s, d in scratch],
        compiler_params=pltpu.CompilerParams(vmem_limit_bytes=VMEM_LIMIT),
        cost_estimate=pl.CostEstimate(flops=flops, bytes_accessed=1 << 20, transcendentals=0),
    )(*args)


class Plan:
    def __init__(self, shapes, nx, ny, nch):
        features, neighbours, face_send, corner_send, coarse_weight, coarse_grad = shapes
        self.nx, self.ny, self.nch = nx, ny, nch
        self.share, self.voxels = features
        self.channels = self.share * nch
        self.offsets = neighbours[0]
        self.half = self.voxels // nch
        self.face, self.corner = face_send[1], corner_send[1]
        self.coarse_channels, self.coarse = coarse_grad
        self.coarse_share = self.coarse_channels // nch
        self.own_blocks = self.voxels // LOW
        self.paired = ny == 2
        self.widths = [self.face] * (3 if self.paired else 4)
        self.widths += [self.corner] * (2 if self.paired else 4)
        self.slots = len(self.widths)
        self.halo = sum(self.widths)
        self.halo_blocks = self.halo // LOW
        self.starts = [sum(self.widths[:s]) for s in range(self.slots)]
        self.nothing = self.voxels + self.halo

    def pairs(self, slot):
        steps = FACE_STEPS + CORNER_STEPS
        if self.paired:
            directions = ((0,), (1,), (2, 3), (4, 5), (6, 7))[slot]
        else:
            directions = (slot,)
        found = []
        for x in range(self.nx):
            for y in range(self.ny):
                for d in directions:
                    sx, sy = x + steps[d][0], y + steps[d][1]
                    if 0 <= sx < self.nx and 0 <= sy < self.ny:
                        found.append((sx * self.ny + sy, x * self.ny + y))
        return found

    def send_rows(self, slot, y, face, corner):
        if not self.paired:
            if slot < 4:
                index = (1, 0, 3, 2)[slot]
                return face[index : index + 1, :]
            index = (3, 2, 1, 0)[slot - 4]
            return corner[index : index + 1, :]
        if slot == 0:
            return face[1:2, :]
        if slot == 1:
            return face[0:1, :]
        if slot == 2:
            return jnp.where(y == 0, face[3:4, :], face[2:3, :])
        if slot == 3:
            return jnp.where(y == 0, corner[3:4, :], corner[2:3, :])
        return jnp.where(y == 0, corner[1:2, :], corner[0:1, :])

    def rows(self, index, y):
        if not self.paired:
            return jnp.minimum(index, self.nothing)
        v, f, c = self.voxels, self.face, self.corner
        along_y = v + 2 * f
        corners = v + 4 * f
        end = corners + 4 * c
        mine = jnp.where(y == 0, along_y + f, along_y)
        of_y = jnp.where((index >= mine) & (index < mine + f), index - mine + along_y, self.nothing)
        result = jnp.where(index < along_y, index, of_y)
        first = jnp.where(y == 0, c, 0)
        at = index - corners - first
        one = jnp.where((at >= 0) & (at < c), at + v + 3 * f, self.nothing)
        two = jnp.where((at >= 2 * c) & (at < 3 * c), at - c + v + 3 * f, one)
        return jnp.where((index >= corners) & (index < end), two, result)

    def owner_slots(self, side):
        if not self.paired:
            return side
        return jnp.where(side < 3, side, jnp.where(side < 5, 3, jnp.where(side < 7, 4, 5)))


def forward(plan, slot, value):
    return lax.ppermute(value, ("tx", "ty"), plan.pairs(slot))


def backward(plan, slot, value):
    return lax.ppermute(value, ("tx", "ty"), [(b, a) for a, b in plan.pairs(slot)])


def lows(low, height, width):
    iota = lax.broadcasted_iota(jnp.int32, (height, width), 0).astype(BF)
    return jnp.where(iota == low, BF(1), BF(0))


def prepare_kernel(plan, place, neighbours, side, slot, high_out, low_out, side_out, slot_out):
    core, y = place[0], place[1]
    mine = pl.ds(pl.multiple_of(core * plan.half, plan.half), plan.half)
    rows = plan.rows(neighbours[:, mine], y)
    pad = high_out.shape[0] - plan.offsets
    fill = jnp.zeros((pad, plan.half), jnp.int32)
    rows = jnp.concatenate([rows, fill], axis=0) if pad else rows
    high_out[...] = lax.shift_right_logical(rows, 8).astype(F32)
    low_out[...] = (rows & (LOW - 1)).astype(F32)
    side_out[...] = plan.owner_slots(side[:, mine]).astype(F32)
    slot_out[...] = slot[:, mine].astype(F32)


def pack_kernel(plan, place, own, other, face, corner, coarse_grad, table, *messages):
    core, y = place[0], place[1]
    s, n = plan.share, plan.channels
    at_own = pl.multiple_of(core * s, s)
    at_other = pl.multiple_of((1 - core) * s, s)
    for b in range(plan.own_blocks):
        table[pl.ds(b * n + at_own, s), :] = own[:, b * LOW : (b + 1) * LOW]
        table[pl.ds(b * n + at_other, s), :] = other[:, b * LOW : (b + 1) * LOW]
    groups = plan.coarse_channels // n
    for k in range(plan.slots):
        width = plan.widths[k]
        rows = plan.send_rows(k, y, face, corner)
        high = lax.shift_right_logical(rows, 8)
        hot = lows((rows & (LOW - 1)).astype(F32).astype(BF), LOW, width)
        part = jnp.dot(table[...], hot, preferred_element_type=F32)
        picked = jnp.zeros((n, width), F32)
        for b in range(plan.own_blocks):
            picked = jnp.where(high == b, part[b * n : (b + 1) * n], picked)
        messages[k][:, :width] = picked.astype(BF)
        for g in range(groups):
            at = width + g * plan.coarse
            messages[k][:, at : at + plan.coarse] = coarse_grad[g * n : (g + 1) * n, :]


def gather_loop(plan, table, high_ref, low_ref, out, base, blocks, before):
    n = plan.channels
    group = 9 if plan.offsets % 9 == 0 else 1
    steps = plan.offsets // group

    def body(step, carry):
        fs = pl.ds(pl.multiple_of((step // steps) * LOW, LOW), LOW)
        for u in range(group):
            k = (step % steps) * group + u
            at = pl.ds(pl.multiple_of(k * n, n), n)
            low = low_ref[pl.ds(k, 1), fs].astype(BF)
            high = high_ref[pl.ds(k, 1), fs]
            part = jnp.dot(table[...], lows(low, LOW, LOW), preferred_element_type=F32)
            if before is None:
                picked = jnp.zeros((n, LOW), F32)
            else:
                picked = before[at, fs].astype(F32)
            for b in range(blocks):
                picked = jnp.where(high == base + b, part[b * n : (b + 1) * n], picked)
            out[at, fs] = picked.astype(BF)
        return carry

    lax.fori_loop(0, plan.half // LOW * steps, body, 0)


def own_gather_kernel(plan, table, high, low, out):
    gather_loop(plan, table, high, low, out, 0, plan.own_blocks, None)


def middle_kernel(plan, place, *refs):
    n, s, m = plan.channels, plan.share, plan.coarse
    messages, refs = refs[: plan.slots], refs[plan.slots :]
    before, high, low, side, slot, weight, coarse_weight, coarse_grad, refs = (*refs[:8], refs[8:])
    grad_out, mine_out, theirs_out, refs = (*refs[:3], refs[3:])
    parts_out, refs = refs[: plan.slots + 1], refs[plan.slots + 1 :]
    table, rows, coarse_all, pooled_all, sums, parts = refs
    core = place[0]
    for k in range(plan.slots):
        for part in range(0, plan.widths[k], min(LOW, plan.widths[k])):
            width = min(LOW, plan.widths[k])
            at = plan.starts[k] + part
            b, column = at // LOW, at % LOW
            table[b * n : (b + 1) * n, column : column + width] = messages[k][:, part : part + width]
    gather_loop(plan, table, high, low, rows, plan.own_blocks, plan.halo_blocks, before)

    groups = plan.coarse_channels // n
    coarse_all[:, :m] = coarse_grad[...]
    for k in range(plan.slots):
        for g in range(groups):
            at = plan.widths[k] + g * m
            coarse_all[g * n : (g + 1) * n, (k + 1) * m : (k + 2) * m] = messages[k][:, at : at + m]
    grads = jnp.dot(coarse_weight[...], coarse_all[...], preferred_element_type=F32).astype(BF)
    owners = plan.slots + 1
    for k in range(owners):
        pooled_all[k * n : (k + 1) * n, :] = grads[:, k * m : (k + 1) * m]
    chunk = min(plan.half, 512)
    wide = plan.offsets * n
    sums[...] = jnp.zeros_like(sums)
    parts[...] = jnp.zeros_like(parts)
    for c in range(plan.half // chunk):
        fs = slice(c * chunk, (c + 1) * chunk)
        picked = rows[:, fs]
        hidden = lax.dot_general(
            weight[...], picked, (((0,), (0,)), ((), ())), preferred_element_type=F32
        )
        sigma = 1.0 / (1.0 + jnp.exp(-hidden))
        active = (hidden * sigma).astype(BF)
        owner = side[:, fs]
        owner_low = owner.astype(BF)
        hot = lows(slot[:, fs].astype(BF), m, chunk)
        spread = jnp.concatenate(
            [jnp.where(owner_low == BF(k), active, BF(0)) for k in range(owners)], axis=0
        )
        parts[...] += lax.dot_general(
            spread, hot, (((1,), (1,)), ((), ())), preferred_element_type=F32
        )
        found = jnp.dot(pooled_all[...], hot, preferred_element_type=F32)
        above = jnp.zeros((n, chunk), F32)
        for k in range(owners):
            above = jnp.where(owner == float(k), found[k * n : (k + 1) * n], above)
        grad = (above * (sigma * (1.0 + hidden * (1.0 - sigma)))).astype(BF)
        grad_out[:, fs] = grad
        sums[:, :wide] += lax.dot_general(
            grad, picked, (((1,), (1,)), ((), ())), preferred_element_type=F32
        )
    total = jnp.zeros((plan.coarse_channels, n), F32)
    for k in range(owners):
        value = parts[k * n : (k + 1) * n, :]
        parts_out[k][...] = value
        first = value.astype(BF)
        second = (value - first.astype(F32)).astype(BF)
        grads_k = coarse_all[:, k * m : (k + 1) * m]
        for piece in (first, second):
            total = total + lax.dot_general(
                grads_k, piece, (((1,), (1,)), ((), ())), preferred_element_type=F32
            )
    pieces = plan.coarse_share // s
    start = sums.shape[1] - pieces * n
    for h in range(plan.nch):
        for q in range(pieces):
            row = h * plan.coarse_share + q * s
            sums[h * s : (h + 1) * s, start + q * n : start + (q + 1) * n] = total[row : row + s]
    mine_out[...] = sums[pl.ds(pl.multiple_of(core * s, s), s), :]
    theirs_out[...] = sums[pl.ds(pl.multiple_of((1 - core) * s, s), s), :]


def scatter_loop(plan, values, high_ref, low_ref, total, base, blocks):
    group = 9 if plan.offsets % 9 == 0 else 1
    steps = plan.offsets // group
    width = min(plan.half, 512)
    n = plan.channels
    total[...] = jnp.zeros_like(total)

    def body(step, carry):
        fs = pl.ds(pl.multiple_of((step // steps) * width, width), width)
        masked, hots = [], []
        for u in range(group):
            k = (step % steps) * group + u
            high = high_ref[pl.ds(k, 1), fs].astype(BF)
            hots.append(lows(low_ref[pl.ds(k, 1), fs].astype(BF), LOW, width))
            value = values[pl.ds(pl.multiple_of(k * n, n), n), fs]
            masked.append(
                jnp.concatenate(
                    [jnp.where(high == BF(base + b), value, BF(0)) for b in range(blocks)], axis=0
                )
            )
        total[...] += lax.dot_general(
            jnp.concatenate(masked, axis=1),
            jnp.concatenate(hots, axis=1),
            (((1,), (1,)), ((), ())),
            preferred_element_type=F32,
        )
        return carry

    lax.fori_loop(0, plan.half // width * steps, body, 0)


def spread_values(plan, weight, grad, values):
    chunk = min(plan.half, 512)
    for c in range(plan.half // chunk):
        fs = slice(c * chunk, (c + 1) * chunk)
        values[:, fs] = jnp.dot(weight[...], grad[:, fs], preferred_element_type=F32).astype(BF)


def halo_scatter_kernel(plan, weight, grad, high, low, *refs):
    outs, (values, total) = refs[: plan.slots], refs[plan.slots :]
    n = plan.channels
    spread_values(plan, weight, grad, values)
    scatter_loop(plan, values, high, low, total, plan.own_blocks, plan.halo_blocks)
    for k in range(plan.slots):
        width = min(LOW, plan.widths[k])
        for part in range(0, plan.widths[k], width):
            at = plan.starts[k] + part
            b, column = at // LOW, at % LOW
            outs[k][:, part : part + width] = total[b * n : (b + 1) * n, column : column + width].astype(BF)


def own_scatter_kernel(plan, weight, grad, high, low, total, values):
    spread_values(plan, weight, grad, values)
    scatter_loop(plan, values, high, low, total, 0, plan.own_blocks)


def final_kernel(plan, place, total, face, corner, *refs):
    messages, (mine_out, theirs_out, work) = refs[: plan.slots], refs[plan.slots :]
    core, y = place[0], place[1]
    n, s = plan.channels, plan.share
    masked, hots = [], []
    for k in range(plan.slots):
        rows = plan.send_rows(k, y, face, corner)
        high = lax.shift_right_logical(rows, 8).astype(F32).astype(BF)
        hots.append(lows((rows & (LOW - 1)).astype(F32).astype(BF), LOW, plan.widths[k]))
        value = messages[k][...]
        masked.append(
            jnp.concatenate(
                [jnp.where(high == BF(b), value, BF(0)) for b in range(plan.own_blocks)], axis=0
            )
        )
    work[...] = total[...] + lax.dot_general(
        jnp.concatenate(masked, axis=1),
        jnp.concatenate(hots, axis=1),
        (((1,), (1,)), ((), ())),
        preferred_element_type=F32,
    )
    at_own = pl.multiple_of(core * s, s)
    at_other = pl.multiple_of((1 - core) * s, s)
    for b in range(plan.own_blocks):
        mine_out[:, b * LOW : (b + 1) * LOW] = work[pl.ds(b * n + at_own, s), :]
        theirs_out[:, b * LOW : (b + 1) * LOW] = work[pl.ds(b * n + at_other, s), :]


def coarse_kernel(plan, place, mine, theirs, weight, out):
    share = plan.coarse_share
    pooled = (mine[...] + theirs[...]).astype(BF)
    wide = lax.dot_general(
        weight[...], pooled, (((0,), (0,)), ((), ())), preferred_element_type=F32
    ).astype(BF)
    out[...] = jnp.where(place[0] == 0, wide[:share], wide[share:])


def sum_over(value, axis):
    count = lax.axis_size(axis)
    if count & (count - 1):
        return lax.psum(value, axis)
    distance = 1
    while distance < count:
        pairs = [(i, i ^ distance) for i in range(count)]
        value = value + lax.ppermute(value, axis, pairs)
        distance *= 2
    return value


def shards(
    fine_features,
    neighbours,
    face_send,
    corner_send,
    owner_side,
    owner_slot,
    conv_weight,
    coarse_weight,
    coarse_grad,
):
    nx, ny, nch = (lax.axis_size(a) for a in ("tx", "ty", "ch"))
    plan = Plan(
        [
            a.shape
            for a in (fine_features, neighbours, face_send, corner_send, coarse_weight, coarse_grad)
        ],
        nx,
        ny,
        nch,
    )
    n, s, half, m = plan.channels, plan.share, plan.half, plan.coarse
    swap = [(0, 1), (1, 0)]
    wide = plan.offsets * n
    bind = functools.partial
    place = jnp.stack([lax.axis_index("ch"), lax.axis_index("ty")]).astype(jnp.int32)

    other = lax.ppermute(fine_features, "ch", swap)
    tall = -(-plan.offsets // 8) * 8
    high, low, side, slot = call(
        bind(prepare_kernel, plan),
        "prepare",
        [((tall, half), F32), ((tall, half), F32), ((1, half), F32), ((1, half), F32)],
        [],
        1 << 20,
        place,
        neighbours,
        owner_side.reshape(1, -1),
        owner_slot.reshape(1, -1),
    )
    extra = plan.coarse_channels // n * m
    table, *sent = call(
        bind(pack_kernel, plan),
        "pack",
        [((plan.own_blocks * n, LOW), BF)] + [((n, w + extra), BF) for w in plan.widths],
        [],
        1 << 30,
        place,
        fine_features,
        other,
        face_send,
        corner_send,
        coarse_grad,
    )
    received = [forward(plan, k, sent[k]) for k in range(plan.slots)]
    work = 2 * wide * half * LOW
    (before,) = call(
        bind(own_gather_kernel, plan),
        "own_gather",
        [((wide, half), BF)],
        [],
        work * plan.own_blocks,
        table,
        high,
        low,
        smem=0,
    )
    weight = conv_weight.reshape(wide, n)
    owners = plan.slots + 1
    pieces = plan.coarse_share // s
    across = -(-wide // 128) * 128 + pieces * n
    grad, mine, theirs, *parts = call(
        bind(middle_kernel, plan),
        "middle",
        [((n, half), BF), ((s, across), F32), ((s, across), F32)] + [((n, m), F32)] * owners,
        [
            ((plan.halo_blocks * n, LOW), BF),
            ((wide, half), BF),
            ((plan.coarse_channels, owners * m), BF),
            ((owners * n, m), BF),
            ((n, across), F32),
            ((owners * n, m), F32),
        ],
        work * plan.halo_blocks,
        place,
        *received,
        before,
        high,
        low,
        side,
        slot,
        weight,
        coarse_weight,
        coarse_grad,
    )
    mine = mine + lax.ppermute(theirs, "ch", swap)
    returned = [backward(plan, k, parts[k + 1]) for k in range(plan.slots)]
    halo = call(
        bind(halo_scatter_kernel, plan),
        "halo_scatter",
        [((n, w), BF) for w in plan.widths],
        [((wide, half), BF), ((plan.halo_blocks * n, LOW), F32)],
        work * plan.halo_blocks,
        weight,
        grad,
        high,
        low,
        smem=0,
    )
    halo_back = [backward(plan, k, halo[k]) for k in range(plan.slots)]
    (total,) = call(
        bind(own_scatter_kernel, plan),
        "own_scatter",
        [((plan.own_blocks * n, LOW), F32)],
        [((wide, half), BF)],
        work * plan.own_blocks,
        weight,
        grad,
        high,
        low,
        smem=0,
    )
    pooled = sum(returned, parts[0])
    pooled_other = lax.ppermute(pooled, "ch", swap)
    (coarse_out,) = call(
        bind(coarse_kernel, plan),
        "coarse",
        [((plan.coarse_share, m), BF)],
        [],
        1 << 24,
        place,
        pooled,
        pooled_other,
        coarse_weight,
    )
    mine = sum_over(sum_over(mine, "ty"), "tx")
    final_mine, final_theirs = call(
        bind(final_kernel, plan),
        "final",
        [((s, plan.voxels), F32)] * 2,
        [((plan.own_blocks * n, LOW), F32)],
        1 << 30,
        place,
        total,
        face_send,
        corner_send,
        *halo_back,
    )
    input_grad = (final_mine + lax.ppermute(final_theirs, "ch", swap)).astype(BF)
    conv_weight_grad = mine[:, :wide].reshape(s, plan.offsets, n).transpose(1, 2, 0)
    coarse_part = mine[:, across - pieces * n :].reshape(s, pieces, n)
    coarse_weight_grad = coarse_part.transpose(2, 1, 0).reshape(n, plan.coarse_share)
    return (coarse_out, input_grad, conv_weight_grad, coarse_weight_grad)


def solution(mesh):
    tiles = ("group", "tx", "ty")
    in_specs = (
        P("ch", tiles),
        P(None, tiles),
        P(None, tiles),
        P(None, tiles),
        P(tiles),
        P(tiles),
        P(),
        P(),
        P(None, tiles),
    )
    out_specs = (
        P("ch", tiles),
        P("ch", tiles),
        P("group", None, "ch"),
        P("group", "ch"),
    )
    return jax.shard_map(shards, mesh=mesh, in_specs=in_specs, out_specs=out_specs, check_vma=False)
```

time: 1900 us -> 141 us (0.07)
  local copies, waits for them, and re-layouts: 869 us -> 3.7 us
  other arithmetic: 704 us -> 3.13 us
  matrix products: 139 us -> 0 us
  Pallas kernels: 0 us -> 81.5 us
  starting transfers between devices: 91.8 us -> 46.6 us
  blocking collectives: 42.8 us -> 0 us
  waiting for transfers between devices: 42 us -> 4.19 us
    gather x60 -> x0, local copies, waits for them, and re-layouts: 750 us -> none  [the longest x27 402 us: weight_step(): jnp.take(ext_full, lax.dynamic_index_in_dim(neighbours, offset, 0, keepdi...]
    scatter-add x29 -> x0, other arithmetic: 668 us -> none  [the longest x27 651 us: input_step(): grads.at[:, lax.dynamic_index_in_dim(neighbours, offset, 0, keepdims=False)]]
    dot_general x92 -> x0, matrix products: 139 us -> none  [the longest x27 69.2 us: weight_step(): lax.dot_general(picked, hidden_grad, (((1,), (1,)), ((), ())), preferred_...]
    pallas_call x0 -> x8, Pallas kernels: none -> 81.5 us  [call(): pl.pallas_call(kernel, name=name, out_shape=[jax.ShapeDtypeStruct(s, d) f...]
    dot_general x27 -> x0, local copies, waits for them, and re-layouts: 52.7 us -> none  [input_step(): contrib = jnp.dot(weight, full_grad, preferred_element_type=jnp.float32)]
    dynamic_slice x64 -> x0, local copies, waits for them, and re-layouts: 50.5 us -> none  [the longest x27 24.9 us: forward_step(): lax.dynamic_index_in_dim(neighbours, offset, 0, keepdims=False)]
    ppermute x32 -> x22, starting transfers between devices: 91.8 us -> 46.6 us  [the longest x10 27.9 us: backward(): lax.ppermute(value, ('tx', 'ty'), [(b, a) for a, b in plan.pairs(slot)])]
    ppermute x32 -> x22, waiting for transfers between devices: 42 us -> 4.19 us  [the longest x3 1.64 us: sum_over(): value = value + lax.ppermute(value, axis, pairs)]
  transfers between devices with their start and end apart: 32 -> 22, of which waited for: 13 -> 3; matrix products, arithmetic and copies ran while one was open for 2% -> 2% of each run, Pallas kernels for 0% -> 44%
where the time goes in v1:
time: 141 us; the launch traced here: 140 us
  Pallas kernels  81.5 us (58%)
  starting transfers between devices  46.6 us (33%)
  waiting for transfers between devices  4.19 us (3%)
  local copies, waits for them, and re-layouts  3.7 us (3%)
  other arithmetic  3.13 us (2%)
    pallas_call x8, Pallas kernels, call(): pl.pallas_call(kernel, name=name, out_shape=[jax.ShapeDtypeStruct(s, d) f...  81.5 us
    ppermute x10, starting transfers between devices, backward(): lax.ppermute(value, ('tx', 'ty'), [(b, a) for a, b in plan.pairs(slot)])  27.9 us
    ppermute x5, starting transfers between devices, forward(): return lax.ppermute(value, ('tx', 'ty'), plan.pairs(slot))  14.1 us
    ppermute x3, starting transfers between devices, sum_over(): value = value + lax.ppermute(value, axis, pairs)  3.74 us
    unnamed x40, local copies, waits for them, and re-layouts  3.5 us
  transfers between devices with their start and end apart: 22, of which 3 were waited for; matrix products, arithmetic and copies ran while one was open for 2% of the time, Pallas kernels for 44%

profile of v1, /device:TPU:0, one launch (start us, length us, event | category | flops | bytes accessed | tf_op | source)
XLA Modules:
  0.0 140.2 jit_solution(14579653663939385421)
XLA Ops:
  1.8 2.1 %prepare.1 = (f32[32,2048]{1,0:T(8,128)}, f32[32,2048]{1,0:T(8,128)}, f32[1,2048]{1,0:T(1,128)}, f32[1,2048]{1,0:T(1,128)}) custom-call(s32[2]{0:T(128)} %pad_add_fusion.place, s32[27,4096]{1,0:T(8,128)} %neighbours.1, s32[1,4096]{1,0:T(1,128)} %bitcast.11, s32[1,4096]{1,0:T(1,128)} %bitcast.12), custom_call_target="tpu_custom_call" | custom-call | flops 1048576 | bytes 1048576 | tf_op jit(solution)/shard_map/prepare/pallas_call | solution.py:21
  4.6 2.4 %pack.1 = (bf16[512,256]{1,0:T(8,128)(2,1)}, bf16[32,1536]{1,0:T(8,128)(2,1)}, bf16[32,1536]{1,0:T(8,128)(2,1)}, bf16[32,1536]{1,0:T(8,128)(2,1)}, bf16[32,1152]{1,0:T(8,128)(2,1)}, /*index=5*/bf16[32,1152]{1,0:T(8,128)(2,1)}) custom-call(s32[2]{0:T(128)} %pad_add_fusion.place, bf16[16,4096]{1,0:T(8,128)(2,1)} %own.1, bf16[16,4096]{1,0:T(8,128)(2,1)} %copy-done.3, ...), custom_call_target="tpu_custom_call" | custom-call | flops 1073741824 | bytes 1048576 | tf_op jit(solution)/shard_map/pack/pallas_call | solution.py:21
  7.0 5.4 %collective-permute-start.4 = (bf16[32,1152]{1,0:T(8,128)(2,1)}, bf16[32,1152]{1,0:T(8,128)(2,1)S(1)}, u32[]{:S(2)}, u32[]{:S(2)}) collective-permute-start(bf16[32,1152]{1,0:T(8,128)(2,1)} %get-tuple-element.33), channel_id=1, source_target_pairs={{2,4},{0,6},{6,8},{4,10},{10,12},{8,14},{3,5},{1,7},{7,9},{5,11},{... | collective-permute-start | bytes 221192 | tf_op jit(solution)/shard_map/ppermute | solution.py:109
  12.4 1.3 collective-permute-start.5
  13.7 4.5 %collective-permute-start.1 = (bf16[32,1536]{1,0:T(8,128)(2,1)}, bf16[32,1536]{1,0:T(8,128)(2,1)S(1)}, u32[]{:S(2)}, u32[]{:S(2)}) collective-permute-start(bf16[32,1536]{1,0:T(8,128)(2,1)} %get-tuple-element.30), channel_id=1, source_target_pairs={{0,4},{2,6},{4,8},{6,10},{8,12},{10,14},{1,5},{3,7},{5,9},{7,11},{... | collective-permute-start | bytes 294920 | tf_op jit(solution)/shard_map/ppermute | solution.py:109
  18.2 1.3 collective-permute-start.2
  19.5 1.6 %collective-permute-start.3 = (bf16[32,1536]{1,0:T(8,128)(2,1)}, bf16[32,1536]{1,0:T(8,128)(2,1)S(1)}, u32[]{:S(2)}, u32[]{:S(2)}) collective-permute-start(bf16[32,1536]{1,0:T(8,128)(2,1)} %get-tuple-element.32), channel_id=1, source_target_pairs={{2,0},{0,2},{6,4},{4,6},{10,8},{8,10},{14,12},{12,14},{3,1},{1,3},... | collective-permute-start | bytes 294920 | tf_op jit(solution)/shard_map/ppermute | solution.py:109
  21.1 22.0 %own_gather.1.refs_5_ = bf16[864,2048]{1,0:T(8,128)(2,1)} custom-call(bf16[512,256]{1,0:T(8,128)(2,1)} %get-tuple-element.35.table, f32[32,2048]{1,0:T(8,128)} %get-tuple-element.36.high.refs_6_, f32[32,2048]{1,0:T(8,128)} %get-tuple-element.37.low.refs_7_), custom_call_target="tpu_custom_call" | custom-call | flops 14495514624 | bytes 1048576 | tf_op jit(solution)/shard_map/own_gather/pallas_call | solution.py:21
  43.9 16.7 %middle.1 = (bf16[32,2048]{1,0:T(8,128)(2,1)}, f32[16,1024]{1,0:T(8,128)}, f32[16,1024]{1,0:T(8,128)}, f32[32,256]{1,0:T(8,128)}, f32[32,256]{1,0:T(8,128)}, /*i...) custom-call(s32[2]{0:T(128)} %pad_add_fusion.place, bf16[32,1536]{1,0:T(8,128)(2,1)} %copy-done.4, ...), custom_call_target="tpu_custom_call" | custom-call | flops 6341787648 | bytes 1048576 | tf_op jit(solution)/shard_map/middle/pallas_call | solution.py:21
  60.7 1.5 %collective-permute-done.18 = f32[16,1024]{1,0:T(8,128)S(1)} collective-permute-done((f32[16,1024]{1,0:T(8,128)}, f32[16,1024]{1,0:T(8,128)S(1)}, u32[]{:S(2)}, u32[]{:S(2)}) %collective-permute-start.18) | collective-permute-done | bytes 65568 | tf_op jit(solution)/shard_map/ppermute | solution.py:464
  63.6 13.6 %halo_scatter.1 = (bf16[32,512]{1,0:T(8,128)(2,1)}, bf16[32,512]{1,0:T(8,128)(2,1)}, bf16[32,512]{1,0:T(8,128)(2,1)}, bf16[32,128]{1,0:T(8,128)(2,1)}, bf16[32,128]{1,0:T(8,128)(2,1)}) custom-call(bf16[864,32]{1,0:T(8,128)(2,1)} %bitcast.14, bf16[32,2048]{1,0:T(8,128)(2,1)} %get-tuple-element.46.grad, f32[32,2048]{1,0:T(8,128)} %get-tuple-element.36.high.refs_6_, ...), custom_call_target="tpu_custom_call" | custom-call | flops 6341787648 | bytes 1048576 | tf_op jit(solution)/shard_map/halo_scatter/pallas_call | solution.py:21
  78.4 6.1 %collective-permute-start.16 = (bf16[32,128]{1,0:T(8,128)(2,1)}, bf16[32,128]{1,0:T(8,128)(2,1)S(1)}, u32[]{:S(2)}, u32[]{:S(2)}) collective-permute-start(bf16[32,128]{1,0:T(8,128)(2,1)} %get-tuple-element.51), channel_id=1, source_target_pairs={{0,6},{2,4},{4,10},{6,8},{8,14},{10,12},{1,7},{3,5},{5,11},{7,9},{... | collective-permute-start | bytes 24584 | tf_op jit(solution)/shard_map/ppermute | solution.py:113
  84.6 1.3 collective-permute-start.12
  85.9 4.5 %collective-permute-start.13 = (bf16[32,512]{1,0:T(8,128)(2,1)}, bf16[32,512]{1,0:T(8,128)(2,1)S(1)}, u32[]{:S(2)}, u32[]{:S(2)}) collective-permute-start(bf16[32,512]{1,0:T(8,128)(2,1)} %get-tuple-element.48), channel_id=1, source_target_pairs={{0,4},{2,6},{4,8},{6,10},{8,12},{10,14},{1,5},{3,7},{5,9},{7,11},{... | collective-permute-start | bytes 98312 | tf_op jit(solution)/shard_map/ppermute | solution.py:113
  90.4 1.5 %collective-permute-start.14 = (bf16[32,512]{1,0:T(8,128)(2,1)}, bf16[32,512]{1,0:T(8,128)(2,1)S(1)}, u32[]{:S(2)}, u32[]{:S(2)}) collective-permute-start(bf16[32,512]{1,0:T(8,128)(2,1)} %get-tuple-element.49), channel_id=1, source_target_pairs={{0,2},{2,0},{4,6},{6,4},{8,10},{10,8},{12,14},{14,12},{1,3},{3,1},... | collective-permute-start | bytes 98312 | tf_op jit(solution)/shard_map/ppermute | solution.py:113
  92.0 2.1 %collective-permute-start.20 = (f32[16,1024]{1,0:T(8,128)S(1)}, f32[16,1024]{1,0:T(8,128)S(1)}, u32[]{:S(2)}, u32[]{:S(2)}) collective-permute-start(f32[16,1024]{1,0:T(8,128)S(1)} %add.37), channel_id=1, source_target_pairs={{0,4},{4,0},{8,12},{12,8},{1,5},{5,1},{9,13},{13,9},{2,6},{6,2},{1... | collective-permute-start | bytes 196616 | tf_op jit(solution)/shard_map/ppermute | solution.py:364
  94.1 20.3 %own_scatter.1.total = f32[512,256]{1,0:T(8,128)} custom-call(bf16[864,32]{1,0:T(8,128)(2,1)} %bitcast.15, bf16[32,2048]{1,0:T(8,128)(2,1)} %get-tuple-element.46.grad, f32[32,2048]{1,0:T(8,128)} %get-tuple-element.36.high.refs_6_, f32[32,2048]{1,0:T(8,128)} %get-tuple-element.37.low.refs_7_), custom_call_target="tpu_custom_call" | custom-call | flops 14495514624 | bytes 1048576 | tf_op jit(solution)/shard_map/own_scatter/pallas_call | solution.py:21
  114.5 1.3 collective-permute-start.6
  115.8 4.5 %collective-permute-start.7 = (f32[32,256]{1,0:T(8,128)S(1)}, f32[32,256]{1,0:T(8,128)S(1)}, u32[]{:S(2)}, u32[]{:S(2)}) collective-permute-start(f32[32,256]{1,0:T(8,128)S(1)} %copy-done.12), channel_id=1, source_target_pairs={{0,4},{2,6},{4,8},{6,10},{8,12},{10,14},{1,5},{3,7},{5,9},{7,11},{... | collective-permute-start | bytes 98312 | tf_op jit(solution)/shard_map/ppermute | solution.py:113
  122.3 5.4 %collective-permute-start.10 = (f32[32,256]{1,0:T(8,128)S(1)}, f32[32,256]{1,0:T(8,128)S(1)}, u32[]{:S(2)}, u32[]{:S(2)}) collective-permute-start(f32[32,256]{1,0:T(8,128)S(1)} %copy-done.9), channel_id=1, source_target_pairs={{0,6},{2,4},{4,10},{6,8},{8,14},{10,12},{1,7},{3,5},{5,11},{7,9},{... | collective-permute-start | bytes 98312 | tf_op jit(solution)/shard_map/ppermute | solution.py:113
  127.8 2.7 %final.1 = (f32[16,4096]{1,0:T(8,128)}, f32[16,4096]{1,0:T(8,128)}) custom-call(s32[2]{0:T(128)} %pad_add_fusion.place, f32[512,256]{1,0:T(8,128)} %own_scatter.1.total, s32[4,512]{1,0:T(4,128)} %face.3, s32[4,128]{1,0:T(4,128)} %corner.3, bf16[32,512]{1,0:T(8,128)(2,1)} %copy-done.14, bf16[32,512]{1,0:T(8,128)(2,1)} %copy-done.15, ...), custom_call_target="tpu_custom_call" | custom-call | flops 1073741824 | bytes 1048576 | tf_op jit(solution)/shard_map/final/pallas_call | solution.py:21
  133.6 1.6 %coarse.1 = bf16[64,256]{1,0:T(8,128)(2,1)} custom-call(s32[2]{0:T(128)} %pad_add_fusion.place, f32[32,256]{1,0:T(8,128)} %copy-done, f32[32,256]{1,0:T(8,128)} %copy-done.2, bf16[32,128]{1,0:T(8,128)(2,1)} %weight.1), custom_call_target="tpu_custom_call" | custom-call | flops 16777216 | bytes 1048576 | tf_op jit(solution)/shard_map/coarse/pallas_call | solution.py:21
  135.2 1.6 %collective-permute-done.21 = f32[16,1024]{1,0:T(8,128)S(1)} collective-permute-done((f32[16,1024]{1,0:T(8,128)S(1)}, f32[16,1024]{1,0:T(8,128)S(1)}, u32[]{:S(2)}, u32[]{:S(2)}) %collective-permute-start.21) | collective-permute-done | bytes 65568 | tf_op jit(solution)/shard_map/ppermute | solution.py:364
  138.6 1.6 %add_convert_fusion = bf16[16,4096]{1,0:T(8,128)(2,1)} fusion(f32[16,4096]{1,0:T(8,128)} %get-tuple-element.52, f32[16,4096]{1,0:T(8,128)S(1)} %collective-permute-done.17), kind=kLoop, calls=%fused_computation | loop fusion | flops 131072 | bytes 655360 | tf_op jit(solution)/shard_map/convert_element_type | solution.py:517
  (80 shorter events, 12.0 us)
Async XLA Ops:
  0.6 3.3 %collective-permute-start = (bf16[16,4096]{1,0:T(8,128)(2,1)}, bf16[16,4096]{1,0:T(8,128)(2,1)S(1)}, u32[]{:S(2)}, u32[]{:S(2)}) collective-permute-start(bf16[16,4096]{1,0:T(8,128)(2,1)} %own.1), channel_id=1, source_target_pairs={{0,1},{1,0},{2,3},{3,2},{4,5},{5,4},{6,7},{7,6},{8,9},{9,8},{10,11... | collective-permute-start | bytes 393224 | tf_op jit(solution)/shard_map/ppermute | solution.py:396
  7.0 36.2 %collective-permute-start.4 = (bf16[32,1152]{1,0:T(8,128)(2,1)}, bf16[32,1152]{1,0:T(8,128)(2,1)S(1)}, u32[]{:S(2)}, u32[]{:S(2)}) collective-permute-start(bf16[32,1152]{1,0:T(8,128)(2,1)} %get-tuple-element.33), channel_id=1, source_target_pairs={{2,4},{0,6},{6,8},{4,10},{10,12},{8,14},{3,5},{1,7},{7,9},{5,11},{... | collective-permute-start | bytes 221192 | tf_op jit(solution)/shard_map/ppermute | solution.py:109
  12.4 30.7 %collective-permute-start.5 = (bf16[32,1152]{1,0:T(8,128)(2,1)}, bf16[32,1152]{1,0:T(8,128)(2,1)S(1)}, u32[]{:S(2)}, u32[]{:S(2)}) collective-permute-start(bf16[32,1152]{1,0:T(8,128)(2,1)} %get-tuple-element.34), channel_id=1, source_target_pairs={{6,0},{4,2},{10,4},{8,6},{14,8},{12,10},{7,1},{5,3},{11,5},{9,7},{... | collective-permute-start | bytes 221192 | tf_op jit(solution)/shard_map/ppermute | solution.py:109
  13.7 29.5 %collective-permute-start.1 = (bf16[32,1536]{1,0:T(8,128)(2,1)}, bf16[32,1536]{1,0:T(8,128)(2,1)S(1)}, u32[]{:S(2)}, u32[]{:S(2)}) collective-permute-start(bf16[32,1536]{1,0:T(8,128)(2,1)} %get-tuple-element.30), channel_id=1, source_target_pairs={{0,4},{2,6},{4,8},{6,10},{8,12},{10,14},{1,5},{3,7},{5,9},{7,11},{... | collective-permute-start | bytes 294920 | tf_op jit(solution)/shard_map/ppermute | solution.py:109
  18.2 24.9 %collective-permute-start.2 = (bf16[32,1536]{1,0:T(8,128)(2,1)}, bf16[32,1536]{1,0:T(8,128)(2,1)S(1)}, u32[]{:S(2)}, u32[]{:S(2)}) collective-permute-start(bf16[32,1536]{1,0:T(8,128)(2,1)} %get-tuple-element.31), channel_id=1, source_target_pairs={{4,0},{6,2},{8,4},{10,6},{12,8},{14,10},{5,1},{7,3},{9,5},{11,7},{... | collective-permute-start | bytes 294920 | tf_op jit(solution)/shard_map/ppermute | solution.py:109
  19.5 23.7 %collective-permute-start.3 = (bf16[32,1536]{1,0:T(8,128)(2,1)}, bf16[32,1536]{1,0:T(8,128)(2,1)S(1)}, u32[]{:S(2)}, u32[]{:S(2)}) collective-permute-start(bf16[32,1536]{1,0:T(8,128)(2,1)} %get-tuple-element.32), channel_id=1, source_target_pairs={{2,0},{0,2},{6,4},{4,6},{10,8},{8,10},{14,12},{12,14},{3,1},{1,3},... | collective-permute-start | bytes 294920 | tf_op jit(solution)/shard_map/ppermute | solution.py:109
  60.6 1.5 %collective-permute-start.18 = (f32[16,1024]{1,0:T(8,128)}, f32[16,1024]{1,0:T(8,128)S(1)}, u32[]{:S(2)}, u32[]{:S(2)}) collective-permute-start(f32[16,1024]{1,0:T(8,128)} %get-tuple-element.55), channel_id=1, source_target_pairs={{0,1},{1,0},{2,3},{3,2},{4,5},{5,4},{6,7},{7,6},{8,9},{9,8},{10,11... | collective-permute-start | bytes 196616 | tf_op jit(solution)/shard_map/ppermute | solution.py:464
  63.0 27.4 %collective-permute-start.19 = (f32[16,1024]{1,0:T(8,128)S(1)}, f32[16,1024]{1,0:T(8,128)S(1)}, u32[]{:S(2)}, u32[]{:S(2)}) collective-permute-start(f32[16,1024]{1,0:T(8,128)S(1)} %add.36), channel_id=1, source_target_pairs={{0,2},{2,0},{1,3},{3,1},{4,6},{6,4},{5,7},{7,5},{8,10},{10,8},{9,1... | collective-permute-start | bytes 196616 | tf_op jit(solution)/shard_map/ppermute | solution.py:364
  77.2 14.9 %collective-permute-start.15 = (bf16[32,128]{1,0:T(8,128)(2,1)}, bf16[32,128]{1,0:T(8,128)(2,1)S(1)}, u32[]{:S(2)}, u32[]{:S(2)}) collective-permute-start(bf16[32,128]{1,0:T(8,128)(2,1)} %get-tuple-element.50), channel_id=1, source_target_pairs={{4,2},{6,0},{8,6},{10,4},{12,10},{14,8},{5,3},{7,1},{9,7},{11,5},{... | collective-permute-start | bytes 24584 | tf_op jit(solution)/shard_map/ppermute | solution.py:113
  78.4 36.0 %collective-permute-start.16 = (bf16[32,128]{1,0:T(8,128)(2,1)}, bf16[32,128]{1,0:T(8,128)(2,1)S(1)}, u32[]{:S(2)}, u32[]{:S(2)}) collective-permute-start(bf16[32,128]{1,0:T(8,128)(2,1)} %get-tuple-element.51), channel_id=1, source_target_pairs={{0,6},{2,4},{4,10},{6,8},{8,14},{10,12},{1,7},{3,5},{5,11},{7,9},{... | collective-permute-start | bytes 24584 | tf_op jit(solution)/shard_map/ppermute | solution.py:113
  84.6 31.2 %collective-permute-start.12 = (bf16[32,512]{1,0:T(8,128)(2,1)}, bf16[32,512]{1,0:T(8,128)(2,1)S(1)}, u32[]{:S(2)}, u32[]{:S(2)}) collective-permute-start(bf16[32,512]{1,0:T(8,128)(2,1)} %get-tuple-element.47), channel_id=1, source_target_pairs={{4,0},{6,2},{8,4},{10,6},{12,8},{14,10},{5,1},{7,3},{9,5},{11,7},{... | collective-permute-start | bytes 98312 | tf_op jit(solution)/shard_map/ppermute | solution.py:113
  85.9 34.5 %collective-permute-start.13 = (bf16[32,512]{1,0:T(8,128)(2,1)}, bf16[32,512]{1,0:T(8,128)(2,1)S(1)}, u32[]{:S(2)}, u32[]{:S(2)}) collective-permute-start(bf16[32,512]{1,0:T(8,128)(2,1)} %get-tuple-element.48), channel_id=1, source_target_pairs={{0,4},{2,6},{4,8},{6,10},{8,12},{10,14},{1,5},{3,7},{5,9},{7,11},{... | collective-permute-start | bytes 98312 | tf_op jit(solution)/shard_map/ppermute | solution.py:113
  90.4 30.6 %collective-permute-start.14 = (bf16[32,512]{1,0:T(8,128)(2,1)}, bf16[32,512]{1,0:T(8,128)(2,1)S(1)}, u32[]{:S(2)}, u32[]{:S(2)}) collective-permute-start(bf16[32,512]{1,0:T(8,128)(2,1)} %get-tuple-element.49), channel_id=1, source_target_pairs={{0,2},{2,0},{4,6},{6,4},{8,10},{10,8},{12,14},{14,12},{1,3},{3,1},... | collective-permute-start | bytes 98312 | tf_op jit(solution)/shard_map/ppermute | solution.py:113
  92.0 29.0 %copy-start.10 = (f32[32,256]{1,0:T(8,128)S(1)}, f32[32,256]{1,0:T(8,128)}, u32[]{:S(2)}) copy-start(f32[32,256]{1,0:T(8,128)} %get-tuple-element.44) | copy-start | bytes 98308
  92.0 30.3 %copy-start.9 = (f32[32,256]{1,0:T(8,128)S(1)}, f32[32,256]{1,0:T(8,128)}, u32[]{:S(2)}) copy-start(f32[32,256]{1,0:T(8,128)} %get-tuple-element.45) | copy-start | bytes 98308
  92.0 30.2 %collective-permute-start.20 = (f32[16,1024]{1,0:T(8,128)S(1)}, f32[16,1024]{1,0:T(8,128)S(1)}, u32[]{:S(2)}, u32[]{:S(2)}) collective-permute-start(f32[16,1024]{1,0:T(8,128)S(1)} %add.37), channel_id=1, source_target_pairs={{0,4},{4,0},{8,12},{12,8},{1,5},{5,1},{9,13},{13,9},{2,6},{6,2},{1... | collective-permute-start | bytes 196616 | tf_op jit(solution)/shard_map/ppermute | solution.py:364
  114.5 16.0 %collective-permute-start.6 = (f32[32,256]{1,0:T(8,128)S(1)}, f32[32,256]{1,0:T(8,128)S(1)}, u32[]{:S(2)}, u32[]{:S(2)}) collective-permute-start(f32[32,256]{1,0:T(8,128)S(1)} %copy-done.13), channel_id=1, source_target_pairs={{4,0},{6,2},{8,4},{10,6},{12,8},{14,10},{5,1},{7,3},{9,5},{11,7},{... | collective-permute-start | bytes 98312 | tf_op jit(solution)/shard_map/ppermute | solution.py:113
  115.8 14.8 %collective-permute-start.7 = (f32[32,256]{1,0:T(8,128)S(1)}, f32[32,256]{1,0:T(8,128)S(1)}, u32[]{:S(2)}, u32[]{:S(2)}) collective-permute-start(f32[32,256]{1,0:T(8,128)S(1)} %copy-done.12), channel_id=1, source_target_pairs={{0,4},{2,6},{4,8},{6,10},{8,12},{10,14},{1,5},{3,7},{5,9},{7,11},{... | collective-permute-start | bytes 98312 | tf_op jit(solution)/shard_map/ppermute | solution.py:113
  120.4 11.3 %collective-permute-start.8 = (f32[32,256]{1,0:T(8,128)S(1)}, f32[32,256]{1,0:T(8,128)S(1)}, u32[]{:S(2)}, u32[]{:S(2)}) collective-permute-start(f32[32,256]{1,0:T(8,128)S(1)} %copy-done.11), channel_id=1, source_target_pairs={{0,2},{2,0},{4,6},{6,4},{8,10},{10,8},{12,14},{14,12},{1,3},{3,1},... | collective-permute-start | bytes 98312 | tf_op jit(solution)/shard_map/ppermute | solution.py:113
  121.0 10.7 %collective-permute-start.9 = (f32[32,256]{1,0:T(8,128)S(1)}, f32[32,256]{1,0:T(8,128)S(1)}, u32[]{:S(2)}, u32[]{:S(2)}) collective-permute-start(f32[32,256]{1,0:T(8,128)S(1)} %copy-done.10), channel_id=1, source_target_pairs={{4,2},{6,0},{8,6},{10,4},{12,10},{14,8},{5,3},{7,1},{9,7},{11,5},{... | collective-permute-start | bytes 98312 | tf_op jit(solution)/shard_map/ppermute | solution.py:113
  122.3 9.3 %collective-permute-start.10 = (f32[32,256]{1,0:T(8,128)S(1)}, f32[32,256]{1,0:T(8,128)S(1)}, u32[]{:S(2)}, u32[]{:S(2)}) collective-permute-start(f32[32,256]{1,0:T(8,128)S(1)} %copy-done.9), channel_id=1, source_target_pairs={{0,6},{2,4},{4,10},{6,8},{8,14},{10,12},{1,7},{3,5},{5,11},{7,9},{... | collective-permute-start | bytes 98312 | tf_op jit(solution)/shard_map/ppermute | solution.py:113
  130.5 8.1 %collective-permute-start.17 = (f32[16,4096]{1,0:T(8,128)}, f32[16,4096]{1,0:T(8,128)S(1)}, u32[]{:S(2)}, u32[]{:S(2)}) collective-permute-start(f32[16,4096]{1,0:T(8,128)} %get-tuple-element.53), channel_id=1, source_target_pairs={{0,1},{1,0},{2,3},{3,2},{4,5},{5,4},{6,7},{7,6},{8,9},{9,8},{10,11... | collective-permute-start | bytes 786440 | tf_op jit(solution)/shard_map/ppermute | solution.py:517
  130.6 6.3 %collective-permute-start.21 = (f32[16,1024]{1,0:T(8,128)S(1)}, f32[16,1024]{1,0:T(8,128)S(1)}, u32[]{:S(2)}, u32[]{:S(2)}) collective-permute-start(f32[16,1024]{1,0:T(8,128)S(1)} %add.38), channel_id=1, source_target_pairs={{0,8},{4,12},{8,0},{12,4},{1,9},{5,13},{9,1},{13,5},{2,10},{6,14},... | collective-permute-start | bytes 196616 | tf_op jit(solution)/shard_map/ppermute | solution.py:364
  131.7 1.3 collective-permute-start.11
  (17 other events, 159.7 us)

commit v2 on v1

v2 whole, which is shorter than its diff:
```python
import functools

import jax
import jax.numpy as jnp
from jax import lax
from jax.experimental import pallas as pl
from jax.experimental.pallas import tpu as pltpu
from jax.sharding import PartitionSpec as P

BF = jnp.bfloat16
F32 = jnp.float32
STEPS = ((-1, 0), (1, 0), (0, -1), (0, 1), (-1, -1), (-1, 1), (1, -1), (1, 1))
LOW = 256
VMEM_LIMIT = 56 << 20


def call(kernel, name, outs, scratch, flops, *args):
    return pl.pallas_call(
        kernel,
        name=name,
        out_shape=[jax.ShapeDtypeStruct(s, d) for s, d in outs],
        in_specs=[pl.BlockSpec(memory_space=pltpu.VMEM)] * len(args),
        out_specs=[pl.BlockSpec(memory_space=pltpu.VMEM)] * len(outs),
        scratch_shapes=[pltpu.VMEM(s, d) for s, d in scratch],
        compiler_params=pltpu.CompilerParams(vmem_limit_bytes=VMEM_LIMIT),
        cost_estimate=pl.CostEstimate(flops=flops, bytes_accessed=1 << 20, transcendentals=0),
    )(*args)


class Plan:
    def __init__(self, shapes, nx, ny, nch):
        features, neighbours, face_send, corner_send, coarse_weight, coarse_grad = shapes
        self.nx, self.ny, self.nch = nx, ny, nch
        self.share, self.voxels = features
        self.channels = self.share * nch
        self.offsets = neighbours[0]
        self.half = self.voxels // nch
        self.face, self.corner = face_send[1], corner_send[1]
        self.coarse_channels, self.coarse = coarse_grad
        self.coarse_share = self.coarse_channels // nch
        self.own_blocks = self.voxels // LOW
        self.paired = ny == 2
        self.widths = [self.face] * (3 if self.paired else 4)
        self.widths += [self.corner] * (2 if self.paired else 4)
        self.slots = len(self.widths)
        self.halo = sum(self.widths)
        self.halo_blocks = self.halo // LOW
        self.starts = [sum(self.widths[:s]) for s in range(self.slots)]
        self.nothing = self.voxels + self.halo
        self.itself = self.offsets // 2
        self.tiles = nx * ny
        self.groups = ((0, 1), (3, 4), (2, 2)) if self.paired else ((0, 1), (2, 3), (4, 5), (6, 7))
        self.swaps = sum(a != b for a, b in self.groups)
        self.early = min(2, self.half // LOW)
        self.padded = -(-self.offsets * self.channels // 128) * 128
        self.sum_width = self.padded + self.coarse_channels * self.channels // nch // self.share

    def directions(self, slot):
        if self.paired:
            return ((0,), (1,), (2, 3), (4, 5), (6, 7))[slot]
        return (slot,)

    def pairs(self, first, second):
        found = []
        for core, slot in enumerate((first, second)):
            for x in range(self.nx):
                for y in range(self.ny):
                    for d in self.directions(slot):
                        sx, sy = x + STEPS[d][0], y + STEPS[d][1]
                        if 0 <= sx < self.nx and 0 <= sy < self.ny:
                            here, there = x * self.ny + y, sx * self.ny + sy
                            found.append((there * self.nch + core, here * self.nch + core))
        return found

    def opposite(self, slot):
        return ((1, 0, 2, 4, 3) if self.paired else (1, 0, 3, 2, 7, 6, 5, 4))[slot]

    def bordering(self, slot, x, y):
        step = STEPS[self.directions(slot)[0]]
        to_x = x + step[0]
        there = (to_x >= 0) & (to_x < self.nx)
        if self.paired:
            to_y = 1 - y if step[1] else y
        else:
            to_y = y + step[1]
            there = there & (to_y >= 0) & (to_y < self.ny)
        return jnp.where(there, to_x * self.ny + to_y, -1)

    def send_rows(self, slot, y, face, corner):
        if not self.paired:
            if slot < 4:
                index = (1, 0, 3, 2)[slot]
                return face[index : index + 1, :]
            index = (3, 2, 1, 0)[slot - 4]
            return corner[index : index + 1, :]
        if slot == 0:
            return face[1:2, :]
        if slot == 1:
            return face[0:1, :]
        if slot == 2:
            return jnp.where(y == 0, face[3:4, :], face[2:3, :])
        if slot == 3:
            return jnp.where(y == 0, corner[3:4, :], corner[2:3, :])
        return jnp.where(y == 0, corner[1:2, :], corner[0:1, :])

    def rows(self, index, y):
        if not self.paired:
            return jnp.minimum(index, self.nothing)
        v, f, c = self.voxels, self.face, self.corner
        along_y = v + 2 * f
        corners = v + 4 * f
        end = corners + 4 * c
        mine = jnp.where(y == 0, along_y + f, along_y)
        of_y = jnp.where((index >= mine) & (index < mine + f), index - mine + along_y, self.nothing)
        result = jnp.where(index < along_y, index, of_y)
        first = jnp.where(y == 0, c, 0)
        at = index - corners - first
        one = jnp.where((at >= 0) & (at < c), at + v + 3 * f, self.nothing)
        two = jnp.where((at >= 2 * c) & (at < 3 * c), at - c + v + 3 * f, one)
        return jnp.where((index >= corners) & (index < end), two, result)

    def owner_slots(self, side):
        if not self.paired:
            return side
        return jnp.where(side < 3, side, jnp.where(side < 5, 3, jnp.where(side < 7, 4, 5)))


def lows(low, height, width):
    iota = lax.broadcasted_iota(jnp.int32, (height, width), 0).astype(BF)
    return jnp.where(iota == low, BF(1), BF(0))


def where_am_i(plan):
    core, x, y = (lax.axis_index(a) for a in ("ch", "tx", "ty"))
    return core, x, y


def prepare_kernel(plan, neighbours, side, slot, high_out, low_out, side_out, slot_out):
    core, _, y = where_am_i(plan)
    mine = pl.ds(pl.multiple_of(core * plan.half, plan.half), plan.half)
    rows = plan.rows(neighbours[:, mine], y)
    pad = high_out.shape[0] - plan.offsets
    fill = jnp.zeros((pad, plan.half), jnp.int32)
    rows = jnp.concatenate([rows, fill], axis=0) if pad else rows
    high_out[...] = lax.shift_right_logical(rows, 8).astype(F32)
    low_out[...] = (rows & (LOW - 1)).astype(F32)
    side_out[...] = plan.owner_slots(side[:, mine]).astype(F32)
    slot_out[...] = slot[:, mine].astype(F32)


def pack_kernel(plan, own, other, face, corner, coarse_grad, table, *messages):
    core, _, y = where_am_i(plan)
    s, n = plan.share, plan.channels
    at_own = pl.multiple_of(core * s, s)
    at_other = pl.multiple_of((1 - core) * s, s)
    for b in range(plan.own_blocks):
        table[pl.ds(b * n + at_own, s), :] = own[:, b * LOW : (b + 1) * LOW]
        table[pl.ds(b * n + at_other, s), :] = other[:, b * LOW : (b + 1) * LOW]
    groups = plan.coarse_channels // n
    for g, (first, second) in enumerate(plan.groups):
        width = plan.widths[first]
        rows = plan.send_rows(first, y, face, corner)
        if second != first:
            rows = jnp.where(core == 0, rows, plan.send_rows(second, y, face, corner))
        high = lax.shift_right_logical(rows, 8)
        hot = lows((rows & (LOW - 1)).astype(F32).astype(BF), LOW, width)
        part = jnp.dot(table[...], hot, preferred_element_type=F32)
        picked = jnp.zeros((n, width), F32)
        for b in range(plan.own_blocks):
            picked = jnp.where(high == b, part[b * n : (b + 1) * n], picked)
        messages[g][:, :width] = picked.astype(BF)
        for q in range(groups):
            at = width + q * plan.coarse
            messages[g][:, at : at + plan.coarse] = coarse_grad[q * n : (q + 1) * n, :]


def gather_block(plan, table, high_ref, low_ref, out, fs, base, blocks, before=None):
    n = plan.channels
    for k in range(plan.offsets):
        if k == plan.itself:
            continue
        at = slice(k * n, (k + 1) * n)
        low = low_ref[k : k + 1, fs].astype(BF)
        high = high_ref[k : k + 1, fs]
        part = jnp.dot(table[...], lows(low, LOW, LOW), preferred_element_type=F32)
        if before is None:
            picked = jnp.zeros((n, LOW), F32)
        else:
            picked = before[at, fs].astype(F32)
        for b in range(blocks):
            picked = jnp.where(high == float(base + b), part[b * n : (b + 1) * n], picked)
        out[at, fs] = picked.astype(BF)


def columns(block):
    return pl.ds(pl.multiple_of(block * LOW, LOW), LOW)


def own_gather_kernel(plan, table, high, low, out):
    def body(j, carry):
        gather_block(plan, table, high, low, out, columns(j), 0, plan.own_blocks)
        return carry

    lax.fori_loop(0, plan.early, body, 0)


def middle_kernel(plan, *refs):
    n, s, m = plan.channels, plan.share, plan.coarse
    count = len(plan.groups)
    received, refs = refs[:count], refs[count:]
    swapped, refs = refs[: plan.swaps], refs[plan.swaps :]
    own_table, before, high, low, side, slot, weight, coarse_weight, coarse_grad, refs = (
        *refs[:9],
        refs[9:],
    )
    grad_out, mine_out, theirs_out, table, rows, coarse_all, pooled_all, sums, parts, coarse_sum = refs
    core, _, _ = where_am_i(plan)
    messages = {}
    other = iter(swapped)
    for g, (first, second) in enumerate(plan.groups):
        here = received[g][...]
        if first == second:
            messages[first] = here
        else:
            there = next(other)[...]
            messages[first] = jnp.where(core == 0, here, there)
            messages[second] = jnp.where(core == 0, there, here)
    own = plan.own_blocks * n
    table[:own, :] = own_table[...]
    for k in range(plan.slots):
        for part in range(0, plan.widths[k], min(LOW, plan.widths[k])):
            width = min(LOW, plan.widths[k])
            at = plan.starts[k] + part
            b, column = at // LOW, at % LOW
            table[own + b * n : own + (b + 1) * n, column : column + width] = messages[k][
                :, part : part + width
            ]
    groups = plan.coarse_channels // n
    coarse_all[:, :m] = coarse_grad[...]
    for k in range(plan.slots):
        for g in range(groups):
            at = plan.widths[k] + g * m
            coarse_all[g * n : (g + 1) * n, (k + 1) * m : (k + 2) * m] = messages[k][:, at : at + m]

    def rest(j, carry):
        fs = columns(j)
        gather_block(plan, table.at[own:, :], high, low, rows, fs, plan.own_blocks, plan.halo_blocks, before)
        return carry

    def whole(j, carry):
        fs = columns(j)
        gather_block(plan, table, high, low, rows, fs, 0, plan.own_blocks + plan.halo_blocks)
        return carry

    if plan.early:
        lax.fori_loop(0, plan.early, rest, 0)
    lax.fori_loop(plan.early, plan.half // LOW, whole, 0)
    for j in range(plan.half // LOW):
        at = pl.multiple_of((core * (plan.half // LOW) + j) * n, n)
        rows[plan.itself * n : (plan.itself + 1) * n, j * LOW : (j + 1) * LOW] = table[pl.ds(at, n), :]

    grads = jnp.dot(coarse_weight[...], coarse_all[...], preferred_element_type=F32).astype(BF)
    owners = plan.slots + 1
    for k in range(owners):
        pooled_all[k * n : (k + 1) * n, :] = grads[:, k * m : (k + 1) * m]
    chunk = min(plan.half, 512)
    wide = plan.offsets * n
    sums[...] = jnp.zeros_like(sums)
    parts[...] = jnp.zeros_like(parts)
    for c in range(plan.half // chunk):
        fs = slice(c * chunk, (c + 1) * chunk)
        picked = rows[:, fs]
        hidden = lax.dot_general(
            weight[...], picked, (((0,), (0,)), ((), ())), preferred_element_type=F32
        )
        sigma = 1.0 / (1.0 + jnp.exp(-hidden))
        active = (hidden * sigma).astype(BF)
        owner = side[:, fs]
        owner_low = owner.astype(BF)
        hot = lows(slot[:, fs].astype(BF), m, chunk)
        spread = jnp.concatenate(
            [jnp.where(owner_low == BF(k), active, BF(0)) for k in range(owners)], axis=0
        )
        parts[...] += lax.dot_general(
            spread, hot, (((1,), (1,)), ((), ())), preferred_element_type=F32
        )
        found = jnp.dot(pooled_all[...], hot, preferred_element_type=F32)
        above = jnp.zeros((n, chunk), F32)
        for k in range(owners):
            above = jnp.where(owner == float(k), found[k * n : (k + 1) * n], above)
        grad = (above * (sigma * (1.0 + hidden * (1.0 - sigma)))).astype(BF)
        grad_out[:, fs] = grad
        sums[:, :wide] += lax.dot_general(
            grad, picked, (((1,), (1,)), ((), ())), preferred_element_type=F32
        )
    total = jnp.zeros((n, plan.coarse_channels), F32)
    for k in range(owners):
        value = parts[k * n : (k + 1) * n, :]
        first = value.astype(BF)
        second = (value - first.astype(F32)).astype(BF)
        grads_k = coarse_all[:, k * m : (k + 1) * m]
        for piece in (first, second):
            total = total + lax.dot_general(
                piece, grads_k, (((1,), (1,)), ((), ())), preferred_element_type=F32
            )
    for h in range(plan.nch):
        half = total[:, h * plan.coarse_share : (h + 1) * plan.coarse_share]
        for q in range(n // s):
            at = q * plan.coarse_share
            coarse_sum[h * s : (h + 1) * s, at : at + plan.coarse_share] = half[q * s : (q + 1) * s]
    at_own = pl.multiple_of(core * s, s)
    at_other = pl.multiple_of((1 - core) * s, s)
    padded = sums.shape[1]
    after = padded + coarse_sum.shape[1]
    for out, at in ((mine_out, at_own), (theirs_out, at_other)):
        out[:, :padded] = sums[pl.ds(at, s), :]
        out[:, padded:after] = coarse_sum[pl.ds(at, s), :]
        for k in range(owners):
            out[:, after + k * m : after + (k + 1) * m] = parts[pl.ds(k * n + at, s), :]


def scatter_loop(plan, values, high_ref, low_ref, total, base, blocks):
    n = plan.channels
    total[...] = jnp.zeros_like(total)

    def body(j, carry):
        fs = columns(j)
        masked, hots = [], []
        for k in range(plan.offsets):
            if k == plan.itself:
                continue
            high = high_ref[k : k + 1, fs].astype(BF)
            hots.append(lows(low_ref[k : k + 1, fs].astype(BF), LOW, LOW))
            value = values[k * n : (k + 1) * n, fs]
            masked.append(
                jnp.concatenate(
                    [jnp.where(high == BF(base + b), value, BF(0)) for b in range(blocks)], axis=0
                )
            )
        total[...] += lax.dot_general(
            jnp.concatenate(masked, axis=1),
            jnp.concatenate(hots, axis=1),
            (((1,), (1,)), ((), ())),
            preferred_element_type=F32,
        )
        return carry

    lax.fori_loop(0, plan.half // LOW, body, 0)


def spread_values(plan, weight, grad, values):
    chunk = min(plan.half, 512)
    for c in range(plan.half // chunk):
        fs = slice(c * chunk, (c + 1) * chunk)
        values[:, fs] = jnp.dot(weight[...], grad[:, fs], preferred_element_type=F32).astype(BF)


def halo_scatter_kernel(plan, weight, grad, high, low, total, values):
    spread_values(plan, weight, grad, values)
    scatter_loop(plan, values, high, low, total, plan.own_blocks, plan.halo_blocks)


def join_kernel(plan, mine, theirs, halo, joined_out, send):
    _, x, y = where_am_i(plan)
    n, s, m = plan.channels, plan.share, plan.coarse
    joined_out[...] = mine[...] + theirs[...]
    width = plan.sum_width // (n // s)
    for t in range(plan.tiles):
        for q in range(n // s):
            send[t, q * s : (q + 1) * s, :width] = joined_out[:, q * width : (q + 1) * width].astype(BF)
    part = m // (n // s)
    for k in range(plan.slots):
        tile = plan.bordering(k, x, y)

        @pl.when(tile >= 0)
        def _():
            at = plan.sum_width + (k + 1) * m
            for q in range(n // s):
                send[tile, q * s : (q + 1) * s, width : width + part] = joined_out[
                    :, at + q * part : at + (q + 1) * part
                ].astype(BF)
            size = min(LOW, plan.widths[k])
            for start in range(0, plan.widths[k], size):
                b, column = (plan.starts[k] + start) // LOW, (plan.starts[k] + start) % LOW
                to = width + part + start
                send[tile, :, to : to + size] = halo[b * n : (b + 1) * n, column : column + size].astype(BF)


def own_scatter_kernel(plan, weight, grad, high, low, total, values):
    core, _, _ = where_am_i(plan)
    n = plan.channels
    spread_values(plan, weight, grad, values)
    scatter_loop(plan, values, high, low, total, 0, plan.own_blocks)
    for j in range(plan.half // LOW):
        at = pl.ds(pl.multiple_of((core * (plan.half // LOW) + j) * n, n), n)
        total[at, :] += values[plan.itself * n : (plan.itself + 1) * n, j * LOW : (j + 1) * LOW].astype(F32)


def final_kernel(plan, total, joined, arrived, face, corner, coarse_weight, *refs):
    mine_out, theirs_out, coarse_mine, coarse_theirs, conv_out, coarse_grad_out, work, product = refs
    core, x, y = where_am_i(plan)
    n, s, m = plan.channels, plan.share, plan.coarse
    width = plan.sum_width // (n // s)
    part = m // (n // s)
    masked, hots = [], []
    pooled = joined[:, plan.sum_width : plan.sum_width + m]
    for k in range(plan.slots):
        tile = plan.bordering(k, x, y)
        there = tile >= 0
        tile = jnp.maximum(tile, 0)
        rows = plan.send_rows(plan.opposite(k), y, face, corner)
        high = lax.shift_right_logical(rows, 8).astype(F32).astype(BF)
        high = jnp.where(there, high, BF(-1))
        hots.append(lows((rows & (LOW - 1)).astype(F32).astype(BF), LOW, plan.widths[k]))
        value = arrived[tile, :, width + part : width + part + plan.widths[k]]
        masked.append(
            jnp.concatenate(
                [jnp.where(high == BF(b), value, BF(0)) for b in range(plan.own_blocks)], axis=0
            )
        )
        more = jnp.concatenate(
            [arrived[tile, q * s : (q + 1) * s, width : width + part] for q in range(n // s)], axis=1
        )
        pooled = pooled + jnp.where(there, more.astype(F32), 0.0)
    work[...] = total[...] + lax.dot_general(
        jnp.concatenate(masked, axis=1),
        jnp.concatenate(hots, axis=1),
        (((1,), (1,)), ((), ())),
        preferred_element_type=F32,
    )
    at_own = pl.multiple_of(core * s, s)
    at_other = pl.multiple_of((1 - core) * s, s)
    for b in range(plan.own_blocks):
        mine_out[:, b * LOW : (b + 1) * LOW] = work[pl.ds(b * n + at_own, s), :]
        theirs_out[:, b * LOW : (b + 1) * LOW] = work[pl.ds(b * n + at_other, s), :]
    share = plan.coarse_share
    product[...] = lax.dot_general(
        coarse_weight[pl.ds(at_own, s), :], pooled.astype(BF), (((0,), (0,)), ((), ())), preferred_element_type=F32
    )
    coarse_mine[...] = product[pl.ds(pl.multiple_of(core * share, share), share), :]
    coarse_theirs[...] = product[pl.ds(pl.multiple_of((1 - core) * share, share), share), :]
    summed = arrived[0, :, :width].astype(F32)
    for t in range(1, plan.tiles):
        summed = summed + arrived[t, :, :width].astype(F32)
    summed = jnp.concatenate([summed[q * s : (q + 1) * s] for q in range(n // s)], axis=1)
    conv_out[...] = jnp.transpose(summed)[: plan.offsets * n]
    for q in range(n // s):
        at = plan.padded + q * share
        coarse_grad_out[q * s : (q + 1) * s, :] = summed[:, at : at + share]


def add_kernel(plan, mine, theirs, coarse_mine, coarse_theirs, out, coarse_out):
    out[...] = (mine[...] + theirs[...]).astype(BF)
    coarse_out[...] = (coarse_mine[...] + coarse_theirs[...]).astype(BF)


def shards(
    fine_features,
    neighbours,
    face_send,
    corner_send,
    owner_side,
    owner_slot,
    conv_weight,
    coarse_weight,
    coarse_grad,
):
    nx, ny, nch = (lax.axis_size(a) for a in ("tx", "ty", "ch"))
    plan = Plan(
        [
            a.shape
            for a in (fine_features, neighbours, face_send, corner_send, coarse_weight, coarse_grad)
        ],
        nx,
        ny,
        nch,
    )
    n, s, half, m = plan.channels, plan.share, plan.half, plan.coarse
    wide = plan.offsets * n

    def swap(value):
        return lax.ppermute(value, "ch", [(0, 1), (1, 0)])

    def run(kernel, name, outs, scratch, flops, *args):
        return call(functools.partial(kernel, plan), name, outs, scratch, flops, *args)

    other = swap(fine_features)
    tall = -(-plan.offsets // 8) * 8
    high, low, side, slot = run(
        prepare_kernel,
        "prepare",
        [((tall, half), F32), ((tall, half), F32), ((1, half), F32), ((1, half), F32)],
        [],
        1 << 20,
        neighbours,
        owner_side.reshape(1, -1),
        owner_slot.reshape(1, -1),
    )
    extra = plan.coarse_channels // n * m
    table, *sent = run(
        pack_kernel,
        "pack",
        [((plan.own_blocks * n, LOW), BF)]
        + [((n, plan.widths[first] + extra), BF) for first, _ in plan.groups],
        [],
        1 << 30,
        fine_features,
        other,
        face_send,
        corner_send,
        coarse_grad,
    )
    received = [
        lax.ppermute(value, ("tx", "ty", "ch"), plan.pairs(first, second))
        for value, (first, second) in zip(sent, plan.groups)
    ]
    split = [g for g, (first, second) in enumerate(plan.groups) if first != second]
    early_table, *ready = lax.optimization_barrier((table, *[received[g] for g in split]))
    for g, value in zip(split, ready):
        received[g] = value
    swapped = [swap(received[g]) for g in split]
    work = 2 * wide * half * LOW
    early = plan.early * LOW
    (before,) = run(
        own_gather_kernel,
        "own_gather",
        [((wide, early), BF)],
        [],
        work * plan.own_blocks * early // half,
        early_table,
        high,
        low,
    )
    weight = conv_weight.reshape(wide, n)
    owners = plan.slots + 1
    across = plan.sum_width + owners * m
    grad, mine, theirs = run(
        middle_kernel,
        "middle",
        [((n, half), BF), ((s, across), F32), ((s, across), F32)],
        [
            (((plan.own_blocks + plan.halo_blocks) * n, LOW), BF),
            ((wide, half), BF),
            ((plan.coarse_channels, owners * m), BF),
            ((owners * n, m), BF),
            ((n, plan.padded), F32),
            ((owners * n, m), F32),
            ((n, plan.sum_width - plan.padded), F32),
        ],
        work * (plan.own_blocks + plan.halo_blocks),
        *received,
        *swapped,
        table,
        before,
        high,
        low,
        side,
        slot,
        weight,
        coarse_weight,
        coarse_grad,
    )
    theirs = swap(theirs)
    (halo,) = run(
        halo_scatter_kernel,
        "halo_scatter",
        [((plan.halo_blocks * n, LOW), F32)],
        [((wide, half), BF)],
        work * plan.halo_blocks,
        weight,
        grad,
        high,
        low,
    )
    message = plan.sum_width // (n // s) + m // (n // s) + max(plan.widths)
    joined, send = run(
        join_kernel,
        "join",
        [((s, across), F32), ((plan.tiles, n, message), BF)],
        [],
        1 << 20,
        mine,
        theirs,
        halo,
    )
    arrived = lax.all_to_all(send, ("tx", "ty"), 0, 0, tiled=True)
    (total,) = run(
        own_scatter_kernel,
        "own_scatter",
        [((plan.own_blocks * n, LOW), F32)],
        [((wide, half), BF)],
        work * plan.own_blocks,
        weight,
        grad,
        high,
        low,
    )
    share = plan.coarse_share
    mine, theirs, coarse_mine, coarse_theirs, conv_weight_grad, coarse_weight_grad = run(
        final_kernel,
        "final",
        [((s, plan.voxels), F32)] * 2 + [((share, m), F32)] * 2 + [((wide, s), F32), ((n, share), F32)],
        [((plan.own_blocks * n, LOW), F32), ((plan.coarse_channels, m), F32)],
        1 << 30,
        total,
        joined,
        arrived,
        face_send,
        corner_send,
        coarse_weight,
    )
    input_grad, coarse_out = run(
        add_kernel,
        "add",
        [((s, plan.voxels), BF), ((share, m), BF)],
        [],
        1 << 20,
        mine,
        swap(theirs),
        coarse_mine,
        swap(coarse_theirs),
    )
    return (coarse_out, input_grad, conv_weight_grad.reshape(plan.offsets, n, s), coarse_weight_grad)


def solution(mesh):
    tiles = ("group", "tx", "ty")
    in_specs = (
        P("ch", tiles),
        P(None, tiles),
        P(None, tiles),
        P(None, tiles),
        P(tiles),
        P(tiles),
        P(),
        P(),
        P(None, tiles),
    )
    out_specs = (
        P("ch", tiles),
        P("ch", tiles),
        P("group", None, "ch"),
        P("group", "ch"),
    )
    return jax.shard_map(shards, mesh=mesh, in_specs=in_specs, out_specs=out_specs, check_vma=False)
```

time: 141 us -> 97 us (0.69)
  starting transfers between devices: 46.6 us -> 16.4 us
  Pallas kernels: 81.5 us -> 72.7 us
  other arithmetic: 3.13 us -> 0 us
  waiting for transfers between devices: 4.19 us -> 1.22 us
  local copies, waits for them, and re-layouts: 3.7 us -> 5.41 us
    ppermute x22 -> x9, starting transfers between devices: 46.6 us -> 11.5 us  [the longest x3 9.77 us: shards(): lax.ppermute(value, ('tx', 'ty', 'ch'), plan.pairs(first, second))]
    pallas_call x8 -> x9, Pallas kernels: 81.5 us -> 72.7 us  [call(): pl.pallas_call(kernel, name=name, out_shape=[jax.ShapeDtypeStruct(s, d) f...]
    all_to_all x0 -> x1, starting transfers between devices: none -> 4.98 us  [shards(): arrived = lax.all_to_all(send, ('tx', 'ty'), 0, 0, tiled=True)]
    ppermute x22 -> x9, waiting for transfers between devices: 4.19 us -> 1.22 us  [the longest x6 1.21 us: swap(): return lax.ppermute(value, 'ch', [(0, 1), (1, 0)])]
    unnamed x40 -> x23, local copies, waits for them, and re-layouts: 3.5 us -> 5.41 us
    convert_element_type x1 -> x0, other arithmetic: 1.63 us -> none  [shards(): (final_mine + lax.ppermute(final_theirs, 'ch', swap)).astype(BF)]
  transfers between devices with their start and end apart: 22 -> 10, of which waited for: 3 -> 1; matrix products, arithmetic and copies ran while one was open for 2% -> 2% of each run, Pallas kernels for 44% -> 41%
where the time goes in v2:
time: 97 us; the launch traced here: 96.5 us
  Pallas kernels  72.7 us (75%)
  starting transfers between devices  16.4 us (17%)
  local copies, waits for them, and re-layouts  5.41 us (6%)
  waiting for transfers between devices  1.22 us (1%)
    pallas_call x9, Pallas kernels, call(): pl.pallas_call(kernel, name=name, out_shape=[jax.ShapeDtypeStruct(s, d) f...  72.7 us
    ppermute x3, starting transfers between devices, shards(): lax.ppermute(value, ('tx', 'ty', 'ch'), plan.pairs(first, second))  9.77 us
    unnamed x23, local copies, waits for them, and re-layouts  5.41 us
    all_to_all x1, starting transfers between devices, shards(): arrived = lax.all_to_all(send, ('tx', 'ty'), 0, 0, tiled=True)  4.98 us
  transfers between devices with their start and end apart: 10, of which 1 were waited for; matrix products, arithmetic and copies ran while one was open for 2% of the time, Pallas kernels for 41%

profile of v2, /device:TPU:0, one launch (start us, length us, event | category | flops | bytes accessed | tf_op | source)
XLA Modules:
  0.0 96.5 jit_solution(11687756910936129231)
XLA Ops:
  0.6 0.5 collective-permute-start
  1.1 1.2 %collective-permute-done.other = bf16[16,4096]{1,0:T(8,128)(2,1)S(1)} collective-permute-done((bf16[16,4096]{1,0:T(8,128)(2,1)}, bf16[16,4096]{1,0:T(8,128)(2,1)S(1)}, u32[]{:S(2)}, u32[]{:S(2)}) %collective-permute-start) | collective-permute-done | bytes 131104 | tf_op jit(solution)/shard_map/ppermute | solution.py:482
  2.3 0.7 copy-done.4
  3.0 2.2 %pack.1 = (bf16[512,256]{1,0:T(8,128)(2,1)}, bf16[32,1536]{1,0:T(8,128)(2,1)}, bf16[32,1152]{1,0:T(8,128)(2,1)}, bf16[32,1536]{1,0:T(8,128)(2,1)}) custom-call(bf16[16,4096]{1,0:T(8,128)(2,1)} %own.1, bf16[16,4096]{1,0:T(8,128)(2,1)} %copy-done.4, s32[4,512]{1,0:T(4,128)} %face.3, s32[4,128]{1,0:T(4,128)} %corner.3, bf16[128,256]{1,0:T(8,128)(2,1)} %refs_13_.1), custom_call_target="tpu_custom_call" | custom-call | flops 1073741824 | bytes 1048576 | tf_op jit(solution)/shard_map/pack/pallas_call | solution.py:18
  5.2 4.8 %collective-permute-start.1 = (bf16[32,1536]{1,0:T(8,128)(2,1)}, bf16[32,1536]{1,0:T(8,128)(2,1)S(1)}, u32[]{:S(2)}, u32[]{:S(2)}) collective-permute-start(bf16[32,1536]{1,0:T(8,128)(2,1)} %get-tuple-element.29), channel_id=1, source_target_pairs={{0,4},{2,6},{4,8},{6,10},{8,12},{10,14},{5,1},{7,3},{9,5},{11,7},{... | collective-permute-start | bytes 294920 | tf_op jit(solution)/shard_map/ppermute | solution.py:514
  10.0 4.4 %collective-permute-start.2 = (bf16[32,1152]{1,0:T(8,128)(2,1)}, bf16[32,1152]{1,0:T(8,128)(2,1)S(1)}, u32[]{:S(2)}, u32[]{:S(2)}) collective-permute-start(bf16[32,1152]{1,0:T(8,128)(2,1)} %get-tuple-element.30), channel_id=1, source_target_pairs={{2,4},{0,6},{6,8},{4,10},{10,12},{8,14},{7,1},{5,3},{11,5},{9,7},{... | collective-permute-start | bytes 221192 | tf_op jit(solution)/shard_map/ppermute | solution.py:514
  14.4 2.2 %prepare.1 = (f32[32,2048]{1,0:T(8,128)}, f32[32,2048]{1,0:T(8,128)}, f32[1,2048]{1,0:T(1,128)}, f32[1,2048]{1,0:T(1,128)}) custom-call(s32[27,4096]{1,0:T(8,128)} %neighbours.1, s32[1,4096]{1,0:T(1,128)} %bitcast.5, s32[1,4096]{1,0:T(1,128)} %bitcast.6), custom_call_target="tpu_custom_call" | custom-call | flops 1048576 | bytes 1048576 | tf_op jit(solution)/shard_map/prepare/pallas_call | solution.py:18
  16.6 0.5 collective-permute-start.3
  17.2 0.5 collective-permute-start.4
  17.7 6.0 %own_gather.1.refs_6_ = bf16[864,512]{1,0:T(8,128)(2,1)} custom-call(bf16[512,256]{1,0:T(8,128)(2,1)} %get-tuple-element.34.table.refs_5_, f32[32,2048]{1,0:T(8,128)} %get-tuple-element.35.high.refs_7_, f32[32,2048]{1,0:T(8,128)} %get-tuple-element.36.low.refs_8_), custom_call_target="tpu_custom_call" | custom-call | flops 3623878656 | bytes 1048576 | tf_op jit(solution)/shard_map/own_gather/pallas_call | solution.py:18
  23.8 0.6 copy-done.6
  24.4 23.6 %middle.1 = (bf16[32,2048]{1,0:T(8,128)(2,1)}, f32[16,2560]{1,0:T(8,128)}, f32[16,2560]{1,0:T(8,128)}) custom-call(bf16[32,1536]{1,0:T(8,128)(2,1)} %copy-done.5, bf16[32,1152]{1,0:T(8,128)(2,1)} %copy-done.9, bf16[32,1536]{1,0:T(8,128)(2,1)} %copy-done.6, bf16[32,1536]{1,0:T(8,128)(2,1)} %copy-done.8, bf16[32,1152]{1,0:T(8,128)(2,1)} %copy-done.10, ...), custom_call_target="tpu_custom_call" | custom-call | flops 20837302272 | bytes 1048576 | tf_op jit(solution)/shard_map/middle/pallas_call | solution.py:18
  48.1 13.0 %halo_scatter.1.halo = f32[224,256]{1,0:T(8,128)} custom-call(bf16[864,32]{1,0:T(8,128)(2,1)} %bitcast.8, bf16[32,2048]{1,0:T(8,128)(2,1)} %get-tuple-element.39.grad, f32[32,2048]{1,0:T(8,128)} %get-tuple-element.35.high.refs_7_, f32[32,2048]{1,0:T(8,128)} %get-tuple-element.36.low.refs_8_), custom_call_target="tpu_custom_call" | custom-call | flops 6341787648 | bytes 1048576 | tf_op jit(solution)/shard_map/halo_scatter/pallas_call | solution.py:18
  61.1 0.7 copy-done.2
  61.8 2.1 %join.1 = (f32[16,2560]{1,0:T(8,128)}, bf16[8,32,1152]{2,1,0:T(8,128)(2,1)}) custom-call(f32[16,2560]{1,0:T(8,128)} %get-tuple-element.40.mine, f32[16,2560]{1,0:T(8,128)} %copy-done.2, f32[224,256]{1,0:T(8,128)} %halo_scatter.1.halo), custom_call_target="tpu_custom_call" | custom-call | flops 1048576 | bytes 1048576 | tf_op jit(solution)/shard_map/join/pallas_call | solution.py:18
  63.8 5.0 %all-to-all-start = ((bf16[8,32,1152]{2,1,0:T(8,128)(2,1)}), bf16[8,32,1152]{2,1,0:T(8,128)(2,1)S(1)}, u32[]{:S(2)}, u32[]{:S(2)}) async-start(bf16[8,32,1152]{2,1,0:T(8,128)(2,1)} %get-tuple-element.43), calls=%async_computation | async-start | bytes 1179648 | tf_op jit(solution)/shard_map/all_to_all | solution.py:586
  68.8 18.9 %own_scatter.1.total = f32[512,256]{1,0:T(8,128)} custom-call(bf16[864,32]{1,0:T(8,128)(2,1)} %bitcast.9, bf16[32,2048]{1,0:T(8,128)(2,1)} %get-tuple-element.39.grad, f32[32,2048]{1,0:T(8,128)} %get-tuple-element.35.high.refs_7_, f32[32,2048]{1,0:T(8,128)} %get-tuple-element.36.low.refs_8_), custom_call_target="tpu_custom_call" | custom-call | flops 14495514624 | bytes 1048576 | tf_op jit(solution)/shard_map/own_scatter/pallas_call | solution.py:18
  87.7 0.8 copy-done
  88.6 3.2 %final.1 = (f32[16,4096]{1,0:T(8,128)}, f32[16,4096]{1,0:T(8,128)}, f32[64,256]{1,0:T(8,128)}, f32[64,256]{1,0:T(8,128)}, f32[864,16]{1,0:T(8,128)}, /*index=5*/f32[32,64]{1,0:T(8,128)}) custom-call(f32[512,256]{1,0:T(8,128)} %own_scatter.1.total, f32[16,2560]{1,0:T(8,128)} %get-tuple-element.42.joined, bf16[8,32,1152]{2,1,0:T(8,128)(2,1)} %copy-done, ...), custom_call_target="tpu_custom_call" | custom-call | flops 1073741824 | bytes 1048576 | tf_op jit(solution)/shard_map/final/pallas_call | solution.py:18
  91.7 0.2 collective-permute-start.7
  91.9 0.3 collective-permute-start.8
  92.2 1.9 %copy.13 = f32[27,32,16]{1,2,0:T(8,128)} copy(f32[27,32,16]{2,1,0:T(8,128)} %bitcast.4) | data formatting | bytes 110592
  94.1 0.6 copy-done.3
  94.8 1.7 %add.1 = (bf16[16,4096]{1,0:T(8,128)(2,1)}, bf16[64,256]{1,0:T(8,128)(2,1)}) custom-call(f32[16,4096]{1,0:T(8,128)} %get-tuple-element.44.mine, f32[16,4096]{1,0:T(8,128)} %copy-done.1, f32[64,256]{1,0:T(8,128)} %get-tuple-element.46.coarse_mine, f32[64,256]{1,0:T(8,128)} %copy-done.3), custom_call_target="tpu_custom_call" | custom-call | flops 1048576 | bytes 1048576 | tf_op jit(solution)/shard_map/add/pallas_call | solution.py:18
  (28 shorter events, 0.4 us)
Async XLA Ops:
  0.6 1.7 %collective-permute-start = (bf16[16,4096]{1,0:T(8,128)(2,1)}, bf16[16,4096]{1,0:T(8,128)(2,1)S(1)}, u32[]{:S(2)}, u32[]{:S(2)}) collective-permute-start(bf16[16,4096]{1,0:T(8,128)(2,1)} %own.1), channel_id=1, source_target_pairs={{0,1},{1,0},{2,3},{3,2},{4,5},{5,4},{6,7},{7,6},{8,9},{9,8},{10,11... | collective-permute-start | bytes 393224 | tf_op jit(solution)/shard_map/ppermute | solution.py:482
  2.3 0.7 copy-start.4
  5.2 12.0 %collective-permute-start.1 = (bf16[32,1536]{1,0:T(8,128)(2,1)}, bf16[32,1536]{1,0:T(8,128)(2,1)S(1)}, u32[]{:S(2)}, u32[]{:S(2)}) collective-permute-start(bf16[32,1536]{1,0:T(8,128)(2,1)} %get-tuple-element.29), channel_id=1, source_target_pairs={{0,4},{2,6},{4,8},{6,10},{8,12},{10,14},{5,1},{7,3},{9,5},{11,7},{... | collective-permute-start | bytes 294920 | tf_op jit(solution)/shard_map/ppermute | solution.py:514
  10.0 7.1 %collective-permute-start.2 = (bf16[32,1152]{1,0:T(8,128)(2,1)}, bf16[32,1152]{1,0:T(8,128)(2,1)S(1)}, u32[]{:S(2)}, u32[]{:S(2)}) collective-permute-start(bf16[32,1152]{1,0:T(8,128)(2,1)} %get-tuple-element.30), channel_id=1, source_target_pairs={{2,4},{0,6},{6,8},{4,10},{10,12},{8,14},{7,1},{5,3},{11,5},{9,7},{... | collective-permute-start | bytes 221192 | tf_op jit(solution)/shard_map/ppermute | solution.py:514
  14.4 2.2 %copy-start.7 = (bf16[32,1536]{1,0:T(8,128)(2,1)S(1)}, bf16[32,1536]{1,0:T(8,128)(2,1)}, u32[]{:S(2)}) copy-start(bf16[32,1536]{1,0:T(8,128)(2,1)} %get-tuple-element.33) | copy-start | bytes 294916
  16.6 7.1 %collective-permute-start.3 = (bf16[32,1536]{1,0:T(8,128)(2,1)S(1)}, bf16[32,1536]{1,0:T(8,128)(2,1)S(1)}, u32[]{:S(2)}, u32[]{:S(2)}) collective-permute-start(bf16[32,1536]{1,0:T(8,128)(2,1)S(1)} %copy-done.7), channel_id=1, source_target_pairs={{2,0},{0,2},{6,4},{4,6},{10,8},{8,10},{14,12},{12,14},{3,1},{1,3},... | collective-permute-start | bytes 294920 | tf_op jit(solution)/shard_map/ppermute | solution.py:514
  17.1 6.5 %copy-start.9 = (bf16[32,1152]{1,0:T(8,128)(2,1)}, bf16[32,1152]{1,0:T(8,128)(2,1)S(1)}, u32[]{:S(2)}) copy-start(bf16[32,1152]{1,0:T(8,128)(2,1)S(1)} %collective-permute-done.2.refs_1_) | copy-start | bytes 221188
  17.2 6.5 %copy-start.5 = (bf16[32,1536]{1,0:T(8,128)(2,1)}, bf16[32,1536]{1,0:T(8,128)(2,1)S(1)}, u32[]{:S(2)}) copy-start(bf16[32,1536]{1,0:T(8,128)(2,1)S(1)} %collective-permute-done.1.refs_0_) | copy-start | bytes 294916
  17.2 6.6 %collective-permute-start.5 = (bf16[32,1152]{1,0:T(8,128)(2,1)S(1)}, bf16[32,1152]{1,0:T(8,128)(2,1)S(1)}, u32[]{:S(2)}, u32[]{:S(2)}) collective-permute-start(bf16[32,1152]{1,0:T(8,128)(2,1)S(1)} %collective-permute-done.2.refs_1_), channel_id=1, source_target_pairs={{0,1},{1,0},{2,3},{3,2},{4,5},{5,4},{6,7},{7,6},{8,9},{9,8},{10,11... | collective-permute-start | bytes 221192 | tf_op jit(solution)/shard_map/ppermute | solution.py:482
  17.2 6.5 %collective-permute-start.4 = (bf16[32,1536]{1,0:T(8,128)(2,1)S(1)}, bf16[32,1536]{1,0:T(8,128)(2,1)S(1)}, u32[]{:S(2)}, u32[]{:S(2)}) collective-permute-start(bf16[32,1536]{1,0:T(8,128)(2,1)S(1)} %collective-permute-done.1.refs_0_), channel_id=1, source_target_pairs={{0,1},{1,0},{2,3},{3,2},{4,5},{5,4},{6,7},{7,6},{8,9},{9,8},{10,11... | collective-permute-start | bytes 294920 | tf_op jit(solution)/shard_map/ppermute | solution.py:482
  23.7 0.6 copy-start.6
  23.7 0.7 copy-start.10
  23.7 0.7 copy-start.8
  48.1 13.1 %collective-permute-start.6 = (f32[16,2560]{1,0:T(8,128)}, f32[16,2560]{1,0:T(8,128)S(1)}, u32[]{:S(2)}, u32[]{:S(2)}) collective-permute-start(f32[16,2560]{1,0:T(8,128)} %get-tuple-element.41), channel_id=1, source_target_pairs={{0,1},{1,0},{2,3},{3,2},{4,5},{5,4},{6,7},{7,6},{8,9},{9,8},{10,11... | collective-permute-start | bytes 491528 | tf_op jit(solution)/shard_map/ppermute | solution.py:482
  61.1 0.7 copy-start.2
  63.8 23.9 %all-to-all-start = ((bf16[8,32,1152]{2,1,0:T(8,128)(2,1)}), bf16[8,32,1152]{2,1,0:T(8,128)(2,1)S(1)}, u32[]{:S(2)}, u32[]{:S(2)}) async-start(bf16[8,32,1152]{2,1,0:T(8,128)(2,1)} %get-tuple-element.43), calls=%async_computation | async-start | bytes 1179648 | tf_op jit(solution)/shard_map/all_to_all | solution.py:586
  87.7 0.8 copy-start
  91.7 2.4 %collective-permute-start.7 = (f32[16,4096]{1,0:T(8,128)}, f32[16,4096]{1,0:T(8,128)S(1)}, u32[]{:S(2)}, u32[]{:S(2)}) collective-permute-start(f32[16,4096]{1,0:T(8,128)} %get-tuple-element.45), channel_id=1, source_target_pairs={{0,1},{1,0},{2,3},{3,2},{4,5},{5,4},{6,7},{7,6},{8,9},{9,8},{10,11... | collective-permute-start | bytes 786440 | tf_op jit(solution)/shard_map/ppermute | solution.py:482
  91.9 2.2 %collective-permute-start.8 = (f32[64,256]{1,0:T(8,128)}, f32[64,256]{1,0:T(8,128)S(1)}, u32[]{:S(2)}, u32[]{:S(2)}) collective-permute-start(f32[64,256]{1,0:T(8,128)} %get-tuple-element.47), channel_id=1, source_target_pairs={{0,1},{1,0},{2,3},{3,2},{4,5},{5,4},{6,7},{7,6},{8,9},{9,8},{10,11... | collective-permute-start | bytes 196616 | tf_op jit(solution)/shard_map/ppermute | solution.py:482
  94.1 0.6 copy-start.3
  94.1 0.7 copy-start.1

commit v3 on v2

--- a/solution.py
+++ b/solution.py
@@ -11,10 +11,9 @@
 F32 = jnp.float32
 STEPS = ((-1, 0), (1, 0), (0, -1), (0, 1), (-1, -1), (-1, 1), (1, -1), (1, 1))
 LOW = 256
-VMEM_LIMIT = 56 << 20
-
-
-def call(kernel, name, outs, scratch, flops, *args):
+
+
+def call(kernel, name, outs, scratch, flops, mib, *args):
     return pl.pallas_call(
         kernel,
         name=name,
@@ -22,7 +21,7 @@
         in_specs=[pl.BlockSpec(memory_space=pltpu.VMEM)] * len(args),
         out_specs=[pl.BlockSpec(memory_space=pltpu.VMEM)] * len(outs),
         scratch_shapes=[pltpu.VMEM(s, d) for s, d in scratch],
-        compiler_params=pltpu.CompilerParams(vmem_limit_bytes=VMEM_LIMIT),
+        compiler_params=pltpu.CompilerParams(vmem_limit_bytes=mib << 20),
         cost_estimate=pl.CostEstimate(flops=flops, bytes_accessed=1 << 20, transcendentals=0),
     )(*args)
 
@@ -51,7 +50,7 @@
         self.tiles = nx * ny
         self.groups = ((0, 1), (3, 4), (2, 2)) if self.paired else ((0, 1), (2, 3), (4, 5), (6, 7))
         self.swaps = sum(a != b for a, b in self.groups)
-        self.early = min(2, self.half // LOW)
+        self.early = (2, 1)
         self.padded = -(-self.offsets * self.channels // 128) * 128
         self.sum_width = self.padded + self.coarse_channels * self.channels // nch // self.share
 
@@ -174,7 +173,8 @@
             messages[g][:, at : at + plan.coarse] = coarse_grad[q * n : (q + 1) * n, :]
 
 
-def gather_block(plan, table, high_ref, low_ref, out, fs, base, blocks, before=None):
+def gather_block(plan, table, high_ref, low_ref, out, fs, base, blocks, to=None, before=None):
+    to = fs if to is None else to
     n = plan.channels
     for k in range(plan.offsets):
         if k == plan.itself:
@@ -186,22 +186,24 @@
         if before is None:
             picked = jnp.zeros((n, LOW), F32)
         else:
-            picked = before[at, fs].astype(F32)
+            picked = before[at, to].astype(F32)
         for b in range(blocks):
             picked = jnp.where(high == float(base + b), part[b * n : (b + 1) * n], picked)
-        out[at, fs] = picked.astype(BF)
+        out[at, fs if before is not None else to] = picked.astype(BF)
 
 
 def columns(block):
     return pl.ds(pl.multiple_of(block * LOW, LOW), LOW)
 
 
-def own_gather_kernel(plan, table, high, low, out):
+def own_gather_kernel(plan, first, count, table, high, low, out):
+    n = plan.channels
+
     def body(j, carry):
-        gather_block(plan, table, high, low, out, columns(j), 0, plan.own_blocks)
+        gather_block(plan, table, high, low, out, columns(first + j), 0, plan.own_blocks, columns(j))
         return carry
 
-    lax.fori_loop(0, plan.early, body, 0)
+    lax.fori_loop(0, count, body, 0)
 
 
 def middle_kernel(plan, *refs):
@@ -209,10 +211,8 @@
     count = len(plan.groups)
     received, refs = refs[:count], refs[count:]
     swapped, refs = refs[: plan.swaps], refs[plan.swaps :]
-    own_table, before, high, low, side, slot, weight, coarse_weight, coarse_grad, refs = (
-        *refs[:9],
-        refs[9:],
-    )
+    befores, refs = refs[: len(plan.early)], refs[len(plan.early) :]
+    own_table, high, low, side, slot, weight, coarse_weight, coarse_grad, refs = (*refs[:8], refs[8:])
     grad_out, mine_out, theirs_out, table, rows, coarse_all, pooled_all, sums, parts, coarse_sum = refs
     core, _, _ = where_am_i(plan)
     messages = {}
@@ -242,19 +242,32 @@
             at = plan.widths[k] + g * m
             coarse_all[g * n : (g + 1) * n, (k + 1) * m : (k + 2) * m] = messages[k][:, at : at + m]
 
-    def rest(j, carry):
-        fs = columns(j)
-        gather_block(plan, table.at[own:, :], high, low, rows, fs, plan.own_blocks, plan.halo_blocks, before)
+    def whole(j, carry):
+        gather_block(plan, table, high, low, rows, columns(j), 0, plan.own_blocks + plan.halo_blocks)
         return carry
 
-    def whole(j, carry):
-        fs = columns(j)
-        gather_block(plan, table, high, low, rows, fs, 0, plan.own_blocks + plan.halo_blocks)
-        return carry
-
-    if plan.early:
-        lax.fori_loop(0, plan.early, rest, 0)
-    lax.fori_loop(plan.early, plan.half // LOW, whole, 0)
+    done = 0
+    halo_table = table.at[own:, :]
+    for before, count in zip(befores, plan.early):
+
+        def rest(j, carry):
+            gather_block(
+                plan,
+                halo_table,
+                high,
+                low,
+                rows,
+                columns(done + j),
+                plan.own_blocks,
+                plan.halo_blocks,
+                columns(j),
+                before,
+            )
+            return carry
+
+        lax.fori_loop(0, count, rest, 0)
+        done += count
+    lax.fori_loop(done, plan.half // LOW, whole, 0)
     for j in range(plan.half // LOW):
         at = pl.multiple_of((core * (plan.half // LOW) + j) * n, n)
         rows[plan.itself * n : (plan.itself + 1) * n, j * LOW : (j + 1) * LOW] = table[pl.ds(at, n), :]
@@ -323,14 +336,16 @@
     n = plan.channels
     total[...] = jnp.zeros_like(total)
 
+    width = min(plan.half, 2 * LOW)
+
     def body(j, carry):
-        fs = columns(j)
+        fs = pl.ds(pl.multiple_of(j * width, width), width)
         masked, hots = [], []
         for k in range(plan.offsets):
             if k == plan.itself:
                 continue
             high = high_ref[k : k + 1, fs].astype(BF)
-            hots.append(lows(low_ref[k : k + 1, fs].astype(BF), LOW, LOW))
+            hots.append(lows(low_ref[k : k + 1, fs].astype(BF), LOW, width))
             value = values[k * n : (k + 1) * n, fs]
             masked.append(
                 jnp.concatenate(
@@ -345,7 +360,7 @@
         )
         return carry
 
-    lax.fori_loop(0, plan.half // LOW, body, 0)
+    lax.fori_loop(0, plan.half // width, body, 0)
 
 
 def spread_values(plan, weight, grad, values):
@@ -443,7 +458,8 @@
     for t in range(1, plan.tiles):
         summed = summed + arrived[t, :, :width].astype(F32)
     summed = jnp.concatenate([summed[q * s : (q + 1) * s] for q in range(n // s)], axis=1)
-    conv_out[...] = jnp.transpose(summed)[: plan.offsets * n]
+    for k in range(plan.offsets):
+        conv_out[k] = summed[:, k * n : (k + 1) * n]
     for q in range(n // s):
         at = plan.padded + q * share
         coarse_grad_out[q * s : (q + 1) * s, :] = summed[:, at : at + share]
@@ -481,8 +497,8 @@
     def swap(value):
         return lax.ppermute(value, "ch", [(0, 1), (1, 0)])
 
-    def run(kernel, name, outs, scratch, flops, *args):
-        return call(functools.partial(kernel, plan), name, outs, scratch, flops, *args)
+    def run(kernel, name, outs, scratch, flops, mib, *args):
+        return call(functools.partial(kernel, plan), name, outs, scratch, flops, mib, *args)
 
     other = swap(fine_features)
     tall = -(-plan.offsets // 8) * 8
@@ -492,11 +508,13 @@
         [((tall, half), F32), ((tall, half), F32), ((1, half), F32), ((1, half), F32)],
         [],
         1 << 20,
+        6,
         neighbours,
         owner_side.reshape(1, -1),
         owner_slot.reshape(1, -1),
     )
     extra = plan.coarse_channels // n * m
+    own, side = lax.optimization_barrier((fine_features, side))
     table, *sent = run(
         pack_kernel,
         "pack",
@@ -504,7 +522,8 @@
         + [((n, plan.widths[first] + extra), BF) for first, _ in plan.groups],
         [],
         1 << 30,
-        fine_features,
+        6,
+        own,
         other,
         face_send,
         corner_send,
@@ -515,22 +534,31 @@
         for value, (first, second) in zip(sent, plan.groups)
     ]
     split = [g for g, (first, second) in enumerate(plan.groups) if first != second]
-    early_table, *ready = lax.optimization_barrier((table, *[received[g] for g in split]))
-    for g, value in zip(split, ready):
-        received[g] = value
-    swapped = [swap(received[g]) for g in split]
     work = 2 * wide * half * LOW
-    early = plan.early * LOW
-    (before,) = run(
-        own_gather_kernel,
-        "own_gather",
-        [((wide, early), BF)],
-        [],
-        work * plan.own_blocks * early // half,
-        early_table,
-        high,
-        low,
-    )
+    befores = []
+    early_table, first = table, 0
+    for step, count in enumerate(plan.early):
+        (before,) = call(
+            functools.partial(own_gather_kernel, plan, first, count),
+            "own_gather",
+            [((wide, count * LOW), BF)],
+            [],
+            work * plan.own_blocks * count * LOW // half,
+            16,
+            early_table,
+            high,
+            low,
+        )
+        befores.append(before)
+        first += count
+        if step == 0:
+            early_table, before, *ready = lax.optimization_barrier(
+                (table, before, *[received[g] for g in split])
+            )
+            befores[0] = before
+            for g, value in zip(split, ready):
+                received[g] = value
+            swapped = [swap(received[g]) for g in split]
     weight = conv_weight.reshape(wide, n)
     owners = plan.slots + 1
     across = plan.sum_width + owners * m
@@ -548,10 +576,11 @@
             ((n, plan.sum_width - plan.padded), F32),
         ],
         work * (plan.own_blocks + plan.halo_blocks),
+        24,
         *received,
         *swapped,
+        *befores,
         table,
-        before,
         high,
         low,
         side,
@@ -567,6 +596,7 @@
         [((plan.halo_blocks * n, LOW), F32)],
         [((wide, half), BF)],
         work * plan.halo_blocks,
+        16,
         weight,
         grad,
         high,
@@ -579,6 +609,7 @@
         [((s, across), F32), ((plan.tiles, n, message), BF)],
         [],
         1 << 20,
+        6,
         mine,
         theirs,
         halo,
@@ -590,6 +621,7 @@
         [((plan.own_blocks * n, LOW), F32)],
         [((wide, half), BF)],
         work * plan.own_blocks,
+        16,
         weight,
         grad,
         high,
@@ -599,9 +631,10 @@
     mine, theirs, coarse_mine, coarse_theirs, conv_weight_grad, coarse_weight_grad = run(
         final_kernel,
         "final",
-        [((s, plan.voxels), F32)] * 2 + [((share, m), F32)] * 2 + [((wide, s), F32), ((n, share), F32)],
+        [((s, plan.voxels), F32)] * 2 + [((share, m), F32)] * 2 + [((plan.offsets, s, n), F32), ((n, share), F32)],
         [((plan.own_blocks * n, LOW), F32), ((plan.coarse_channels, m), F32)],
         1 << 30,
+        12,
         total,
         joined,
         arrived,
@@ -615,12 +648,13 @@
         [((s, plan.voxels), BF), ((share, m), BF)],
         [],
         1 << 20,
+        6,
         mine,
         swap(theirs),
         coarse_mine,
         swap(coarse_theirs),
     )
-    return (coarse_out, input_grad, conv_weight_grad.reshape(plan.offsets, n, s), coarse_weight_grad)
+    return (coarse_out, input_grad, conv_weight_grad.transpose(0, 2, 1), coarse_weight_grad)
 
 
 def solution(mesh):

time: 97 us -> 76.5 us (0.79)
  Pallas kernels: 72.7 us -> 55.6 us
  local copies, waits for them, and re-layouts: 5.41 us -> 3.09 us
  starting transfers between devices: 16.4 us -> 15 us
    pallas_call x9 -> x10, Pallas kernels: 72.7 us -> 55.6 us  [call(): pl.pallas_call(kernel, name=name, out_shape=[jax.ShapeDtypeStruct(s, d) f...]
    unnamed x23 -> x18, local copies, waits for them, and re-layouts: 5.41 us -> 3.09 us
    all_to_all x1, starting transfers between devices: 4.98 us -> 3.79 us  [shards(): arrived = lax.all_to_all(send, ('tx', 'ty'), 0, 0, tiled=True)]
  transfers between devices with their start and end apart: 10 -> 10, of which waited for: 1 -> 2; matrix products, arithmetic and copies ran while one was open for 2% -> 0% of each run, Pallas kernels for 41% -> 43%
where the time goes in v3:
time: 76.5 us; the launch traced here: 76.1 us
  Pallas kernels  55.6 us (73%)
  starting transfers between devices  15 us (20%)
  local copies, waits for them, and re-layouts  3.09 us (4%)
  waiting for transfers between devices  1.64 us (2%)
  between operations  0.8 us (1%)
    pallas_call x10, Pallas kernels, call(): pl.pallas_call(kernel, name=name, out_shape=[jax.ShapeDtypeStruct(s, d) f...  55.6 us
    ppermute x3, starting transfers between devices, shards(): lax.ppermute(value, ('tx', 'ty', 'ch'), plan.pairs(first, second))  9.51 us
    all_to_all x1, starting transfers between devices, shards(): arrived = lax.all_to_all(send, ('tx', 'ty'), 0, 0, tiled=True)  3.79 us
    unnamed x18, local copies, waits for them, and re-layouts  3.09 us
    ppermute x6, starting transfers between devices, swap(): return lax.ppermute(value, 'ch', [(0, 1), (1, 0)])  1.71 us
  transfers between devices with their start and end apart: 10, of which 2 were waited for; matrix products, arithmetic and copies ran while one was open for 0% of the time, Pallas kernels for 43%

profile of v3, /device:TPU:0, one launch (start us, length us, event | category | flops | bytes accessed | tf_op | source)
XLA Modules:
  0.0 76.1 jit_solution(4497082668887380971)
XLA Ops:
  0.6 0.5 collective-permute-start
  1.2 1.0 %copy-done = s32[27,4096]{1,0:T(8,128)S(1)} copy-done((s32[27,4096]{1,0:T(8,128)S(1)}, s32[27,4096]{1,0:T(8,128)}, u32[]{:S(2)}) %copy-start) | copy-done | bytes 442392
  2.2 0.7 copy-done.1
  2.9 0.7 copy-done.2
  3.6 0.3 prepare.1
  3.9 0.6 copy-done.4
  4.5 0.5 pack.1
  5.1 5.4 %collective-permute-start.2 = (bf16[32,1152]{1,0:T(8,128)(2,1)S(1)}, bf16[32,1152]{1,0:T(8,128)(2,1)S(1)}, u32[]{:S(2)}, u32[]{:S(2)}) collective-permute-start(bf16[32,1152]{1,0:T(8,128)(2,1)S(1)} %get-tuple-element.37), channel_id=1, source_target_pairs={{2,4},{0,6},{6,8},{4,10},{10,12},{8,14},{7,1},{5,3},{11,5},{9,7},{... | collective-permute-start | bytes 221192 | tf_op jit(solution)/shard_map/ppermute | solution.py:533
  10.5 3.5 %collective-permute-start.1 = (bf16[32,1536]{1,0:T(8,128)(2,1)S(1)}, bf16[32,1536]{1,0:T(8,128)(2,1)S(1)}, u32[]{:S(2)}, u32[]{:S(2)}) collective-permute-start(bf16[32,1536]{1,0:T(8,128)(2,1)S(1)} %get-tuple-element.36), channel_id=1, source_target_pairs={{0,4},{2,6},{4,8},{6,10},{8,12},{10,14},{5,1},{7,3},{9,5},{11,7},{... | collective-permute-start | bytes 294920 | tf_op jit(solution)/shard_map/ppermute | solution.py:533
  14.0 0.6 collective-permute-start.3
  14.6 3.9 %own_gather.2.refs_5_ = bf16[864,512]{1,0:T(8,128)(2,1)S(1)} custom-call(bf16[512,256]{1,0:T(8,128)(2,1)S(1)} %get-tuple-element.42.table.refs_7_, f32[32,2048]{1,0:T(8,128)S(1)} %get-tuple-element.34.high.refs_8_, f32[32,2048]{1,0:T(8,128)S(1)} %get-tuple-element.35.low.refs_9_), custom_call_target="tpu_custom_call" | custom-call | flops 3623878656 | bytes 1048576 | tf_op jit(solution)/shard_map/own_gather/pallas_call | solution.py:17
  18.6 0.5 collective-permute-start.4
  19.1 1.9 %own_gather.3.refs_6_ = bf16[864,256]{1,0:T(8,128)(2,1)S(1)} custom-call(bf16[512,256]{1,0:T(8,128)(2,1)S(1)} %get-tuple-element.42.table.refs_7_, f32[32,2048]{1,0:T(8,128)S(1)} %get-tuple-element.34.high.refs_8_, f32[32,2048]{1,0:T(8,128)S(1)} %get-tuple-element.35.low.refs_9_), custom_call_target="tpu_custom_call" | custom-call | flops 1811939328 | bytes 1048576 | tf_op jit(solution)/shard_map/own_gather/pallas_call | solution.py:17
  21.1 19.5 %middle.1 = (bf16[32,2048]{1,0:T(8,128)(2,1)S(1)}, f32[16,2560]{1,0:T(8,128)S(1)}, f32[16,2560]{1,0:T(8,128)S(1)}) custom-call(bf16[32,1536]{1,0:T(8,128)(2,1)S(1)} %collective-permute-done.1.refs_0_, bf16[32,1152]{1,0:T(8,128)(2,1)S(1)} %collective-permute-done.2.refs_1_, bf16[32,1536]{1,0:T(8,128)(2,1)S(1)} %collective-permute-done.3.refs_2_, ...), custom_call_target="tpu_custom_call" | custom-call | flops 20837302272 | bytes 1048576 | tf_op jit(solution)/shard_map/middle/pallas_call | solution.py:17
  40.6 0.1 collective-permute-start.6
  40.7 10.4 %halo_scatter.1.halo = f32[224,256]{1,0:T(8,128)S(1)} custom-call(bf16[864,32]{1,0:T(8,128)(2,1)S(1)} %bitcast.7, bf16[32,2048]{1,0:T(8,128)(2,1)S(1)} %get-tuple-element.45.grad, f32[32,2048]{1,0:T(8,128)S(1)} %get-tuple-element.34.high.refs_8_, f32[32,2048]{1,0:T(8,128)S(1)} %get-tuple-element.35.low.refs_9_), custom_call_target="tpu_custom_call" | custom-call | flops 6341787648 | bytes 1048576 | tf_op jit(solution)/shard_map/halo_scatter/pallas_call | solution.py:17
  51.2 0.9 %join.1 = (f32[16,2560]{1,0:T(8,128)S(1)}, bf16[8,32,1152]{2,1,0:T(8,128)(2,1)}) custom-call(f32[16,2560]{1,0:T(8,128)S(1)} %get-tuple-element.46.mine, f32[16,2560]{1,0:T(8,128)S(1)} %collective-permute-done.6.theirs, f32[224,256]{1,0:T(8,128)S(1)} %halo_scatter.1.halo), custom_call_target="tpu_custom_call" | custom-call | flops 1048576 | bytes 1048576 | tf_op jit(solution)/shard_map/join/pallas_call | solution.py:17
  52.1 3.8 %all-to-all-start = ((bf16[8,32,1152]{2,1,0:T(8,128)(2,1)}), bf16[8,32,1152]{2,1,0:T(8,128)(2,1)S(1)}, u32[]{:S(2)}, u32[]{:S(2)}) async-start(bf16[8,32,1152]{2,1,0:T(8,128)(2,1)} %get-tuple-element.49), calls=%async_computation | async-start | bytes 1179648 | tf_op jit(solution)/shard_map/all_to_all | solution.py:617
  55.9 16.0 %own_scatter.1.total = f32[512,256]{1,0:T(8,128)S(1)} custom-call(bf16[864,32]{1,0:T(8,128)(2,1)S(1)} %bitcast.8, bf16[32,2048]{1,0:T(8,128)(2,1)S(1)} %get-tuple-element.45.grad, f32[32,2048]{1,0:T(8,128)S(1)} %get-tuple-element.34.high.refs_8_, f32[32,2048]{1,0:T(8,128)S(1)} %get-tuple-element.35.low.refs_9_), custom_call_target="tpu_custom_call" | custom-call | flops 14495514624 | bytes 1048576 | tf_op jit(solution)/shard_map/own_scatter/pallas_call | solution.py:17
  71.9 0.5 all-to-all-done.arrived
  72.4 1.4 %final.1 = (f32[16,4096]{1,0:T(8,128)S(1)}, f32[16,4096]{1,0:T(8,128)S(1)}, f32[64,256]{1,0:T(8,128)S(1)}, f32[64,256]{1,0:T(8,128)S(1)}, f32[27,16,32]{2,1,0:T(8,128)}, /*index=5*/f32[32,64]{1,0:T(8,128)}) custom-call(f32[512,256]{1,0:T(8,128)S(1)} %own_scatter.1.total, f32[16,2560]{1,0:T(8,128)S(1)} %get-tuple-element.48.joined, ...), custom_call_target="tpu_custom_call" | custom-call | flops 1073741824 | bytes 1048576 | tf_op jit(solution)/shard_map/final/pallas_call | solution.py:17
  73.8 0.5 collective-permute-start.8
  74.3 1.1 %collective-permute-done.8.coarse_theirs = f32[64,256]{1,0:T(8,128)S(1)} collective-permute-done((f32[64,256]{1,0:T(8,128)S(1)}, f32[64,256]{1,0:T(8,128)S(1)}, u32[]{:S(2)}, u32[]{:S(2)}) %collective-permute-start.8) | collective-permute-done | bytes 65568 | tf_op jit(solution)/shard_map/ppermute | solution.py:498
  75.4 0.7 add.1
  (24 shorter events, 0.1 us)
Async XLA Ops:
  0.6 3.3 %collective-permute-start = (bf16[16,4096]{1,0:T(8,128)(2,1)}, bf16[16,4096]{1,0:T(8,128)(2,1)S(1)}, u32[]{:S(2)}, u32[]{:S(2)}) collective-permute-start(bf16[16,4096]{1,0:T(8,128)(2,1)} %own), channel_id=1, source_target_pairs={{0,1},{1,0},{2,3},{3,2},{4,5},{5,4},{6,7},{7,6},{8,9},{9,8},{10,11... | collective-permute-start | bytes 393224 | tf_op jit(solution)/shard_map/ppermute | solution.py:498
  1.2 1.0 %copy-start = (s32[27,4096]{1,0:T(8,128)S(1)}, s32[27,4096]{1,0:T(8,128)}, u32[]{:S(2)}) copy-start(s32[27,4096]{1,0:T(8,128)} %neighbours.1) | copy-start | bytes 1327108
  2.2 0.7 copy-start.1
  2.9 0.7 copy-start.2
  3.6 0.9 %copy-start.4 = (bf16[16,4096]{1,0:T(8,128)(2,1)S(1)}, bf16[16,4096]{1,0:T(8,128)(2,1)}, u32[]{:S(2)}) copy-start(bf16[16,4096]{1,0:T(8,128)(2,1)} %own) | copy-start | bytes 393220
  3.6 0.9 %copy-start.5 = (bf16[128,256]{1,0:T(8,128)(2,1)S(1)}, bf16[128,256]{1,0:T(8,128)(2,1)}, u32[]{:S(2)}) copy-start(bf16[128,256]{1,0:T(8,128)(2,1)} %refs_14_.1) | copy-start | bytes 196612
  3.6 0.9 %copy-start.6 = (s32[4,512]{1,0:T(4,128)S(1)}, s32[4,512]{1,0:T(4,128)}, u32[]{:S(2)}) copy-start(s32[4,512]{1,0:T(4,128)} %face.3) | copy-start | bytes 24580
  3.6 0.9 %copy-start.8 = (s32[4,128]{1,0:T(4,128)S(1)}, s32[4,128]{1,0:T(4,128)}, u32[]{:S(2)}) copy-start(s32[4,128]{1,0:T(4,128)} %corner.3) | copy-start | bytes 6148
  5.1 13.5 %collective-permute-start.2 = (bf16[32,1152]{1,0:T(8,128)(2,1)S(1)}, bf16[32,1152]{1,0:T(8,128)(2,1)S(1)}, u32[]{:S(2)}, u32[]{:S(2)}) collective-permute-start(bf16[32,1152]{1,0:T(8,128)(2,1)S(1)} %get-tuple-element.37), channel_id=1, source_target_pairs={{2,4},{0,6},{6,8},{4,10},{10,12},{8,14},{7,1},{5,3},{11,5},{9,7},{... | collective-permute-start | bytes 221192 | tf_op jit(solution)/shard_map/ppermute | solution.py:533
  10.5 8.0 %collective-permute-start.1 = (bf16[32,1536]{1,0:T(8,128)(2,1)S(1)}, bf16[32,1536]{1,0:T(8,128)(2,1)S(1)}, u32[]{:S(2)}, u32[]{:S(2)}) collective-permute-start(bf16[32,1536]{1,0:T(8,128)(2,1)S(1)} %get-tuple-element.36), channel_id=1, source_target_pairs={{0,4},{2,6},{4,8},{6,10},{8,12},{10,14},{5,1},{7,3},{9,5},{11,7},{... | collective-permute-start | bytes 294920 | tf_op jit(solution)/shard_map/ppermute | solution.py:533
  14.0 7.1 %collective-permute-start.3 = (bf16[32,1536]{1,0:T(8,128)(2,1)S(1)}, bf16[32,1536]{1,0:T(8,128)(2,1)S(1)}, u32[]{:S(2)}, u32[]{:S(2)}) collective-permute-start(bf16[32,1536]{1,0:T(8,128)(2,1)S(1)} %get-tuple-element.40), channel_id=1, source_target_pairs={{2,0},{0,2},{6,4},{4,6},{10,8},{8,10},{14,12},{12,14},{3,1},{1,3},... | collective-permute-start | bytes 294920 | tf_op jit(solution)/shard_map/ppermute | solution.py:533
  18.5 2.6 %copy-start.3 = (bf16[27,32,32]{2,1,0:T(8,128)(2,1)S(1)}, bf16[27,32,32]{2,1,0:T(8,128)(2,1)}, u32[]{:S(2)}) copy-start(bf16[27,32,32]{2,1,0:T(8,128)(2,1)} %param.15) | copy-start | bytes 165892
  18.5 2.6 %copy-start.7 = (bf16[32,128]{1,0:T(8,128)(2,1)S(1)}, bf16[32,128]{1,0:T(8,128)(2,1)}, u32[]{:S(2)}) copy-start(bf16[32,128]{1,0:T(8,128)(2,1)} %coarse_weight.1) | copy-start | bytes 24580
  18.5 2.5 %collective-permute-start.5 = (bf16[32,1152]{1,0:T(8,128)(2,1)S(1)}, bf16[32,1152]{1,0:T(8,128)(2,1)S(1)}, u32[]{:S(2)}, u32[]{:S(2)}) collective-permute-start(bf16[32,1152]{1,0:T(8,128)(2,1)S(1)} %collective-permute-done.2.refs_1_), channel_id=1, source_target_pairs={{0,1},{1,0},{2,3},{3,2},{4,5},{5,4},{6,7},{7,6},{8,9},{9,8},{10,11... | collective-permute-start | bytes 221192 | tf_op jit(solution)/shard_map/ppermute | solution.py:498
  18.6 2.5 %collective-permute-start.4 = (bf16[32,1536]{1,0:T(8,128)(2,1)S(1)}, bf16[32,1536]{1,0:T(8,128)(2,1)S(1)}, u32[]{:S(2)}, u32[]{:S(2)}) collective-permute-start(bf16[32,1536]{1,0:T(8,128)(2,1)S(1)} %collective-permute-done.1.refs_0_), channel_id=1, source_target_pairs={{0,1},{1,0},{2,3},{3,2},{4,5},{5,4},{6,7},{7,6},{8,9},{9,8},{10,11... | collective-permute-start | bytes 294920 | tf_op jit(solution)/shard_map/ppermute | solution.py:498
  40.6 10.6 %collective-permute-start.6 = (f32[16,2560]{1,0:T(8,128)S(1)}, f32[16,2560]{1,0:T(8,128)S(1)}, u32[]{:S(2)}, u32[]{:S(2)}) collective-permute-start(f32[16,2560]{1,0:T(8,128)S(1)} %get-tuple-element.47), channel_id=1, source_target_pairs={{0,1},{1,0},{2,3},{3,2},{4,5},{5,4},{6,7},{7,6},{8,9},{9,8},{10,11... | collective-permute-start | bytes 491528 | tf_op jit(solution)/shard_map/ppermute | solution.py:498
  52.1 20.3 %all-to-all-start = ((bf16[8,32,1152]{2,1,0:T(8,128)(2,1)}), bf16[8,32,1152]{2,1,0:T(8,128)(2,1)S(1)}, u32[]{:S(2)}, u32[]{:S(2)}) async-start(bf16[8,32,1152]{2,1,0:T(8,128)(2,1)} %get-tuple-element.49), calls=%async_computation | async-start | bytes 1179648 | tf_op jit(solution)/shard_map/all_to_all | solution.py:617
  73.8 1.6 %collective-permute-start.7 = (f32[16,4096]{1,0:T(8,128)S(1)}, f32[16,4096]{1,0:T(8,128)S(1)}, u32[]{:S(2)}, u32[]{:S(2)}) collective-permute-start(f32[16,4096]{1,0:T(8,128)S(1)} %get-tuple-element.51), channel_id=1, source_target_pairs={{0,1},{1,0},{2,3},{3,2},{4,5},{5,4},{6,7},{7,6},{8,9},{9,8},{10,11... | collective-permute-start | bytes 786440 | tf_op jit(solution)/shard_map/ppermute | solution.py:498
  73.8 1.6 %collective-permute-start.8 = (f32[64,256]{1,0:T(8,128)S(1)}, f32[64,256]{1,0:T(8,128)S(1)}, u32[]{:S(2)}, u32[]{:S(2)}) collective-permute-start(f32[64,256]{1,0:T(8,128)S(1)} %get-tuple-element.53), channel_id=1, source_target_pairs={{0,1},{1,0},{2,3},{3,2},{4,5},{5,4},{6,7},{7,6},{8,9},{9,8},{10,11... | collective-permute-start | bytes 196616 | tf_op jit(solution)/shard_map/ppermute | solution.py:498

commit v4 on v3

--- a/solution.py
+++ b/solution.py
@@ -46,6 +46,7 @@
         self.halo_blocks = self.halo // LOW
         self.starts = [sum(self.widths[:s]) for s in range(self.slots)]
         self.nothing = self.voxels + self.halo
+        self.wrapped = self.paired and nx % 2 == 0
         self.itself = self.offsets // 2
         self.tiles = nx * ny
         self.groups = ((0, 1), (3, 4), (2, 2)) if self.paired else ((0, 1), (2, 3), (4, 5), (6, 7))
@@ -59,17 +60,25 @@
             return ((0,), (1,), (2, 3), (4, 5), (6, 7))[slot]
         return (slot,)
 
+    def is_first(self, core, x):
+        return (core + x) % 2 == 1 if self.paired else core == 0
+
     def pairs(self, first, second):
         found = []
-        for core, slot in enumerate((first, second)):
+        for core in range(self.nch):
             for x in range(self.nx):
                 for y in range(self.ny):
-                    for d in self.directions(slot):
+                    for d in self.directions(first if self.is_first(core, x) else second):
                         sx, sy = x + STEPS[d][0], y + STEPS[d][1]
+                        if self.wrapped:
+                            sx %= self.nx
                         if 0 <= sx < self.nx and 0 <= sy < self.ny:
                             here, there = x * self.ny + y, sx * self.ny + sy
                             found.append((there * self.nch + core, here * self.nch + core))
         return found
+
+    def sent_first(self, core, x):
+        return jnp.logical_not(self.is_first(core, x)) if self.paired else self.is_first(core, x)
 
     def opposite(self, slot):
         return ((1, 0, 2, 4, 3) if self.paired else (1, 0, 3, 2, 7, 6, 5, 4))[slot]
@@ -134,7 +143,7 @@
     return core, x, y
 
 
-def prepare_kernel(plan, neighbours, side, slot, high_out, low_out, side_out, slot_out):
+def prepare_kernel(plan, neighbours, high_out, low_out):
     core, _, y = where_am_i(plan)
     mine = pl.ds(pl.multiple_of(core * plan.half, plan.half), plan.half)
     rows = plan.rows(neighbours[:, mine], y)
@@ -143,12 +152,10 @@
     rows = jnp.concatenate([rows, fill], axis=0) if pad else rows
     high_out[...] = lax.shift_right_logical(rows, 8).astype(F32)
     low_out[...] = (rows & (LOW - 1)).astype(F32)
-    side_out[...] = plan.owner_slots(side[:, mine]).astype(F32)
-    slot_out[...] = slot[:, mine].astype(F32)
 
 
 def pack_kernel(plan, own, other, face, corner, coarse_grad, table, *messages):
-    core, _, y = where_am_i(plan)
+    core, x, y = where_am_i(plan)
     s, n = plan.share, plan.channels
     at_own = pl.multiple_of(core * s, s)
     at_other = pl.multiple_of((1 - core) * s, s)
@@ -160,7 +167,7 @@
         width = plan.widths[first]
         rows = plan.send_rows(first, y, face, corner)
         if second != first:
-            rows = jnp.where(core == 0, rows, plan.send_rows(second, y, face, corner))
+            rows = jnp.where(plan.sent_first(core, x), rows, plan.send_rows(second, y, face, corner))
         high = lax.shift_right_logical(rows, 8)
         hot = lows((rows & (LOW - 1)).astype(F32).astype(BF), LOW, width)
         part = jnp.dot(table[...], hot, preferred_element_type=F32)
@@ -214,7 +221,8 @@
     befores, refs = refs[: len(plan.early)], refs[len(plan.early) :]
     own_table, high, low, side, slot, weight, coarse_weight, coarse_grad, refs = (*refs[:8], refs[8:])
     grad_out, mine_out, theirs_out, table, rows, coarse_all, pooled_all, sums, parts, coarse_sum = refs
-    core, _, _ = where_am_i(plan)
+    core, x, y = where_am_i(plan)
+    is_first = plan.is_first(core, x)
     messages = {}
     other = iter(swapped)
     for g, (first, second) in enumerate(plan.groups):
@@ -223,8 +231,12 @@
             messages[first] = here
         else:
             there = next(other)[...]
-            messages[first] = jnp.where(core == 0, here, there)
-            messages[second] = jnp.where(core == 0, there, here)
+            messages[first] = jnp.where(is_first, here, there)
+            messages[second] = jnp.where(is_first, there, here)
+    if plan.wrapped:
+        for k in range(plan.slots):
+            here = messages[k]
+            messages[k] = jnp.where(plan.bordering(k, x, y) >= 0, here, jnp.zeros_like(here))
     own = plan.own_blocks * n
     table[:own, :] = own_table[...]
     for k in range(plan.slots):
@@ -288,9 +300,10 @@
         )
         sigma = 1.0 / (1.0 + jnp.exp(-hidden))
         active = (hidden * sigma).astype(BF)
-        owner = side[:, fs]
+        mine = pl.ds(pl.multiple_of(core * plan.half + c * chunk, LOW), chunk)
+        owner = plan.owner_slots(side[:, mine]).astype(F32)
         owner_low = owner.astype(BF)
-        hot = lows(slot[:, fs].astype(BF), m, chunk)
+        hot = lows(slot[:, mine].astype(F32).astype(BF), m, chunk)
         spread = jnp.concatenate(
             [jnp.where(owner_low == BF(k), active, BF(0)) for k in range(owners)], axis=0
         )
@@ -502,19 +515,16 @@
 
     other = swap(fine_features)
     tall = -(-plan.offsets // 8) * 8
-    high, low, side, slot = run(
+    high, low = run(
         prepare_kernel,
         "prepare",
-        [((tall, half), F32), ((tall, half), F32), ((1, half), F32), ((1, half), F32)],
+        [((tall, half), F32), ((tall, half), F32)],
         [],
         1 << 20,
         6,
         neighbours,
-        owner_side.reshape(1, -1),
-        owner_slot.reshape(1, -1),
     )
     extra = plan.coarse_channels // n * m
-    own, side = lax.optimization_barrier((fine_features, side))
     table, *sent = run(
         pack_kernel,
         "pack",
@@ -523,7 +533,7 @@
         [],
         1 << 30,
         6,
-        own,
+        fine_features,
         other,
         face_send,
         corner_send,
@@ -583,8 +593,8 @@
         table,
         high,
         low,
-        side,
-        slot,
+        owner_side.reshape(1, -1),
+        owner_slot.reshape(1, -1),
         weight,
         coarse_weight,
         coarse_grad,

time: 76.5 us -> 73.1 us (0.956)
  starting transfers between devices: 15 us -> 12.9 us
  local copies, waits for them, and re-layouts: 3.09 us -> 1.68 us
    ppermute x3, starting transfers between devices: 9.51 us -> 4.22 us  [shards(): lax.ppermute(value, ('tx', 'ty', 'ch'), plan.pairs(first, second))]
    ppermute x6, starting transfers between devices: 1.71 us -> 3.92 us  [swap(): return lax.ppermute(value, 'ch', [(0, 1), (1, 0)])]
    unnamed x18, local copies, waits for them, and re-layouts: 3.09 us -> 1.68 us
    all_to_all x1, starting transfers between devices: 3.79 us -> 4.77 us  [shards(): arrived = lax.all_to_all(send, ('tx', 'ty'), 0, 0, tiled=True)]
  transfers between devices with their start and end apart: 10 -> 10, of which waited for: 2 -> 3; matrix products, arithmetic and copies ran while one was open for 0% -> 0% of each run, Pallas kernels for 43% -> 45%
where the time goes in v4:
time: 73.1 us; the launch traced here: 72.8 us
  Pallas kernels  55.6 us (76%)
  starting transfers between devices  12.9 us (18%)
  waiting for transfers between devices  1.83 us (3%)
  local copies, waits for them, and re-layouts  1.68 us (2%)
  between operations  0.8 us (1%)
    pallas_call x10, Pallas kernels, call(): pl.pallas_call(kernel, name=name, out_shape=[jax.ShapeDtypeStruct(s, d) f...  55.6 us
    all_to_all x1, starting transfers between devices, shards(): arrived = lax.all_to_all(send, ('tx', 'ty'), 0, 0, tiled=True)  4.77 us
    ppermute x3, starting transfers between devices, shards(): lax.ppermute(value, ('tx', 'ty', 'ch'), plan.pairs(first, second))  4.22 us
    ppermute x6, starting transfers between devices, swap(): return lax.ppermute(value, 'ch', [(0, 1), (1, 0)])  3.92 us
    unnamed x18, local copies, waits for them, and re-layouts  1.68 us
  transfers between devices with their start and end apart: 10, of which 3 were waited for; matrix products, arithmetic and copies ran while one was open for 0% of the time, Pallas kernels for 45%

profile of v4, /device:TPU:0, one launch (start us, length us, event | category | flops | bytes accessed | tf_op | source)
XLA Modules:
  0.0 72.8 jit_solution(17712344406423479929)
XLA Ops:
  0.6 0.5 collective-permute-start
  1.2 1.0 %copy-done = s32[27,4096]{1,0:T(8,128)S(1)} copy-done((s32[27,4096]{1,0:T(8,128)S(1)}, s32[27,4096]{1,0:T(8,128)}, u32[]{:S(2)}) %copy-start) | copy-done | bytes 442392
  2.2 0.3 prepare.1
  2.5 0.6 copy-done.2
  3.1 0.5 pack.1
  3.6 3.6 %collective-permute-start.2 = (bf16[32,1152]{1,0:T(8,128)(2,1)S(1)}, bf16[32,1152]{1,0:T(8,128)(2,1)S(1)}, u32[]{:S(2)}, u32[]{:S(2)}) collective-permute-start(bf16[32,1152]{1,0:T(8,128)(2,1)S(1)} %get-tuple-element.31), channel_id=1, source_target_pairs={{6,0},{4,2},{2,4},{0,6},{14,8},{12,10},{10,12},{8,14},{15,1},{13,3... | collective-permute-start | bytes 221192 | tf_op jit(solution)/shard_map/ppermute | solution.py:543
  7.2 0.5 collective-permute-start.1
  7.7 0.2 collective-permute-start.3
  7.9 3.9 %own_gather.2.refs_5_ = bf16[864,512]{1,0:T(8,128)(2,1)S(1)} custom-call(bf16[512,256]{1,0:T(8,128)(2,1)S(1)} %get-tuple-element.36.table.refs_7_, f32[32,2048]{1,0:T(8,128)S(1)} %get-tuple-element.28.high.refs_8_, f32[32,2048]{1,0:T(8,128)S(1)} %get-tuple-element.29.low.refs_9_), custom_call_target="tpu_custom_call" | custom-call | flops 3623878656 | bytes 1048576 | tf_op jit(solution)/shard_map/own_gather/pallas_call | solution.py:17
  11.8 0.0 copy-start.1
  11.8 0.6 collective-permute-done.1.refs_0_
  12.4 2.4 %collective-permute-start.5 = (bf16[32,1152]{1,0:T(8,128)(2,1)S(1)}, bf16[32,1152]{1,0:T(8,128)(2,1)S(1)}, u32[]{:S(2)}, u32[]{:S(2)}) collective-permute-start(bf16[32,1152]{1,0:T(8,128)(2,1)S(1)} %collective-permute-done.2.refs_1_), channel_id=1, source_target_pairs={{0,1},{1,0},{2,3},{3,2},{4,5},{5,4},{6,7},{7,6},{8,9},{9,8},{10,11... | collective-permute-start | bytes 221192 | tf_op jit(solution)/shard_map/ppermute | solution.py:511
  14.7 1.9 %own_gather.3.refs_6_ = bf16[864,256]{1,0:T(8,128)(2,1)S(1)} custom-call(bf16[512,256]{1,0:T(8,128)(2,1)S(1)} %get-tuple-element.36.table.refs_7_, f32[32,2048]{1,0:T(8,128)S(1)} %get-tuple-element.28.high.refs_8_, f32[32,2048]{1,0:T(8,128)S(1)} %get-tuple-element.29.low.refs_9_), custom_call_target="tpu_custom_call" | custom-call | flops 1811939328 | bytes 1048576 | tf_op jit(solution)/shard_map/own_gather/pallas_call | solution.py:17
  16.8 19.5 %middle.1 = (bf16[32,2048]{1,0:T(8,128)(2,1)S(1)}, f32[16,2560]{1,0:T(8,128)S(1)}, f32[16,2560]{1,0:T(8,128)S(1)}) custom-call(bf16[32,1536]{1,0:T(8,128)(2,1)S(1)} %collective-permute-done.1.refs_0_, bf16[32,1152]{1,0:T(8,128)(2,1)S(1)} %collective-permute-done.2.refs_1_, bf16[32,1536]{1,0:T(8,128)(2,1)S(1)} %collective-permute-done.3.refs_2_, ...), custom_call_target="tpu_custom_call" | custom-call | flops 20837302272 | bytes 1048576 | tf_op jit(solution)/shard_map/middle/pallas_call | solution.py:17
  36.3 0.5 collective-permute-start.6
  36.8 10.4 %halo_scatter.1.halo = f32[224,256]{1,0:T(8,128)S(1)} custom-call(bf16[864,32]{1,0:T(8,128)(2,1)S(1)} %bitcast.5, bf16[32,2048]{1,0:T(8,128)(2,1)S(1)} %get-tuple-element.37.grad, f32[32,2048]{1,0:T(8,128)S(1)} %get-tuple-element.28.high.refs_8_, f32[32,2048]{1,0:T(8,128)S(1)} %get-tuple-element.29.low.refs_9_), custom_call_target="tpu_custom_call" | custom-call | flops 6341787648 | bytes 1048576 | tf_op jit(solution)/shard_map/halo_scatter/pallas_call | solution.py:17
  47.2 0.9 %join.1 = (f32[16,2560]{1,0:T(8,128)S(1)}, bf16[8,32,1152]{2,1,0:T(8,128)(2,1)}) custom-call(f32[16,2560]{1,0:T(8,128)S(1)} %get-tuple-element.38.mine, f32[16,2560]{1,0:T(8,128)S(1)} %collective-permute-done.6.theirs, f32[224,256]{1,0:T(8,128)S(1)} %halo_scatter.1.halo), custom_call_target="tpu_custom_call" | custom-call | flops 1048576 | bytes 1048576 | tf_op jit(solution)/shard_map/join/pallas_call | solution.py:17
  48.2 4.8 %all-to-all-start = ((bf16[8,32,1152]{2,1,0:T(8,128)(2,1)}), bf16[8,32,1152]{2,1,0:T(8,128)(2,1)S(1)}, u32[]{:S(2)}, u32[]{:S(2)}) async-start(bf16[8,32,1152]{2,1,0:T(8,128)(2,1)} %get-tuple-element.41), calls=%async_computation | async-start | bytes 1179648 | tf_op jit(solution)/shard_map/all_to_all | solution.py:627
  52.9 16.0 %own_scatter.1.total = f32[512,256]{1,0:T(8,128)S(1)} custom-call(bf16[864,32]{1,0:T(8,128)(2,1)S(1)} %bitcast.6, bf16[32,2048]{1,0:T(8,128)(2,1)S(1)} %get-tuple-element.37.grad, f32[32,2048]{1,0:T(8,128)S(1)} %get-tuple-element.28.high.refs_8_, f32[32,2048]{1,0:T(8,128)S(1)} %get-tuple-element.29.low.refs_9_), custom_call_target="tpu_custom_call" | custom-call | flops 14495514624 | bytes 1048576 | tf_op jit(solution)/shard_map/own_scatter/pallas_call | solution.py:17
  68.9 0.1 all-to-all-done.arrived
  69.1 1.4 %final.1 = (f32[16,4096]{1,0:T(8,128)S(1)}, f32[16,4096]{1,0:T(8,128)S(1)}, f32[64,256]{1,0:T(8,128)S(1)}, f32[64,256]{1,0:T(8,128)S(1)}, f32[27,16,32]{2,1,0:T(8,128)}, /*index=5*/f32[32,64]{1,0:T(8,128)}) custom-call(f32[512,256]{1,0:T(8,128)S(1)} %own_scatter.1.total, f32[16,2560]{1,0:T(8,128)S(1)} %get-tuple-element.40.joined, ...), custom_call_target="tpu_custom_call" | custom-call | flops 1073741824 | bytes 1048576 | tf_op jit(solution)/shard_map/final/pallas_call | solution.py:17
  70.5 0.5 collective-permute-start.8
  71.0 1.1 %collective-permute-done.8.coarse_theirs = f32[64,256]{1,0:T(8,128)S(1)} collective-permute-done((f32[64,256]{1,0:T(8,128)S(1)}, f32[64,256]{1,0:T(8,128)S(1)}, u32[]{:S(2)}, u32[]{:S(2)}) %collective-permute-start.8) | collective-permute-done | bytes 65568 | tf_op jit(solution)/shard_map/ppermute | solution.py:511
  72.1 0.7 add.1
  (24 shorter events, 0.1 us)
Async XLA Ops:
  0.6 1.9 %collective-permute-start = (bf16[16,4096]{1,0:T(8,128)(2,1)}, bf16[16,4096]{1,0:T(8,128)(2,1)S(1)}, u32[]{:S(2)}, u32[]{:S(2)}) collective-permute-start(bf16[16,4096]{1,0:T(8,128)(2,1)} %own.1), channel_id=1, source_target_pairs={{0,1},{1,0},{2,3},{3,2},{4,5},{5,4},{6,7},{7,6},{8,9},{9,8},{10,11... | collective-permute-start | bytes 393224 | tf_op jit(solution)/shard_map/ppermute | solution.py:511
  1.1 1.0 %copy-start = (s32[27,4096]{1,0:T(8,128)S(1)}, s32[27,4096]{1,0:T(8,128)}, u32[]{:S(2)}) copy-start(s32[27,4096]{1,0:T(8,128)} %neighbours.1) | copy-start | bytes 1327108
  2.2 0.9 %copy-start.2 = (bf16[16,4096]{1,0:T(8,128)(2,1)S(1)}, bf16[16,4096]{1,0:T(8,128)(2,1)}, u32[]{:S(2)}) copy-start(bf16[16,4096]{1,0:T(8,128)(2,1)} %own.1) | copy-start | bytes 393220
  2.2 0.9 %copy-start.3 = (bf16[128,256]{1,0:T(8,128)(2,1)S(1)}, bf16[128,256]{1,0:T(8,128)(2,1)}, u32[]{:S(2)}) copy-start(bf16[128,256]{1,0:T(8,128)(2,1)} %refs_14_.1) | copy-start | bytes 196612
  2.2 0.9 %copy-start.6 = (s32[4,512]{1,0:T(4,128)S(1)}, s32[4,512]{1,0:T(4,128)}, u32[]{:S(2)}) copy-start(s32[4,512]{1,0:T(4,128)} %face.3) | copy-start | bytes 24580
  2.2 0.9 %copy-start.8 = (s32[4,128]{1,0:T(4,128)S(1)}, s32[4,128]{1,0:T(4,128)}, u32[]{:S(2)}) copy-start(s32[4,128]{1,0:T(4,128)} %corner.3) | copy-start | bytes 6148
  3.6 8.2 %collective-permute-start.2 = (bf16[32,1152]{1,0:T(8,128)(2,1)S(1)}, bf16[32,1152]{1,0:T(8,128)(2,1)S(1)}, u32[]{:S(2)}, u32[]{:S(2)}) collective-permute-start(bf16[32,1152]{1,0:T(8,128)(2,1)S(1)} %get-tuple-element.31), channel_id=1, source_target_pairs={{6,0},{4,2},{2,4},{0,6},{14,8},{12,10},{10,12},{8,14},{15,1},{13,3... | collective-permute-start | bytes 221192 | tf_op jit(solution)/shard_map/ppermute | solution.py:543
  7.2 5.2 %collective-permute-start.1 = (bf16[32,1536]{1,0:T(8,128)(2,1)S(1)}, bf16[32,1536]{1,0:T(8,128)(2,1)S(1)}, u32[]{:S(2)}, u32[]{:S(2)}) collective-permute-start(bf16[32,1536]{1,0:T(8,128)(2,1)S(1)} %get-tuple-element.30), channel_id=1, source_target_pairs={{4,0},{6,2},{0,4},{2,6},{12,8},{14,10},{8,12},{10,14},{13,1},{15,3... | collective-permute-start | bytes 294920 | tf_op jit(solution)/shard_map/ppermute | solution.py:543
  7.7 9.0 %collective-permute-start.3 = (bf16[32,1536]{1,0:T(8,128)(2,1)S(1)}, bf16[32,1536]{1,0:T(8,128)(2,1)S(1)}, u32[]{:S(2)}, u32[]{:S(2)}) collective-permute-start(bf16[32,1536]{1,0:T(8,128)(2,1)S(1)} %get-tuple-element.34), channel_id=1, source_target_pairs={{2,0},{0,2},{6,4},{4,6},{10,8},{8,10},{14,12},{12,14},{3,1},{1,3},... | collective-permute-start | bytes 294920 | tf_op jit(solution)/shard_map/ppermute | solution.py:543
  11.8 5.0 %copy-start.1 = (bf16[27,32,32]{2,1,0:T(8,128)(2,1)S(1)}, bf16[27,32,32]{2,1,0:T(8,128)(2,1)}, u32[]{:S(2)}) copy-start(bf16[27,32,32]{2,1,0:T(8,128)(2,1)} %param.15) | copy-start | bytes 165892
  11.8 5.0 %copy-start.4 = (s32[4096]{0:T(1024)S(1)}, s32[4096]{0:T(1024)}, u32[]{:S(2)}) copy-start(s32[4096]{0:T(1024)} %param.13) | copy-start | bytes 49156
  11.8 5.0 %copy-start.5 = (s32[4096]{0:T(1024)S(1)}, s32[4096]{0:T(1024)}, u32[]{:S(2)}) copy-start(s32[4096]{0:T(1024)} %param.14) | copy-start | bytes 49156
  11.8 5.0 %copy-start.7 = (bf16[32,128]{1,0:T(8,128)(2,1)S(1)}, bf16[32,128]{1,0:T(8,128)(2,1)}, u32[]{:S(2)}) copy-start(bf16[32,128]{1,0:T(8,128)(2,1)} %coarse_weight.1) | copy-start | bytes 24580
  12.4 4.3 %collective-permute-start.5 = (bf16[32,1152]{1,0:T(8,128)(2,1)S(1)}, bf16[32,1152]{1,0:T(8,128)(2,1)S(1)}, u32[]{:S(2)}, u32[]{:S(2)}) collective-permute-start(bf16[32,1152]{1,0:T(8,128)(2,1)S(1)} %collective-permute-done.2.refs_1_), channel_id=1, source_target_pairs={{0,1},{1,0},{2,3},{3,2},{4,5},{5,4},{6,7},{7,6},{8,9},{9,8},{10,11... | collective-permute-start | bytes 221192 | tf_op jit(solution)/shard_map/ppermute | solution.py:511
  14.7 2.0 %collective-permute-start.4 = (bf16[32,1536]{1,0:T(8,128)(2,1)S(1)}, bf16[32,1536]{1,0:T(8,128)(2,1)S(1)}, u32[]{:S(2)}, u32[]{:S(2)}) collective-permute-start(bf16[32,1536]{1,0:T(8,128)(2,1)S(1)} %collective-permute-done.1.refs_0_), channel_id=1, source_target_pairs={{0,1},{1,0},{2,3},{3,2},{4,5},{5,4},{6,7},{7,6},{8,9},{9,8},{10,11... | collective-permute-start | bytes 294920 | tf_op jit(solution)/shard_map/ppermute | solution.py:511
  36.3 11.0 %collective-permute-start.6 = (f32[16,2560]{1,0:T(8,128)S(1)}, f32[16,2560]{1,0:T(8,128)S(1)}, u32[]{:S(2)}, u32[]{:S(2)}) collective-permute-start(f32[16,2560]{1,0:T(8,128)S(1)} %get-tuple-element.39), channel_id=1, source_target_pairs={{0,1},{1,0},{2,3},{3,2},{4,5},{5,4},{6,7},{7,6},{8,9},{9,8},{10,11... | collective-permute-start | bytes 491528 | tf_op jit(solution)/shard_map/ppermute | solution.py:511
  48.2 20.9 %all-to-all-start = ((bf16[8,32,1152]{2,1,0:T(8,128)(2,1)}), bf16[8,32,1152]{2,1,0:T(8,128)(2,1)S(1)}, u32[]{:S(2)}, u32[]{:S(2)}) async-start(bf16[8,32,1152]{2,1,0:T(8,128)(2,1)} %get-tuple-element.41), calls=%async_computation | async-start | bytes 1179648 | tf_op jit(solution)/shard_map/all_to_all | solution.py:627
  70.5 1.6 %collective-permute-start.7 = (f32[16,4096]{1,0:T(8,128)S(1)}, f32[16,4096]{1,0:T(8,128)S(1)}, u32[]{:S(2)}, u32[]{:S(2)}) collective-permute-start(f32[16,4096]{1,0:T(8,128)S(1)} %get-tuple-element.43), channel_id=1, source_target_pairs={{0,1},{1,0},{2,3},{3,2},{4,5},{5,4},{6,7},{7,6},{8,9},{9,8},{10,11... | collective-permute-start | bytes 786440 | tf_op jit(solution)/shard_map/ppermute | solution.py:511
  70.5 1.6 %collective-permute-start.8 = (f32[64,256]{1,0:T(8,128)S(1)}, f32[64,256]{1,0:T(8,128)S(1)}, u32[]{:S(2)}, u32[]{:S(2)}) collective-permute-start(f32[64,256]{1,0:T(8,128)S(1)} %get-tuple-element.45), channel_id=1, source_target_pairs={{0,1},{1,0},{2,3},{3,2},{4,5},{5,4},{6,7},{7,6},{8,9},{9,8},{10,11... | collective-permute-start | bytes 196616 | tf_op jit(solution)/shard_map/ppermute | solution.py:511

commit v5 on v4

--- a/solution.py
+++ b/solution.py
@@ -200,17 +200,33 @@
 
 
 def columns(block):
+    if isinstance(block, int):
+        return slice(block * LOW, (block + 1) * LOW)
     return pl.ds(pl.multiple_of(block * LOW, LOW), LOW)
 
 
+def blocks_loop(first, last, body):
+    pairs = (last - first) // 2
+
+    def two(j, carry):
+        body(first + 2 * j)
+        body(first + 2 * j + 1)
+        return carry
+
+    if pairs > 1:
+        lax.fori_loop(0, pairs, two, 0)
+    elif pairs:
+        two(0, 0)
+    if (last - first) % 2:
+        body(last - 1)
+
+
 def own_gather_kernel(plan, first, count, table, high, low, out):
-    n = plan.channels
-
-    def body(j, carry):
-        gather_block(plan, table, high, low, out, columns(first + j), 0, plan.own_blocks, columns(j))
-        return carry
-
-    lax.fori_loop(0, count, body, 0)
+    def body(j):
+        to = columns(j - first)
+        gather_block(plan, table, high, low, out, columns(j), 0, plan.own_blocks, to)
+
+    blocks_loop(first, first + count, body)
 
 
 def middle_kernel(plan, *refs):
@@ -254,32 +270,23 @@
             at = plan.widths[k] + g * m
             coarse_all[g * n : (g + 1) * n, (k + 1) * m : (k + 2) * m] = messages[k][:, at : at + m]
 
-    def whole(j, carry):
+    halo_table = table.at[own:, :]
+    done = 0
+    for before, count in zip(befores, plan.early):
+
+        def rest(j):
+            of = columns(j - done)
+            gather_block(
+                plan, halo_table, high, low, rows, columns(j), plan.own_blocks, plan.halo_blocks, of, before
+            )
+
+        blocks_loop(done, done + count, rest)
+        done += count
+
+    def whole(j):
         gather_block(plan, table, high, low, rows, columns(j), 0, plan.own_blocks + plan.halo_blocks)
-        return carry
-
-    done = 0
-    halo_table = table.at[own:, :]
-    for before, count in zip(befores, plan.early):
-
-        def rest(j, carry):
-            gather_block(
-                plan,
-                halo_table,
-                high,
-                low,
-                rows,
-                columns(done + j),
-                plan.own_blocks,
-                plan.halo_blocks,
-                columns(j),
-                before,
-            )
-            return carry
-
-        lax.fori_loop(0, count, rest, 0)
-        done += count
-    lax.fori_loop(done, plan.half // LOW, whole, 0)
+
+    blocks_loop(done, plan.half // LOW, whole)
     for j in range(plan.half // LOW):
         at = pl.multiple_of((core * (plan.half // LOW) + j) * n, n)
         rows[plan.itself * n : (plan.itself + 1) * n, j * LOW : (j + 1) * LOW] = table[pl.ds(at, n), :]
@@ -288,7 +295,7 @@
     owners = plan.slots + 1
     for k in range(owners):
         pooled_all[k * n : (k + 1) * n, :] = grads[:, k * m : (k + 1) * m]
-    chunk = min(plan.half, 512)
+    chunk = min(plan.half, 1024)
     wide = plan.offsets * n
     sums[...] = jnp.zeros_like(sums)
     parts[...] = jnp.zeros_like(parts)

time: 73.1 us -> 71.8 us (0.982)
  Pallas kernels: 55.6 us -> 54.3 us
    pallas_call x10, Pallas kernels: 55.6 us -> 54.3 us  [call(): pl.pallas_call(kernel, name=name, out_shape=[jax.ShapeDtypeStruct(s, d) f...]
where the time goes in v5:
time: 71.8 us; the launch traced here: 71.5 us
  Pallas kernels  54.3 us (76%)
  starting transfers between devices  12.7 us (18%)
  waiting for transfers between devices  2.02 us (3%)
  local copies, waits for them, and re-layouts  1.68 us (2%)
  between operations  0.8 us (1%)
    pallas_call x10, Pallas kernels, call(): pl.pallas_call(kernel, name=name, out_shape=[jax.ShapeDtypeStruct(s, d) f...  54.3 us
    all_to_all x1, starting transfers between devices, shards(): arrived = lax.all_to_all(send, ('tx', 'ty'), 0, 0, tiled=True)  4.58 us
    ppermute x3, starting transfers between devices, shards(): lax.ppermute(value, ('tx', 'ty', 'ch'), plan.pairs(first, second))  4.22 us
    ppermute x6, starting transfers between devices, swap(): return lax.ppermute(value, 'ch', [(0, 1), (1, 0)])  3.92 us
    unnamed x18, local copies, waits for them, and re-layouts  1.68 us
  transfers between devices with their start and end apart: 10, of which 3 were waited for; matrix products, arithmetic and copies ran while one was open for 0% of the time, Pallas kernels for 45%

profile of v5, /device:TPU:0, one launch (start us, length us, event | category | flops | bytes accessed | tf_op | source)
XLA Modules:
  0.0 71.5 jit_solution(16737254726079730593)
XLA Ops:
  0.6 0.5 collective-permute-start
  1.2 1.0 %copy-done = s32[27,4096]{1,0:T(8,128)S(1)} copy-done((s32[27,4096]{1,0:T(8,128)S(1)}, s32[27,4096]{1,0:T(8,128)}, u32[]{:S(2)}) %copy-start) | copy-done | bytes 442392
  2.2 0.3 prepare.1
  2.5 0.6 copy-done.2
  3.1 0.5 pack.1
  3.6 3.6 %collective-permute-start.2 = (bf16[32,1152]{1,0:T(8,128)(2,1)S(1)}, bf16[32,1152]{1,0:T(8,128)(2,1)S(1)}, u32[]{:S(2)}, u32[]{:S(2)}) collective-permute-start(bf16[32,1152]{1,0:T(8,128)(2,1)S(1)} %get-tuple-element.31), channel_id=1, source_target_pairs={{6,0},{4,2},{2,4},{0,6},{14,8},{12,10},{10,12},{8,14},{15,1},{13,3... | collective-permute-start | bytes 221192 | tf_op jit(solution)/shard_map/ppermute | solution.py:550
  7.2 0.5 collective-permute-start.1
  7.7 0.2 collective-permute-start.3
  7.9 3.7 %own_gather.2.refs_5_ = bf16[864,512]{1,0:T(8,128)(2,1)S(1)} custom-call(bf16[512,256]{1,0:T(8,128)(2,1)S(1)} %get-tuple-element.36.table.refs_7_, f32[32,2048]{1,0:T(8,128)S(1)} %get-tuple-element.28.high.refs_8_, f32[32,2048]{1,0:T(8,128)S(1)} %get-tuple-element.29.low.refs_9_), custom_call_target="tpu_custom_call" | custom-call | flops 3623878656 | bytes 1048576 | tf_op jit(solution)/shard_map/own_gather/pallas_call | solution.py:17
  11.6 0.0 copy-start.4
  11.7 0.7 %collective-permute-done.1.refs_0_ = bf16[32,1536]{1,0:T(8,128)(2,1)S(1)} collective-permute-done((bf16[32,1536]{1,0:T(8,128)(2,1)S(1)}, bf16[32,1536]{1,0:T(8,128)(2,1)S(1)}, u32[]{:S(2)}, u32[]{:S(2)}) %collective-permute-start.1) | collective-permute-done | bytes 98336 | tf_op jit(solution)/shard_map/ppermute | solution.py:550
  12.4 2.4 %collective-permute-start.5 = (bf16[32,1152]{1,0:T(8,128)(2,1)S(1)}, bf16[32,1152]{1,0:T(8,128)(2,1)S(1)}, u32[]{:S(2)}, u32[]{:S(2)}) collective-permute-start(bf16[32,1152]{1,0:T(8,128)(2,1)S(1)} %collective-permute-done.2.refs_1_), channel_id=1, source_target_pairs={{0,1},{1,0},{2,3},{3,2},{4,5},{5,4},{6,7},{7,6},{8,9},{9,8},{10,11... | collective-permute-start | bytes 221192 | tf_op jit(solution)/shard_map/ppermute | solution.py:518
  14.7 1.9 %own_gather.3.refs_6_ = bf16[864,256]{1,0:T(8,128)(2,1)S(1)} custom-call(bf16[512,256]{1,0:T(8,128)(2,1)S(1)} %get-tuple-element.36.table.refs_7_, f32[32,2048]{1,0:T(8,128)S(1)} %get-tuple-element.28.high.refs_8_, f32[32,2048]{1,0:T(8,128)S(1)} %get-tuple-element.29.low.refs_9_), custom_call_target="tpu_custom_call" | custom-call | flops 1811939328 | bytes 1048576 | tf_op jit(solution)/shard_map/own_gather/pallas_call | solution.py:17
  16.8 18.4 %middle.1 = (bf16[32,2048]{1,0:T(8,128)(2,1)S(1)}, f32[16,2560]{1,0:T(8,128)S(1)}, f32[16,2560]{1,0:T(8,128)S(1)}) custom-call(bf16[32,1536]{1,0:T(8,128)(2,1)S(1)} %collective-permute-done.1.refs_0_, bf16[32,1152]{1,0:T(8,128)(2,1)S(1)} %collective-permute-done.2.refs_1_, bf16[32,1536]{1,0:T(8,128)(2,1)S(1)} %collective-permute-done.3.refs_2_, ...), custom_call_target="tpu_custom_call" | custom-call | flops 20837302272 | bytes 1048576 | tf_op jit(solution)/shard_map/middle/pallas_call | solution.py:17
  35.1 0.5 collective-permute-start.6
  35.7 10.5 %halo_scatter.1.halo = f32[224,256]{1,0:T(8,128)S(1)} custom-call(bf16[864,32]{1,0:T(8,128)(2,1)S(1)} %bitcast.5, bf16[32,2048]{1,0:T(8,128)(2,1)S(1)} %get-tuple-element.37.grad, f32[32,2048]{1,0:T(8,128)S(1)} %get-tuple-element.28.high.refs_8_, f32[32,2048]{1,0:T(8,128)S(1)} %get-tuple-element.29.low.refs_9_), custom_call_target="tpu_custom_call" | custom-call | flops 6341787648 | bytes 1048576 | tf_op jit(solution)/shard_map/halo_scatter/pallas_call | solution.py:17
  46.1 0.9 %join.1 = (f32[16,2560]{1,0:T(8,128)S(1)}, bf16[8,32,1152]{2,1,0:T(8,128)(2,1)}) custom-call(f32[16,2560]{1,0:T(8,128)S(1)} %get-tuple-element.38.mine, f32[16,2560]{1,0:T(8,128)S(1)} %collective-permute-done.6.theirs, f32[224,256]{1,0:T(8,128)S(1)} %halo_scatter.1.halo), custom_call_target="tpu_custom_call" | custom-call | flops 1048576 | bytes 1048576 | tf_op jit(solution)/shard_map/join/pallas_call | solution.py:17
  47.0 4.6 %all-to-all-start = ((bf16[8,32,1152]{2,1,0:T(8,128)(2,1)}), bf16[8,32,1152]{2,1,0:T(8,128)(2,1)S(1)}, u32[]{:S(2)}, u32[]{:S(2)}) async-start(bf16[8,32,1152]{2,1,0:T(8,128)(2,1)} %get-tuple-element.41), calls=%async_computation | async-start | bytes 1179648 | tf_op jit(solution)/shard_map/all_to_all | solution.py:634
  51.6 16.0 %own_scatter.1.total = f32[512,256]{1,0:T(8,128)S(1)} custom-call(bf16[864,32]{1,0:T(8,128)(2,1)S(1)} %bitcast.6, bf16[32,2048]{1,0:T(8,128)(2,1)S(1)} %get-tuple-element.37.grad, f32[32,2048]{1,0:T(8,128)S(1)} %get-tuple-element.28.high.refs_8_, f32[32,2048]{1,0:T(8,128)S(1)} %get-tuple-element.29.low.refs_9_), custom_call_target="tpu_custom_call" | custom-call | flops 14495514624 | bytes 1048576 | tf_op jit(solution)/shard_map/own_scatter/pallas_call | solution.py:17
  67.6 0.2 all-to-all-done.arrived
  67.8 1.4 %final.1 = (f32[16,4096]{1,0:T(8,128)S(1)}, f32[16,4096]{1,0:T(8,128)S(1)}, f32[64,256]{1,0:T(8,128)S(1)}, f32[64,256]{1,0:T(8,128)S(1)}, f32[27,16,32]{2,1,0:T(8,128)}, /*index=5*/f32[32,64]{1,0:T(8,128)}) custom-call(f32[512,256]{1,0:T(8,128)S(1)} %own_scatter.1.total, f32[16,2560]{1,0:T(8,128)S(1)} %get-tuple-element.40.joined, ...), custom_call_target="tpu_custom_call" | custom-call | flops 1073741824 | bytes 1048576 | tf_op jit(solution)/shard_map/final/pallas_call | solution.py:17
  69.2 0.5 collective-permute-start.8
  69.7 1.1 %collective-permute-done.8.coarse_theirs = f32[64,256]{1,0:T(8,128)S(1)} collective-permute-done((f32[64,256]{1,0:T(8,128)S(1)}, f32[64,256]{1,0:T(8,128)S(1)}, u32[]{:S(2)}, u32[]{:S(2)}) %collective-permute-start.8) | collective-permute-done | bytes 65568 | tf_op jit(solution)/shard_map/ppermute | solution.py:518
  70.8 0.7 add.1
  (24 shorter events, 0.1 us)
Async XLA Ops:
  0.6 1.9 %collective-permute-start = (bf16[16,4096]{1,0:T(8,128)(2,1)}, bf16[16,4096]{1,0:T(8,128)(2,1)S(1)}, u32[]{:S(2)}, u32[]{:S(2)}) collective-permute-start(bf16[16,4096]{1,0:T(8,128)(2,1)} %own.1), channel_id=1, source_target_pairs={{0,1},{1,0},{2,3},{3,2},{4,5},{5,4},{6,7},{7,6},{8,9},{9,8},{10,11... | collective-permute-start | bytes 393224 | tf_op jit(solution)/shard_map/ppermute | solution.py:518
  1.1 1.0 %copy-start = (s32[27,4096]{1,0:T(8,128)S(1)}, s32[27,4096]{1,0:T(8,128)}, u32[]{:S(2)}) copy-start(s32[27,4096]{1,0:T(8,128)} %neighbours.1) | copy-start | bytes 1327108
  2.2 0.9 %copy-start.2 = (bf16[16,4096]{1,0:T(8,128)(2,1)S(1)}, bf16[16,4096]{1,0:T(8,128)(2,1)}, u32[]{:S(2)}) copy-start(bf16[16,4096]{1,0:T(8,128)(2,1)} %own.1) | copy-start | bytes 393220
  2.2 0.9 %copy-start.3 = (bf16[128,256]{1,0:T(8,128)(2,1)S(1)}, bf16[128,256]{1,0:T(8,128)(2,1)}, u32[]{:S(2)}) copy-start(bf16[128,256]{1,0:T(8,128)(2,1)} %refs_14_.1) | copy-start | bytes 196612
  2.2 0.9 %copy-start.6 = (s32[4,512]{1,0:T(4,128)S(1)}, s32[4,512]{1,0:T(4,128)}, u32[]{:S(2)}) copy-start(s32[4,512]{1,0:T(4,128)} %face.3) | copy-start | bytes 24580
  2.2 0.9 %copy-start.8 = (s32[4,128]{1,0:T(4,128)S(1)}, s32[4,128]{1,0:T(4,128)}, u32[]{:S(2)}) copy-start(s32[4,128]{1,0:T(4,128)} %corner.3) | copy-start | bytes 6148
  3.6 8.0 %collective-permute-start.2 = (bf16[32,1152]{1,0:T(8,128)(2,1)S(1)}, bf16[32,1152]{1,0:T(8,128)(2,1)S(1)}, u32[]{:S(2)}, u32[]{:S(2)}) collective-permute-start(bf16[32,1152]{1,0:T(8,128)(2,1)S(1)} %get-tuple-element.31), channel_id=1, source_target_pairs={{6,0},{4,2},{2,4},{0,6},{14,8},{12,10},{10,12},{8,14},{15,1},{13,3... | collective-permute-start | bytes 221192 | tf_op jit(solution)/shard_map/ppermute | solution.py:550
  7.2 5.2 %collective-permute-start.1 = (bf16[32,1536]{1,0:T(8,128)(2,1)S(1)}, bf16[32,1536]{1,0:T(8,128)(2,1)S(1)}, u32[]{:S(2)}, u32[]{:S(2)}) collective-permute-start(bf16[32,1536]{1,0:T(8,128)(2,1)S(1)} %get-tuple-element.30), channel_id=1, source_target_pairs={{4,0},{6,2},{0,4},{2,6},{12,8},{14,10},{8,12},{10,14},{13,1},{15,3... | collective-permute-start | bytes 294920 | tf_op jit(solution)/shard_map/ppermute | solution.py:550
  7.7 9.0 %collective-permute-start.3 = (bf16[32,1536]{1,0:T(8,128)(2,1)S(1)}, bf16[32,1536]{1,0:T(8,128)(2,1)S(1)}, u32[]{:S(2)}, u32[]{:S(2)}) collective-permute-start(bf16[32,1536]{1,0:T(8,128)(2,1)S(1)} %get-tuple-element.34), channel_id=1, source_target_pairs={{2,0},{0,2},{6,4},{4,6},{10,8},{8,10},{14,12},{12,14},{3,1},{1,3},... | collective-permute-start | bytes 294920 | tf_op jit(solution)/shard_map/ppermute | solution.py:550
  11.6 5.1 %copy-start.1 = (bf16[27,32,32]{2,1,0:T(8,128)(2,1)S(1)}, bf16[27,32,32]{2,1,0:T(8,128)(2,1)}, u32[]{:S(2)}) copy-start(bf16[27,32,32]{2,1,0:T(8,128)(2,1)} %param.15) | copy-start | bytes 165892
  11.6 5.1 %copy-start.4 = (s32[4096]{0:T(1024)S(1)}, s32[4096]{0:T(1024)}, u32[]{:S(2)}) copy-start(s32[4096]{0:T(1024)} %param.13) | copy-start | bytes 49156
  11.6 5.1 %copy-start.5 = (s32[4096]{0:T(1024)S(1)}, s32[4096]{0:T(1024)}, u32[]{:S(2)}) copy-start(s32[4096]{0:T(1024)} %param.14) | copy-start | bytes 49156
  11.6 5.1 %copy-start.7 = (bf16[32,128]{1,0:T(8,128)(2,1)S(1)}, bf16[32,128]{1,0:T(8,128)(2,1)}, u32[]{:S(2)}) copy-start(bf16[32,128]{1,0:T(8,128)(2,1)} %coarse_weight.1) | copy-start | bytes 24580
  12.4 4.3 %collective-permute-start.5 = (bf16[32,1152]{1,0:T(8,128)(2,1)S(1)}, bf16[32,1152]{1,0:T(8,128)(2,1)S(1)}, u32[]{:S(2)}, u32[]{:S(2)}) collective-permute-start(bf16[32,1152]{1,0:T(8,128)(2,1)S(1)} %collective-permute-done.2.refs_1_), channel_id=1, source_target_pairs={{0,1},{1,0},{2,3},{3,2},{4,5},{5,4},{6,7},{7,6},{8,9},{9,8},{10,11... | collective-permute-start | bytes 221192 | tf_op jit(solution)/shard_map/ppermute | solution.py:518
  14.7 2.0 %collective-permute-start.4 = (bf16[32,1536]{1,0:T(8,128)(2,1)S(1)}, bf16[32,1536]{1,0:T(8,128)(2,1)S(1)}, u32[]{:S(2)}, u32[]{:S(2)}) collective-permute-start(bf16[32,1536]{1,0:T(8,128)(2,1)S(1)} %collective-permute-done.1.refs_0_), channel_id=1, source_target_pairs={{0,1},{1,0},{2,3},{3,2},{4,5},{5,4},{6,7},{7,6},{8,9},{9,8},{10,11... | collective-permute-start | bytes 294920 | tf_op jit(solution)/shard_map/ppermute | solution.py:518
  35.1 11.0 %collective-permute-start.6 = (f32[16,2560]{1,0:T(8,128)S(1)}, f32[16,2560]{1,0:T(8,128)S(1)}, u32[]{:S(2)}, u32[]{:S(2)}) collective-permute-start(f32[16,2560]{1,0:T(8,128)S(1)} %get-tuple-element.39), channel_id=1, source_target_pairs={{0,1},{1,0},{2,3},{3,2},{4,5},{5,4},{6,7},{7,6},{8,9},{9,8},{10,11... | collective-permute-start | bytes 491528 | tf_op jit(solution)/shard_map/ppermute | solution.py:518
  47.0 20.7 %all-to-all-start = ((bf16[8,32,1152]{2,1,0:T(8,128)(2,1)}), bf16[8,32,1152]{2,1,0:T(8,128)(2,1)S(1)}, u32[]{:S(2)}, u32[]{:S(2)}) async-start(bf16[8,32,1152]{2,1,0:T(8,128)(2,1)} %get-tuple-element.41), calls=%async_computation | async-start | bytes 1179648 | tf_op jit(solution)/shard_map/all_to_all | solution.py:634
  69.2 1.6 %collective-permute-start.7 = (f32[16,4096]{1,0:T(8,128)S(1)}, f32[16,4096]{1,0:T(8,128)S(1)}, u32[]{:S(2)}, u32[]{:S(2)}) collective-permute-start(f32[16,4096]{1,0:T(8,128)S(1)} %get-tuple-element.43), channel_id=1, source_target_pairs={{0,1},{1,0},{2,3},{3,2},{4,5},{5,4},{6,7},{7,6},{8,9},{9,8},{10,11... | collective-permute-start | bytes 786440 | tf_op jit(solution)/shard_map/ppermute | solution.py:518
  69.2 1.6 %collective-permute-start.8 = (f32[64,256]{1,0:T(8,128)S(1)}, f32[64,256]{1,0:T(8,128)S(1)}, u32[]{:S(2)}, u32[]{:S(2)}) collective-permute-start(f32[64,256]{1,0:T(8,128)S(1)} %get-tuple-element.45), channel_id=1, source_target_pairs={{0,1},{1,0},{2,3},{3,2},{4,5},{5,4},{6,7},{7,6},{8,9},{9,8},{10,11... | collective-permute-start | bytes 196616 | tf_op jit(solution)/shard_map/ppermute | solution.py:518

commit v6 on v5

--- a/solution.py
+++ b/solution.py
@@ -432,7 +432,7 @@
 
 
 def final_kernel(plan, total, joined, arrived, face, corner, coarse_weight, *refs):
-    mine_out, theirs_out, coarse_mine, coarse_theirs, conv_out, coarse_grad_out, work, product = refs
+    mine_out, theirs_out, coarse_mine, coarse_theirs, work, product = refs
     core, x, y = where_am_i(plan)
     n, s, m = plan.channels, plan.share, plan.coarse
     width = plan.sum_width // (n // s)
@@ -474,6 +474,11 @@
     )
     coarse_mine[...] = product[pl.ds(pl.multiple_of(core * share, share), share), :]
     coarse_theirs[...] = product[pl.ds(pl.multiple_of((1 - core) * share, share), share), :]
+
+
+def sum_kernel(plan, arrived, mine, conv_out, coarse_grad_out):
+    n, s, share = plan.channels, plan.share, plan.coarse_share
+    width = plan.sum_width // (n // s)
     summed = arrived[0, :, :width].astype(F32)
     for t in range(1, plan.tiles):
         summed = summed + arrived[t, :, :width].astype(F32)
@@ -645,10 +650,10 @@
         low,
     )
     share = plan.coarse_share
-    mine, theirs, coarse_mine, coarse_theirs, conv_weight_grad, coarse_weight_grad = run(
+    mine, theirs, coarse_mine, coarse_theirs = run(
         final_kernel,
         "final",
-        [((s, plan.voxels), F32)] * 2 + [((share, m), F32)] * 2 + [((plan.offsets, s, n), F32), ((n, share), F32)],
+        [((s, plan.voxels), F32)] * 2 + [((share, m), F32)] * 2,
         [((plan.own_blocks * n, LOW), F32), ((plan.coarse_channels, m), F32)],
         1 << 30,
         12,
@@ -658,6 +663,16 @@
         face_send,
         corner_send,
         coarse_weight,
+    )
+    conv_weight_grad, coarse_weight_grad = run(
+        sum_kernel,
+        "sum",
+        [((plan.offsets, s, n), F32), ((n, share), F32)],
+        [],
+        1 << 28,
+        6,
+        arrived,
+        coarse_mine,
     )
     input_grad, coarse_out = run(
         add_kernel,

time: 71.8 us -> 71.3 us (level)
  waiting for transfers between devices: 2.02 us -> 1.21 us
    ppermute x6, waiting for transfers between devices: 1.13 us -> 0.33 us  [swap(): return lax.ppermute(value, 'ch', [(0, 1), (1, 0)])]
    pallas_call x10 -> x11, Pallas kernels: 54.3 us -> 54.5 us  [call(): pl.pallas_call(kernel, name=name, out_shape=[jax.ShapeDtypeStruct(s, d) f...]
  transfers between devices with their start and end apart: 10 -> 10, of which waited for: 3 -> 3; matrix products, arithmetic and copies ran while one was open for 0% -> 0% of each run, Pallas kernels for 45% -> 47%
where the time goes in v6:
time: 71.3 us; the launch traced here: 71 us
  Pallas kernels  54.5 us (76%)
  starting transfers between devices  12.8 us (18%)
  local copies, waits for them, and re-layouts  1.68 us (2%)
  waiting for transfers between devices  1.21 us (2%)
  between operations  0.81 us (1%)
    pallas_call x11, Pallas kernels, call(): pl.pallas_call(kernel, name=name, out_shape=[jax.ShapeDtypeStruct(s, d) f...  54.5 us
    all_to_all x1, starting transfers between devices, shards(): arrived = lax.all_to_all(send, ('tx', 'ty'), 0, 0, tiled=True)  4.58 us
    ppermute x3, starting transfers between devices, shards(): lax.ppermute(value, ('tx', 'ty', 'ch'), plan.pairs(first, second))  4.22 us
    ppermute x6, starting transfers between devices, swap(): return lax.ppermute(value, 'ch', [(0, 1), (1, 0)])  3.98 us
    unnamed x18, local copies, waits for them, and re-layouts  1.68 us
  transfers between devices with their start and end apart: 10, of which 3 were waited for; matrix products, arithmetic and copies ran while one was open for 0% of the time, Pallas kernels for 47%

profile of v6, /device:TPU:0, one launch (start us, length us, event | category | flops | bytes accessed | tf_op | source)
XLA Modules:
  0.0 71.0 jit_solution(16594239022697178222)
XLA Ops:
  0.6 0.5 collective-permute-start
  1.2 1.0 %copy-done = s32[27,4096]{1,0:T(8,128)S(1)} copy-done((s32[27,4096]{1,0:T(8,128)S(1)}, s32[27,4096]{1,0:T(8,128)}, u32[]{:S(2)}) %copy-start) | copy-done | bytes 442392
  2.2 0.3 prepare.1
  2.5 0.6 copy-done.2
  3.1 0.5 pack.1
  3.6 3.6 %collective-permute-start.2 = (bf16[32,1152]{1,0:T(8,128)(2,1)S(1)}, bf16[32,1152]{1,0:T(8,128)(2,1)S(1)}, u32[]{:S(2)}, u32[]{:S(2)}) collective-permute-start(bf16[32,1152]{1,0:T(8,128)(2,1)S(1)} %get-tuple-element.31), channel_id=1, source_target_pairs={{6,0},{4,2},{2,4},{0,6},{14,8},{12,10},{10,12},{8,14},{15,1},{13,3... | collective-permute-start | bytes 221192 | tf_op jit(solution)/shard_map/ppermute | solution.py:555
  7.2 0.5 collective-permute-start.1
  7.7 0.2 collective-permute-start.3
  7.9 3.7 %own_gather.2.refs_5_ = bf16[864,512]{1,0:T(8,128)(2,1)S(1)} custom-call(bf16[512,256]{1,0:T(8,128)(2,1)S(1)} %get-tuple-element.36.table.refs_7_, f32[32,2048]{1,0:T(8,128)S(1)} %get-tuple-element.28.high.refs_8_, f32[32,2048]{1,0:T(8,128)S(1)} %get-tuple-element.29.low.refs_9_), custom_call_target="tpu_custom_call" | custom-call | flops 3623878656 | bytes 1048576 | tf_op jit(solution)/shard_map/own_gather/pallas_call | solution.py:17
  11.7 0.7 %collective-permute-done.1.refs_0_ = bf16[32,1536]{1,0:T(8,128)(2,1)S(1)} collective-permute-done((bf16[32,1536]{1,0:T(8,128)(2,1)S(1)}, bf16[32,1536]{1,0:T(8,128)(2,1)S(1)}, u32[]{:S(2)}, u32[]{:S(2)}) %collective-permute-start.1) | collective-permute-done | bytes 98336 | tf_op jit(solution)/shard_map/ppermute | solution.py:555
  12.4 2.4 %collective-permute-start.5 = (bf16[32,1152]{1,0:T(8,128)(2,1)S(1)}, bf16[32,1152]{1,0:T(8,128)(2,1)S(1)}, u32[]{:S(2)}, u32[]{:S(2)}) collective-permute-start(bf16[32,1152]{1,0:T(8,128)(2,1)S(1)} %collective-permute-done.2.refs_1_), channel_id=1, source_target_pairs={{0,1},{1,0},{2,3},{3,2},{4,5},{5,4},{6,7},{7,6},{8,9},{9,8},{10,11... | collective-permute-start | bytes 221192 | tf_op jit(solution)/shard_map/ppermute | solution.py:523
  14.7 1.9 %own_gather.3.refs_6_ = bf16[864,256]{1,0:T(8,128)(2,1)S(1)} custom-call(bf16[512,256]{1,0:T(8,128)(2,1)S(1)} %get-tuple-element.36.table.refs_7_, f32[32,2048]{1,0:T(8,128)S(1)} %get-tuple-element.28.high.refs_8_, f32[32,2048]{1,0:T(8,128)S(1)} %get-tuple-element.29.low.refs_9_), custom_call_target="tpu_custom_call" | custom-call | flops 1811939328 | bytes 1048576 | tf_op jit(solution)/shard_map/own_gather/pallas_call | solution.py:17
  16.8 18.4 %middle.1 = (bf16[32,2048]{1,0:T(8,128)(2,1)S(1)}, f32[16,2560]{1,0:T(8,128)S(1)}, f32[16,2560]{1,0:T(8,128)S(1)}) custom-call(bf16[32,1536]{1,0:T(8,128)(2,1)S(1)} %collective-permute-done.1.refs_0_, bf16[32,1152]{1,0:T(8,128)(2,1)S(1)} %collective-permute-done.2.refs_1_, bf16[32,1536]{1,0:T(8,128)(2,1)S(1)} %collective-permute-done.3.refs_2_, ...), custom_call_target="tpu_custom_call" | custom-call | flops 20837302272 | bytes 1048576 | tf_op jit(solution)/shard_map/middle/pallas_call | solution.py:17
  35.1 0.5 collective-permute-start.6
  35.7 10.5 %halo_scatter.1.halo = f32[224,256]{1,0:T(8,128)S(1)} custom-call(bf16[864,32]{1,0:T(8,128)(2,1)S(1)} %bitcast.5, bf16[32,2048]{1,0:T(8,128)(2,1)S(1)} %get-tuple-element.37.grad, f32[32,2048]{1,0:T(8,128)S(1)} %get-tuple-element.28.high.refs_8_, f32[32,2048]{1,0:T(8,128)S(1)} %get-tuple-element.29.low.refs_9_), custom_call_target="tpu_custom_call" | custom-call | flops 6341787648 | bytes 1048576 | tf_op jit(solution)/shard_map/halo_scatter/pallas_call | solution.py:17
  46.1 0.9 %join.1 = (f32[16,2560]{1,0:T(8,128)S(1)}, bf16[8,32,1152]{2,1,0:T(8,128)(2,1)}) custom-call(f32[16,2560]{1,0:T(8,128)S(1)} %get-tuple-element.38.mine, f32[16,2560]{1,0:T(8,128)S(1)} %collective-permute-done.6.theirs, f32[224,256]{1,0:T(8,128)S(1)} %halo_scatter.1.halo), custom_call_target="tpu_custom_call" | custom-call | flops 1048576 | bytes 1048576 | tf_op jit(solution)/shard_map/join/pallas_call | solution.py:17
  47.1 4.6 %all-to-all-start = ((bf16[8,32,1152]{2,1,0:T(8,128)(2,1)}), bf16[8,32,1152]{2,1,0:T(8,128)(2,1)S(1)}, u32[]{:S(2)}, u32[]{:S(2)}) async-start(bf16[8,32,1152]{2,1,0:T(8,128)(2,1)} %get-tuple-element.41), calls=%async_computation | async-start | bytes 1179648 | tf_op jit(solution)/shard_map/all_to_all | solution.py:639
  51.6 16.0 %own_scatter.1.total = f32[512,256]{1,0:T(8,128)S(1)} custom-call(bf16[864,32]{1,0:T(8,128)(2,1)S(1)} %bitcast.6, bf16[32,2048]{1,0:T(8,128)(2,1)S(1)} %get-tuple-element.37.grad, f32[32,2048]{1,0:T(8,128)S(1)} %get-tuple-element.28.high.refs_8_, f32[32,2048]{1,0:T(8,128)S(1)} %get-tuple-element.29.low.refs_9_), custom_call_target="tpu_custom_call" | custom-call | flops 14495514624 | bytes 1048576 | tf_op jit(solution)/shard_map/own_scatter/pallas_call | solution.py:17
  67.6 0.1 all-to-all-done.arrived
  67.8 0.8 %final.1 = (f32[16,4096]{1,0:T(8,128)S(1)}, f32[16,4096]{1,0:T(8,128)S(1)}, f32[64,256]{1,0:T(8,128)S(1)}, f32[64,256]{1,0:T(8,128)S(1)}) custom-call(f32[512,256]{1,0:T(8,128)S(1)} %own_scatter.1.total, f32[16,2560]{1,0:T(8,128)S(1)} %get-tuple-element.40.joined, bf16[8,32,1152]{2,1,0:T(8,128)(2,1)S(1)} %all-to-all-done.arrived, s32[4,512]{1,0:T(4,128)S(1)} %copy-done.6, ...), custom_call_target="tpu_custom_call" | custom-call | flops 1073741824 | bytes 1048576 | tf_op jit(solution)/shard_map/final/pallas_call | solution.py:17
  68.7 0.5 collective-permute-start.8
  69.2 0.8 %sum.1 = (f32[27,16,32]{2,1,0:T(8,128)}, f32[32,64]{1,0:T(8,128)}) custom-call(bf16[8,32,1152]{2,1,0:T(8,128)(2,1)S(1)} %all-to-all-done.arrived, f32[64,256]{1,0:T(8,128)S(1)} %get-tuple-element.44.coarse_mine.mine), custom_call_target="tpu_custom_call" | custom-call | flops 268435456 | bytes 1048576 | tf_op jit(solution)/shard_map/sum/pallas_call | solution.py:17
  70.0 0.3 collective-permute-done.8.coarse_theirs
  70.3 0.7 add.1
  (25 shorter events, 0.1 us)
Async XLA Ops:
  0.6 1.9 %collective-permute-start = (bf16[16,4096]{1,0:T(8,128)(2,1)}, bf16[16,4096]{1,0:T(8,128)(2,1)S(1)}, u32[]{:S(2)}, u32[]{:S(2)}) collective-permute-start(bf16[16,4096]{1,0:T(8,128)(2,1)} %own.1), channel_id=1, source_target_pairs={{0,1},{1,0},{2,3},{3,2},{4,5},{5,4},{6,7},{7,6},{8,9},{9,8},{10,11... | collective-permute-start | bytes 393224 | tf_op jit(solution)/shard_map/ppermute | solution.py:523
  1.1 1.0 %copy-start = (s32[27,4096]{1,0:T(8,128)S(1)}, s32[27,4096]{1,0:T(8,128)}, u32[]{:S(2)}) copy-start(s32[27,4096]{1,0:T(8,128)} %neighbours.1) | copy-start | bytes 1327108
  2.2 0.9 %copy-start.2 = (bf16[16,4096]{1,0:T(8,128)(2,1)S(1)}, bf16[16,4096]{1,0:T(8,128)(2,1)}, u32[]{:S(2)}) copy-start(bf16[16,4096]{1,0:T(8,128)(2,1)} %own.1) | copy-start | bytes 393220
  2.2 0.9 %copy-start.3 = (bf16[128,256]{1,0:T(8,128)(2,1)S(1)}, bf16[128,256]{1,0:T(8,128)(2,1)}, u32[]{:S(2)}) copy-start(bf16[128,256]{1,0:T(8,128)(2,1)} %refs_14_.1) | copy-start | bytes 196612
  2.2 0.9 %copy-start.6 = (s32[4,512]{1,0:T(4,128)S(1)}, s32[4,512]{1,0:T(4,128)}, u32[]{:S(2)}) copy-start(s32[4,512]{1,0:T(4,128)} %face.3) | copy-start | bytes 24580
  2.2 0.9 %copy-start.8 = (s32[4,128]{1,0:T(4,128)S(1)}, s32[4,128]{1,0:T(4,128)}, u32[]{:S(2)}) copy-start(s32[4,128]{1,0:T(4,128)} %corner.3) | copy-start | bytes 6148
  3.6 8.0 %collective-permute-start.2 = (bf16[32,1152]{1,0:T(8,128)(2,1)S(1)}, bf16[32,1152]{1,0:T(8,128)(2,1)S(1)}, u32[]{:S(2)}, u32[]{:S(2)}) collective-permute-start(bf16[32,1152]{1,0:T(8,128)(2,1)S(1)} %get-tuple-element.31), channel_id=1, source_target_pairs={{6,0},{4,2},{2,4},{0,6},{14,8},{12,10},{10,12},{8,14},{15,1},{13,3... | collective-permute-start | bytes 221192 | tf_op jit(solution)/shard_map/ppermute | solution.py:555
  7.2 5.2 %collective-permute-start.1 = (bf16[32,1536]{1,0:T(8,128)(2,1)S(1)}, bf16[32,1536]{1,0:T(8,128)(2,1)S(1)}, u32[]{:S(2)}, u32[]{:S(2)}) collective-permute-start(bf16[32,1536]{1,0:T(8,128)(2,1)S(1)} %get-tuple-element.30), channel_id=1, source_target_pairs={{4,0},{6,2},{0,4},{2,6},{12,8},{14,10},{8,12},{10,14},{13,1},{15,3... | collective-permute-start | bytes 294920 | tf_op jit(solution)/shard_map/ppermute | solution.py:555
  7.7 9.0 %collective-permute-start.3 = (bf16[32,1536]{1,0:T(8,128)(2,1)S(1)}, bf16[32,1536]{1,0:T(8,128)(2,1)S(1)}, u32[]{:S(2)}, u32[]{:S(2)}) collective-permute-start(bf16[32,1536]{1,0:T(8,128)(2,1)S(1)} %get-tuple-element.34), channel_id=1, source_target_pairs={{2,0},{0,2},{6,4},{4,6},{10,8},{8,10},{14,12},{12,14},{3,1},{1,3},... | collective-permute-start | bytes 294920 | tf_op jit(solution)/shard_map/ppermute | solution.py:555
  11.6 5.1 %copy-start.1 = (bf16[27,32,32]{2,1,0:T(8,128)(2,1)S(1)}, bf16[27,32,32]{2,1,0:T(8,128)(2,1)}, u32[]{:S(2)}) copy-start(bf16[27,32,32]{2,1,0:T(8,128)(2,1)} %param.15) | copy-start | bytes 165892
  11.6 5.1 %copy-start.4 = (s32[4096]{0:T(1024)S(1)}, s32[4096]{0:T(1024)}, u32[]{:S(2)}) copy-start(s32[4096]{0:T(1024)} %param.13) | copy-start | bytes 49156
  11.6 5.1 %copy-start.5 = (s32[4096]{0:T(1024)S(1)}, s32[4096]{0:T(1024)}, u32[]{:S(2)}) copy-start(s32[4096]{0:T(1024)} %param.14) | copy-start | bytes 49156
  11.6 5.1 %copy-start.7 = (bf16[32,128]{1,0:T(8,128)(2,1)S(1)}, bf16[32,128]{1,0:T(8,128)(2,1)}, u32[]{:S(2)}) copy-start(bf16[32,128]{1,0:T(8,128)(2,1)} %coarse_weight.1) | copy-start | bytes 24580
  12.4 4.3 %collective-permute-start.5 = (bf16[32,1152]{1,0:T(8,128)(2,1)S(1)}, bf16[32,1152]{1,0:T(8,128)(2,1)S(1)}, u32[]{:S(2)}, u32[]{:S(2)}) collective-permute-start(bf16[32,1152]{1,0:T(8,128)(2,1)S(1)} %collective-permute-done.2.refs_1_), channel_id=1, source_target_pairs={{0,1},{1,0},{2,3},{3,2},{4,5},{5,4},{6,7},{7,6},{8,9},{9,8},{10,11... | collective-permute-start | bytes 221192 | tf_op jit(solution)/shard_map/ppermute | solution.py:523
  14.7 2.0 %collective-permute-start.4 = (bf16[32,1536]{1,0:T(8,128)(2,1)S(1)}, bf16[32,1536]{1,0:T(8,128)(2,1)S(1)}, u32[]{:S(2)}, u32[]{:S(2)}) collective-permute-start(bf16[32,1536]{1,0:T(8,128)(2,1)S(1)} %collective-permute-done.1.refs_0_), channel_id=1, source_target_pairs={{0,1},{1,0},{2,3},{3,2},{4,5},{5,4},{6,7},{7,6},{8,9},{9,8},{10,11... | collective-permute-start | bytes 294920 | tf_op jit(solution)/shard_map/ppermute | solution.py:523
  35.1 11.0 %collective-permute-start.6 = (f32[16,2560]{1,0:T(8,128)S(1)}, f32[16,2560]{1,0:T(8,128)S(1)}, u32[]{:S(2)}, u32[]{:S(2)}) collective-permute-start(f32[16,2560]{1,0:T(8,128)S(1)} %get-tuple-element.39), channel_id=1, source_target_pairs={{0,1},{1,0},{2,3},{3,2},{4,5},{5,4},{6,7},{7,6},{8,9},{9,8},{10,11... | collective-permute-start | bytes 491528 | tf_op jit(solution)/shard_map/ppermute | solution.py:523
  47.1 20.7 %all-to-all-start = ((bf16[8,32,1152]{2,1,0:T(8,128)(2,1)}), bf16[8,32,1152]{2,1,0:T(8,128)(2,1)S(1)}, u32[]{:S(2)}, u32[]{:S(2)}) async-start(bf16[8,32,1152]{2,1,0:T(8,128)(2,1)} %get-tuple-element.41), calls=%async_computation | async-start | bytes 1179648 | tf_op jit(solution)/shard_map/all_to_all | solution.py:639
  68.6 1.7 %collective-permute-start.7 = (f32[16,4096]{1,0:T(8,128)S(1)}, f32[16,4096]{1,0:T(8,128)S(1)}, u32[]{:S(2)}, u32[]{:S(2)}) collective-permute-start(f32[16,4096]{1,0:T(8,128)S(1)} %get-tuple-element.43), channel_id=1, source_target_pairs={{0,1},{1,0},{2,3},{3,2},{4,5},{5,4},{6,7},{7,6},{8,9},{9,8},{10,11... | collective-permute-start | bytes 786440 | tf_op jit(solution)/shard_map/ppermute | solution.py:523
  68.7 1.6 %collective-permute-start.8 = (f32[64,256]{1,0:T(8,128)S(1)}, f32[64,256]{1,0:T(8,128)S(1)}, u32[]{:S(2)}, u32[]{:S(2)}) collective-permute-start(f32[64,256]{1,0:T(8,128)S(1)} %get-tuple-element.45), channel_id=1, source_target_pairs={{0,1},{1,0},{2,3},{3,2},{4,5},{5,4},{6,7},{7,6},{8,9},{9,8},{10,11... | collective-permute-start | bytes 196616 | tf_op jit(solution)/shard_map/ppermute | solution.py:523

commit v7 on v6

--- a/solution.py
+++ b/solution.py
@@ -47,6 +47,7 @@
         self.starts = [sum(self.widths[:s]) for s in range(self.slots)]
         self.nothing = self.voxels + self.halo
         self.wrapped = self.paired and nx % 2 == 0
+        self.lane_blocks = 2
         self.itself = self.offsets // 2
         self.tiles = nx * ny
         self.groups = ((0, 1), (3, 4), (2, 2)) if self.paired else ((0, 1), (2, 3), (4, 5), (6, 7))
@@ -180,7 +181,7 @@
             messages[g][:, at : at + plan.coarse] = coarse_grad[q * n : (q + 1) * n, :]
 
 
-def gather_block(plan, table, high_ref, low_ref, out, fs, base, blocks, to=None, before=None):
+def gather_block(plan, table, high_ref, low_ref, out, fs, base, blocks, to=None, before=None, side=None):
     to = fs if to is None else to
     n = plan.channels
     for k in range(plan.offsets):
@@ -194,9 +195,29 @@
             picked = jnp.zeros((n, LOW), F32)
         else:
             picked = before[at, to].astype(F32)
+        if side is not None:
+            picked = pick_lanes(side, high, low_ref[k : k + 1, fs], base + blocks, n)
         for b in range(blocks):
             picked = jnp.where(high == float(base + b), part[b * n : (b + 1) * n], picked)
         out[at, fs if before is not None else to] = picked.astype(BF)
+
+
+def pick_lanes(side, high, low, base, n):
+    upper = low >= 128.0
+    row = jnp.broadcast_to(2.0 * (high - float(base)) + jnp.where(upper, 1.0, 0.0), (8, LOW))
+    lane = jnp.broadcast_to((low - jnp.where(upper, 128.0, 0.0)).astype(jnp.int32), (8, LOW))
+    across = []
+    for q in range(LOW // 128):
+        at = slice(q * 128, (q + 1) * 128)
+        down = []
+        for c in range(0, n, 8):
+            found = jnp.zeros((8, 128), F32)
+            for b in range(side.shape[1] // 128):
+                source = side[c : c + 8, b * 128 : (b + 1) * 128]
+                found = jnp.where(row[:, at] == float(b), jnp.take_along_axis(source, lane[:, at], axis=1), found)
+            down.append(found)
+        across.append(jnp.concatenate(down, axis=0))
+    return jnp.concatenate(across, axis=1)
 
 
 def columns(block):
@@ -236,7 +257,7 @@
     swapped, refs = refs[: plan.swaps], refs[plan.swaps :]
     befores, refs = refs[: len(plan.early)], refs[len(plan.early) :]
     own_table, high, low, side, slot, weight, coarse_weight, coarse_grad, refs = (*refs[:8], refs[8:])
-    grad_out, mine_out, theirs_out, table, rows, coarse_all, pooled_all, sums, parts, coarse_sum = refs
+    grad_out, mine_out, theirs_out, table, rows, coarse_all, pooled_all, sums, parts, coarse_sum, lanes = refs
     core, x, y = where_am_i(plan)
     is_first = plan.is_first(core, x)
     messages = {}
@@ -283,8 +304,13 @@
         blocks_loop(done, done + count, rest)
         done += count
 
+    main = plan.own_blocks + plan.halo_blocks - plan.lane_blocks
+    main_table = table.at[: main * n, :]
+    for b in range(plan.lane_blocks):
+        lanes[:, b * LOW : (b + 1) * LOW] = table[(main + b) * n : (main + b + 1) * n, :].astype(F32)
+
     def whole(j):
-        gather_block(plan, table, high, low, rows, columns(j), 0, plan.own_blocks + plan.halo_blocks)
+        gather_block(plan, main_table, high, low, rows, columns(j), 0, main, side=lanes)
 
     blocks_loop(done, plan.half // LOW, whole)
     for j in range(plan.half // LOW):
@@ -596,6 +622,7 @@
             ((n, plan.padded), F32),
             ((owners * n, m), F32),
             ((n, plan.sum_width - plan.padded), F32),
+            ((n, plan.lane_blocks * LOW), F32),
         ],
         work * (plan.own_blocks + plan.halo_blocks),
         24,

time: 71.3 us -> 70.5 us (0.989)
    pallas_call x11, Pallas kernels: 54.5 us -> 53.8 us  [call(): pl.pallas_call(kernel, name=name, out_shape=[jax.ShapeDtypeStruct(s, d) f...]
where the time goes in v7:
time: 70.5 us; the launch traced here: 70.3 us
  Pallas kernels  53.8 us (76%)
  starting transfers between devices  12.8 us (18%)
  local copies, waits for them, and re-layouts  1.68 us (2%)
  waiting for transfers between devices  1.22 us (2%)
  between operations  0.81 us (1%)
    pallas_call x11, Pallas kernels, call(): pl.pallas_call(kernel, name=name, out_shape=[jax.ShapeDtypeStruct(s, d) f...  53.8 us
    all_to_all x1, starting transfers between devices, shards(): arrived = lax.all_to_all(send, ('tx', 'ty'), 0, 0, tiled=True)  4.58 us
    ppermute x3, starting transfers between devices, shards(): lax.ppermute(value, ('tx', 'ty', 'ch'), plan.pairs(first, second))  4.22 us
    ppermute x6, starting transfers between devices, swap(): return lax.ppermute(value, 'ch', [(0, 1), (1, 0)])  3.97 us
    unnamed x18, local copies, waits for them, and re-layouts  1.68 us
  transfers between devices with their start and end apart: 10, of which 3 were waited for; matrix products, arithmetic and copies ran while one was open for 0% of the time, Pallas kernels for 47%

profile of v7, /device:TPU:0, one launch (start us, length us, event | category | flops | bytes accessed | tf_op | source)
XLA Modules:
  0.0 70.3 jit_solution(9607808264412289611)
XLA Ops:
  0.6 0.5 collective-permute-start
  1.2 1.0 %copy-done = s32[27,4096]{1,0:T(8,128)S(1)} copy-done((s32[27,4096]{1,0:T(8,128)S(1)}, s32[27,4096]{1,0:T(8,128)}, u32[]{:S(2)}) %copy-start) | copy-done | bytes 442392
  2.2 0.3 prepare.1
  2.5 0.6 copy-done.2
  3.1 0.5 pack.1
  3.6 3.6 %collective-permute-start.2 = (bf16[32,1152]{1,0:T(8,128)(2,1)S(1)}, bf16[32,1152]{1,0:T(8,128)(2,1)S(1)}, u32[]{:S(2)}, u32[]{:S(2)}) collective-permute-start(bf16[32,1152]{1,0:T(8,128)(2,1)S(1)} %get-tuple-element.31), channel_id=1, source_target_pairs={{6,0},{4,2},{2,4},{0,6},{14,8},{12,10},{10,12},{8,14},{15,1},{13,3... | collective-permute-start | bytes 221192 | tf_op jit(solution)/shard_map/ppermute | solution.py:581
  7.2 0.5 collective-permute-start.1
  7.7 0.2 collective-permute-start.3
  7.9 3.7 %own_gather.2.refs_5_ = bf16[864,512]{1,0:T(8,128)(2,1)S(1)} custom-call(bf16[512,256]{1,0:T(8,128)(2,1)S(1)} %get-tuple-element.36.table.refs_7_, f32[32,2048]{1,0:T(8,128)S(1)} %get-tuple-element.28.high.refs_8_, f32[32,2048]{1,0:T(8,128)S(1)} %get-tuple-element.29.low.refs_9_), custom_call_target="tpu_custom_call" | custom-call | flops 3623878656 | bytes 1048576 | tf_op jit(solution)/shard_map/own_gather/pallas_call | solution.py:17
  11.7 0.7 %collective-permute-done.1.refs_0_ = bf16[32,1536]{1,0:T(8,128)(2,1)S(1)} collective-permute-done((bf16[32,1536]{1,0:T(8,128)(2,1)S(1)}, bf16[32,1536]{1,0:T(8,128)(2,1)S(1)}, u32[]{:S(2)}, u32[]{:S(2)}) %collective-permute-start.1) | collective-permute-done | bytes 98336 | tf_op jit(solution)/shard_map/ppermute | solution.py:581
  12.4 2.4 %collective-permute-start.5 = (bf16[32,1152]{1,0:T(8,128)(2,1)S(1)}, bf16[32,1152]{1,0:T(8,128)(2,1)S(1)}, u32[]{:S(2)}, u32[]{:S(2)}) collective-permute-start(bf16[32,1152]{1,0:T(8,128)(2,1)S(1)} %collective-permute-done.2.refs_1_), channel_id=1, source_target_pairs={{0,1},{1,0},{2,3},{3,2},{4,5},{5,4},{6,7},{7,6},{8,9},{9,8},{10,11... | collective-permute-start | bytes 221192 | tf_op jit(solution)/shard_map/ppermute | solution.py:549
  14.7 1.9 %own_gather.3.refs_6_ = bf16[864,256]{1,0:T(8,128)(2,1)S(1)} custom-call(bf16[512,256]{1,0:T(8,128)(2,1)S(1)} %get-tuple-element.36.table.refs_7_, f32[32,2048]{1,0:T(8,128)S(1)} %get-tuple-element.28.high.refs_8_, f32[32,2048]{1,0:T(8,128)S(1)} %get-tuple-element.29.low.refs_9_), custom_call_target="tpu_custom_call" | custom-call | flops 1811939328 | bytes 1048576 | tf_op jit(solution)/shard_map/own_gather/pallas_call | solution.py:17
  16.8 17.6 %middle.1 = (bf16[32,2048]{1,0:T(8,128)(2,1)S(1)}, f32[16,2560]{1,0:T(8,128)S(1)}, f32[16,2560]{1,0:T(8,128)S(1)}) custom-call(bf16[32,1536]{1,0:T(8,128)(2,1)S(1)} %collective-permute-done.1.refs_0_, bf16[32,1152]{1,0:T(8,128)(2,1)S(1)} %collective-permute-done.2.refs_1_, bf16[32,1536]{1,0:T(8,128)(2,1)S(1)} %collective-permute-done.3.refs_2_, ...), custom_call_target="tpu_custom_call" | custom-call | flops 20837302272 | bytes 1048576 | tf_op jit(solution)/shard_map/middle/pallas_call | solution.py:17
  34.4 0.5 collective-permute-start.6
  34.9 10.3 %halo_scatter.1.halo = f32[224,256]{1,0:T(8,128)S(1)} custom-call(bf16[864,32]{1,0:T(8,128)(2,1)S(1)} %bitcast.5, bf16[32,2048]{1,0:T(8,128)(2,1)S(1)} %get-tuple-element.37.grad, f32[32,2048]{1,0:T(8,128)S(1)} %get-tuple-element.28.high.refs_8_, f32[32,2048]{1,0:T(8,128)S(1)} %get-tuple-element.29.low.refs_9_), custom_call_target="tpu_custom_call" | custom-call | flops 6341787648 | bytes 1048576 | tf_op jit(solution)/shard_map/halo_scatter/pallas_call | solution.py:17
  45.2 1.1 %join.1 = (f32[16,2560]{1,0:T(8,128)S(1)}, bf16[8,32,1152]{2,1,0:T(8,128)(2,1)}) custom-call(f32[16,2560]{1,0:T(8,128)S(1)} %get-tuple-element.38.mine, f32[16,2560]{1,0:T(8,128)S(1)} %collective-permute-done.6.theirs, f32[224,256]{1,0:T(8,128)S(1)} %halo_scatter.1.halo), custom_call_target="tpu_custom_call" | custom-call | flops 1048576 | bytes 1048576 | tf_op jit(solution)/shard_map/join/pallas_call | solution.py:17
  46.3 4.6 %all-to-all-start = ((bf16[8,32,1152]{2,1,0:T(8,128)(2,1)}), bf16[8,32,1152]{2,1,0:T(8,128)(2,1)S(1)}, u32[]{:S(2)}, u32[]{:S(2)}) async-start(bf16[8,32,1152]{2,1,0:T(8,128)(2,1)} %get-tuple-element.41), calls=%async_computation | async-start | bytes 1179648 | tf_op jit(solution)/shard_map/all_to_all | solution.py:666
  50.9 16.0 %own_scatter.1.total = f32[512,256]{1,0:T(8,128)S(1)} custom-call(bf16[864,32]{1,0:T(8,128)(2,1)S(1)} %bitcast.6, bf16[32,2048]{1,0:T(8,128)(2,1)S(1)} %get-tuple-element.37.grad, f32[32,2048]{1,0:T(8,128)S(1)} %get-tuple-element.28.high.refs_8_, f32[32,2048]{1,0:T(8,128)S(1)} %get-tuple-element.29.low.refs_9_), custom_call_target="tpu_custom_call" | custom-call | flops 14495514624 | bytes 1048576 | tf_op jit(solution)/shard_map/own_scatter/pallas_call | solution.py:17
  66.9 0.2 all-to-all-done.arrived
  67.1 0.8 %final.1 = (f32[16,4096]{1,0:T(8,128)S(1)}, f32[16,4096]{1,0:T(8,128)S(1)}, f32[64,256]{1,0:T(8,128)S(1)}, f32[64,256]{1,0:T(8,128)S(1)}) custom-call(f32[512,256]{1,0:T(8,128)S(1)} %own_scatter.1.total, f32[16,2560]{1,0:T(8,128)S(1)} %get-tuple-element.40.joined, bf16[8,32,1152]{2,1,0:T(8,128)(2,1)S(1)} %all-to-all-done.arrived, s32[4,512]{1,0:T(4,128)S(1)} %copy-done.6, ...), custom_call_target="tpu_custom_call" | custom-call | flops 1073741824 | bytes 1048576 | tf_op jit(solution)/shard_map/final/pallas_call | solution.py:17
  68.0 0.5 collective-permute-start.8
  68.5 0.8 %sum.1 = (f32[27,16,32]{2,1,0:T(8,128)}, f32[32,64]{1,0:T(8,128)}) custom-call(bf16[8,32,1152]{2,1,0:T(8,128)(2,1)S(1)} %all-to-all-done.arrived, f32[64,256]{1,0:T(8,128)S(1)} %get-tuple-element.44.coarse_mine.mine), custom_call_target="tpu_custom_call" | custom-call | flops 268435456 | bytes 1048576 | tf_op jit(solution)/shard_map/sum/pallas_call | solution.py:17
  69.3 0.3 collective-permute-done.8.coarse_theirs
  69.6 0.7 add.1
  (25 shorter events, 0.1 us)
Async XLA Ops:
  0.6 1.9 %collective-permute-start = (bf16[16,4096]{1,0:T(8,128)(2,1)}, bf16[16,4096]{1,0:T(8,128)(2,1)S(1)}, u32[]{:S(2)}, u32[]{:S(2)}) collective-permute-start(bf16[16,4096]{1,0:T(8,128)(2,1)} %own.1), channel_id=1, source_target_pairs={{0,1},{1,0},{2,3},{3,2},{4,5},{5,4},{6,7},{7,6},{8,9},{9,8},{10,11... | collective-permute-start | bytes 393224 | tf_op jit(solution)/shard_map/ppermute | solution.py:549
  1.1 1.0 %copy-start = (s32[27,4096]{1,0:T(8,128)S(1)}, s32[27,4096]{1,0:T(8,128)}, u32[]{:S(2)}) copy-start(s32[27,4096]{1,0:T(8,128)} %neighbours.1) | copy-start | bytes 1327108
  2.2 0.9 %copy-start.2 = (bf16[16,4096]{1,0:T(8,128)(2,1)S(1)}, bf16[16,4096]{1,0:T(8,128)(2,1)}, u32[]{:S(2)}) copy-start(bf16[16,4096]{1,0:T(8,128)(2,1)} %own.1) | copy-start | bytes 393220
  2.2 0.9 %copy-start.3 = (bf16[128,256]{1,0:T(8,128)(2,1)S(1)}, bf16[128,256]{1,0:T(8,128)(2,1)}, u32[]{:S(2)}) copy-start(bf16[128,256]{1,0:T(8,128)(2,1)} %refs_14_.1) | copy-start | bytes 196612
  2.2 0.9 %copy-start.6 = (s32[4,512]{1,0:T(4,128)S(1)}, s32[4,512]{1,0:T(4,128)}, u32[]{:S(2)}) copy-start(s32[4,512]{1,0:T(4,128)} %face.3) | copy-start | bytes 24580
  2.2 0.9 %copy-start.8 = (s32[4,128]{1,0:T(4,128)S(1)}, s32[4,128]{1,0:T(4,128)}, u32[]{:S(2)}) copy-start(s32[4,128]{1,0:T(4,128)} %corner.3) | copy-start | bytes 6148
  3.6 8.0 %collective-permute-start.2 = (bf16[32,1152]{1,0:T(8,128)(2,1)S(1)}, bf16[32,1152]{1,0:T(8,128)(2,1)S(1)}, u32[]{:S(2)}, u32[]{:S(2)}) collective-permute-start(bf16[32,1152]{1,0:T(8,128)(2,1)S(1)} %get-tuple-element.31), channel_id=1, source_target_pairs={{6,0},{4,2},{2,4},{0,6},{14,8},{12,10},{10,12},{8,14},{15,1},{13,3... | collective-permute-start | bytes 221192 | tf_op jit(solution)/shard_map/ppermute | solution.py:581
  7.2 5.2 %collective-permute-start.1 = (bf16[32,1536]{1,0:T(8,128)(2,1)S(1)}, bf16[32,1536]{1,0:T(8,128)(2,1)S(1)}, u32[]{:S(2)}, u32[]{:S(2)}) collective-permute-start(bf16[32,1536]{1,0:T(8,128)(2,1)S(1)} %get-tuple-element.30), channel_id=1, source_target_pairs={{4,0},{6,2},{0,4},{2,6},{12,8},{14,10},{8,12},{10,14},{13,1},{15,3... | collective-permute-start | bytes 294920 | tf_op jit(solution)/shard_map/ppermute | solution.py:581
  7.7 9.0 %collective-permute-start.3 = (bf16[32,1536]{1,0:T(8,128)(2,1)S(1)}, bf16[32,1536]{1,0:T(8,128)(2,1)S(1)}, u32[]{:S(2)}, u32[]{:S(2)}) collective-permute-start(bf16[32,1536]{1,0:T(8,128)(2,1)S(1)} %get-tuple-element.34), channel_id=1, source_target_pairs={{2,0},{0,2},{6,4},{4,6},{10,8},{8,10},{14,12},{12,14},{3,1},{1,3},... | collective-permute-start | bytes 294920 | tf_op jit(solution)/shard_map/ppermute | solution.py:581
  11.6 5.1 %copy-start.1 = (bf16[27,32,32]{2,1,0:T(8,128)(2,1)S(1)}, bf16[27,32,32]{2,1,0:T(8,128)(2,1)}, u32[]{:S(2)}) copy-start(bf16[27,32,32]{2,1,0:T(8,128)(2,1)} %param.15) | copy-start | bytes 165892
  11.6 5.1 %copy-start.4 = (s32[4096]{0:T(1024)S(1)}, s32[4096]{0:T(1024)}, u32[]{:S(2)}) copy-start(s32[4096]{0:T(1024)} %param.13) | copy-start | bytes 49156
  11.6 5.1 %copy-start.5 = (s32[4096]{0:T(1024)S(1)}, s32[4096]{0:T(1024)}, u32[]{:S(2)}) copy-start(s32[4096]{0:T(1024)} %param.14) | copy-start | bytes 49156
  11.6 5.1 %copy-start.7 = (bf16[32,128]{1,0:T(8,128)(2,1)S(1)}, bf16[32,128]{1,0:T(8,128)(2,1)}, u32[]{:S(2)}) copy-start(bf16[32,128]{1,0:T(8,128)(2,1)} %coarse_weight.1) | copy-start | bytes 24580
  12.4 4.3 %collective-permute-start.5 = (bf16[32,1152]{1,0:T(8,128)(2,1)S(1)}, bf16[32,1152]{1,0:T(8,128)(2,1)S(1)}, u32[]{:S(2)}, u32[]{:S(2)}) collective-permute-start(bf16[32,1152]{1,0:T(8,128)(2,1)S(1)} %collective-permute-done.2.refs_1_), channel_id=1, source_target_pairs={{0,1},{1,0},{2,3},{3,2},{4,5},{5,4},{6,7},{7,6},{8,9},{9,8},{10,11... | collective-permute-start | bytes 221192 | tf_op jit(solution)/shard_map/ppermute | solution.py:549
  14.7 2.0 %collective-permute-start.4 = (bf16[32,1536]{1,0:T(8,128)(2,1)S(1)}, bf16[32,1536]{1,0:T(8,128)(2,1)S(1)}, u32[]{:S(2)}, u32[]{:S(2)}) collective-permute-start(bf16[32,1536]{1,0:T(8,128)(2,1)S(1)} %collective-permute-done.1.refs_0_), channel_id=1, source_target_pairs={{0,1},{1,0},{2,3},{3,2},{4,5},{5,4},{6,7},{7,6},{8,9},{9,8},{10,11... | collective-permute-start | bytes 294920 | tf_op jit(solution)/shard_map/ppermute | solution.py:549
  34.4 10.8 %collective-permute-start.6 = (f32[16,2560]{1,0:T(8,128)S(1)}, f32[16,2560]{1,0:T(8,128)S(1)}, u32[]{:S(2)}, u32[]{:S(2)}) collective-permute-start(f32[16,2560]{1,0:T(8,128)S(1)} %get-tuple-element.39), channel_id=1, source_target_pairs={{0,1},{1,0},{2,3},{3,2},{4,5},{5,4},{6,7},{7,6},{8,9},{9,8},{10,11... | collective-permute-start | bytes 491528 | tf_op jit(solution)/shard_map/ppermute | solution.py:549
  46.3 20.7 %all-to-all-start = ((bf16[8,32,1152]{2,1,0:T(8,128)(2,1)}), bf16[8,32,1152]{2,1,0:T(8,128)(2,1)S(1)}, u32[]{:S(2)}, u32[]{:S(2)}) async-start(bf16[8,32,1152]{2,1,0:T(8,128)(2,1)} %get-tuple-element.41), calls=%async_computation | async-start | bytes 1179648 | tf_op jit(solution)/shard_map/all_to_all | solution.py:666
  67.9 1.7 %collective-permute-start.7 = (f32[16,4096]{1,0:T(8,128)S(1)}, f32[16,4096]{1,0:T(8,128)S(1)}, u32[]{:S(2)}, u32[]{:S(2)}) collective-permute-start(f32[16,4096]{1,0:T(8,128)S(1)} %get-tuple-element.43), channel_id=1, source_target_pairs={{0,1},{1,0},{2,3},{3,2},{4,5},{5,4},{6,7},{7,6},{8,9},{9,8},{10,11... | collective-permute-start | bytes 786440 | tf_op jit(solution)/shard_map/ppermute | solution.py:549
  68.0 1.6 %collective-permute-start.8 = (f32[64,256]{1,0:T(8,128)S(1)}, f32[64,256]{1,0:T(8,128)S(1)}, u32[]{:S(2)}, u32[]{:S(2)}) collective-permute-start(f32[64,256]{1,0:T(8,128)S(1)} %get-tuple-element.45), channel_id=1, source_target_pairs={{0,1},{1,0},{2,3},{3,2},{4,5},{5,4},{6,7},{7,6},{8,9},{9,8},{10,11... | collective-permute-start | bytes 196616 | tf_op jit(solution)/shard_map/ppermute | solution.py:549
